TPU v7x, 32 devices: a whole 2x2x4 slice. The times are simulated.
32 devices in a mesh: grp: 2 (over y), blk: 16 (over z, x, core).
Axes of the slice: x: 2, y: 2, z: 4, core: 2. Of those that a mesh axis runs over, the one named last changes fastest.
Arguments:
- doc_grads: bfloat16 [16384, 8192], P(('grp', 'blk')), parts along dimension 0, may hold values from -6 to 6
- val_grads: bfloat16 [16, 8192], P('blk'), may hold values from -0.0625 to 0.0625
- inv_hessian: bfloat16 [8192, 8192], P('blk'), as said below
- topic_mask: int32 [128, 16], P(('grp', 'blk')), parts along dimension 0, may hold values 0 or 1
- membership: int32 [16384], P(('grp', 'blk')), parts along dimension 0, may hold values from 0 to 127
- owner_slot: int32 [128], replicated, may hold values from 0 to 127, each once
Outputs:
- cluster_influence: float32 [256, 16], P(('grp', 'blk')), parts along dimension 0
There are 2 independent parts, one for each index of `grp`. A program takes and returns all parts, laid end to end along the dimension named above; an argument that names none is the same for every part. Nothing has to cross between parts.
Inputs may be any that keep to these rules, and one draw needn't show every extreme that they name: inv_hessian is symmetric. `owner_slot`: each output row is the slot of exactly one cluster.
All inputs are finite; a program needn't handle non-finite values. No bound on the sum of `topic_mask` on one device may be relied on, other than what follows from the above.
Results may differ from a plain program's by a relative error of at most 0.0055.
Values may be sent and summed in bfloat16 or wider, within the bound.
No kernel may reach another device: no remote copies, remote signals or barrier semaphores. Data moves between devices by JAX's collectives and lax.ppermute only.
A program may use at most 64 MiB of HBM per device.

v0:
```python
import jax
import jax.numpy as jnp
from jax import lax
from jax.sharding import PartitionSpec as P


def per_device(doc_grads, val_grads, inv_hessian, topic_mask, membership, owner_slot):
    doc_count = doc_grads.shape[0]
    val_local = val_grads.shape[0]
    cluster_total = owner_slot.shape[0]
    val_cols = lax.all_to_all(val_grads, "blk", split_axis=1, concat_axis=0, tiled=True)
    panel = lax.psum_scatter(
        jnp.dot(val_cols, inv_hessian, preferred_element_type=jnp.float32),
        "blk",
        scatter_dimension=0,
        tiled=True,
    ).astype(jnp.bfloat16)
    block = lax.dot_general(
        doc_grads,
        lax.all_gather(panel, "blk", axis=0, tiled=True),
        (((1,), (1,)), ((), ())),
        preferred_element_type=jnp.float32,
    )
    block_rows = doc_count // topic_mask.shape[0]
    mask_full = jnp.repeat(
        jnp.repeat(topic_mask.astype(jnp.float32), block_rows, axis=0), val_local, axis=1
    )
    masked = block * mask_full
    slots = owner_slot[membership]
    slot_ids = lax.broadcasted_iota(jnp.int32, (cluster_total, doc_count), 0)
    one_hot = (slot_ids == slots[None, :]).astype(jnp.bfloat16)
    high_part = masked.astype(jnp.bfloat16)
    low_part = (masked - high_part.astype(jnp.float32)).astype(jnp.bfloat16)
    partial_sums = jnp.dot(one_hot, high_part, preferred_element_type=jnp.float32) + jnp.dot(
        one_hot, low_part, preferred_element_type=jnp.float32
    )
    partial_sums = 0.125 * partial_sums
    return lax.psum_scatter(partial_sums, "blk", scatter_dimension=0, tiled=True)


def solution(mesh):
    in_specs = (
        P(("grp", "blk"), None),
        P("blk", None),
        P("blk", None),
        P(("grp", "blk"), None),
        P(("grp", "blk")),
        P(),
    )
    out_specs = P(("grp", "blk"), None)
    return jax.shard_map(
        per_device, mesh=mesh, in_specs=in_specs, out_specs=out_specs, check_vma=False
    )
```

profile of v0, /device:TPU:0, one launch (start us, length us, event | category | flops | bytes accessed | tf_op | source)
XLA Modules:
  0.0 174.9 jit_solution(13731633655960067890)
XLA Ops:
  0.0 0.0 copy-start
  0.0 0.5 broadcast.5
  0.5 1.5 reduce
  2.0 0.6 reshape.20
  2.6 7.4 %all-to-all-start = ((bf16[16,2,256]{2,1,0:T(2,128)(2,1)}), bf16[16,2,256]{2,1,0:T(2,128)(2,1)S(1)}, u32[]{:S(2)}, u32[]{:S(2)}) async-start(bf16[16,2,256]{2,1,0:T(2,128)(2,1)} %reshape.20), calls=%async_computation | async-start | bytes 32768 | tf_op jit(solution)/shard_map/all_to_all | solution.py:11
  10.0 0.7 compare_select_fusion
  10.7 0.7 convert_element_type.17
  11.4 0.1 copy.10
  11.4 1.2 dynamic-slice
  12.7 0.0 copy-done
  12.7 3.3 %gather_fusion = s32[512]{0:T(512)S(1)} fusion(s32[128]{0:T(128)S(1)} %copy-done, s32[1024]{0:T(1024)S(1)} %pad_clamp_fusion), kind=kCustom, calls=%fused_computation | custom fusion | bytes 6144 | tf_op jit(solution)/shard_map/gather | solution.py:29
  16.7 0.0 all-to-all-done
  16.7 4.6 %fusion.8 = f32[16,8192]{1,0:T(8,128)S(1)} fusion(bf16[512,8192]{1,0:T(8,128)(2,1)} %param.8, bf16[1,16,512]{2,0,1:T(2,128)(2,1)S(1)} %bitcast.24), kind=kOutput, calls=%fused_computation.14 | convolution fusion | flops 134217728 | bytes 8929280 | tf_op jit(solution)/shard_map/dot_general | solution.py:13
  21.3 67.5 %all-reduce.3 = bf16[16,8192]{1,0:T(8,128)(2,1)S(1)} all-reduce(f32[16,8192]{1,0:T(8,128)S(1)} %fusion.8), channel_id=2, replica_groups=mesh['grp'=2,'blk'=16] {'blk'}, use_global_device_ids=true, to_apply=%region_0.0.clone | all-reduce | flops 131072 | bytes 786432
  88.8 0.7 fusion.7
  89.5 18.7 %all-gather = bf16[16,1,8192]{2,1,0:T(2,128)(2,1)S(1)} all-gather(bf16[1,1,8192]{2,1,0:T(2,128)(2,1)S(1)} %fusion.7), channel_id=1, replica_groups=mesh['grp'=2,'blk'=16] {'blk'}, dimensions={0}, use_global_device_ids=true | all-gather | bytes 278528 | tf_op jit(solution)/shard_map/all_gather | solution.py:20
  108.2 0.1 broadcast_in_dim.8
  108.3 5.7 %fusion.1 = f32[512,16]{0,1:T(8,128)S(1)} fusion(bf16[512,8192]{1,0:T(8,128)(2,1)} %param.6, bf16[16,1,8192]{2,1,0:T(2,128)(2,1)S(1)} %all-gather, f32[2,8,4,128]{3,2,1,0:T(4,128)S(1)} %bitcast.23), kind=kOutput, calls=%fused_computation.4 | convolution fusion | flops 134225920 | bytes 8716288 | tf_op jit(solution)/shard_map/dot_general | solution.py:18
  114.0 0.2 fusion.4
  114.2 0.2 fusion
  114.3 60.0 %all-reduce.1 = f32[128,16]{1,0:T(8,128)S(1)} all-reduce(f32[128,16]{1,0:T(8,128)S(1)} %fusion), channel_id=3, replica_groups=mesh['grp'=2,'blk'=16] {'blk'}, use_global_device_ids=true, to_apply=%region_1.0.clone | all-reduce | flops 2048 | bytes 16384
  174.3 0.6 constant_dynamic-slice_fusion
  (2 shorter events, 0.0 us)
Async XLA Ops:
  0.0 12.7 %copy-start = (s32[128]{0:T(128)S(1)}, s32[128]{0:T(128)}, u32[]{:S(2)}) copy-start(s32[128]{0:T(128)} %param.11) | copy-start | bytes 1540
  2.6 14.1 %all-to-all-start = ((bf16[16,2,256]{2,1,0:T(2,128)(2,1)}), bf16[16,2,256]{2,1,0:T(2,128)(2,1)S(1)}, u32[]{:S(2)}, u32[]{:S(2)}) async-start(bf16[16,2,256]{2,1,0:T(2,128)(2,1)} %reshape.20), calls=%async_computation | async-start | bytes 32768 | tf_op jit(solution)/shard_map/all_to_all | solution.py:11
where the time goes:
time: 175 us
  blocking collectives  146 us (83%)
  matrix products  10.6 us (6%)
  starting transfers between devices  7.36 us (4%)
  local copies, waits for them, and re-layouts  7.16 us (4%)
  other arithmetic  2.87 us (2%)
    unnamed x2, blocking collectives  127 us
    all_gather x1, blocking collectives, per_device(): lax.all_gather(panel, 'blk', axis=0, tiled=True)  18.7 us
    all_to_all x1, starting transfers between devices, per_device(): lax.all_to_all(val_grads, 'blk', split_axis=1, concat_axis=0, tiled=True)  7.36 us
    dot_general x1, matrix products, per_device(): lax.dot_general(doc_grads, lax.all_gather(panel, 'blk', axis=0, tiled=Tru...  5.68 us
    dot_general x1, matrix products, per_device(): jnp.dot(val_cols, inv_hessian, preferred_element_type=jnp.float32)  4.58 us
    unnamed x8, local copies, waits for them, and re-layouts  3.66 us
  transfers between devices with their start and end apart: 1, of which 0 were waited for; matrix products, arithmetic and copies ran while one was open for 3% of the time, Pallas kernels for 0%

commit v1 on v0

v1 whole, which is shorter than its diff:
```python
import jax
import jax.numpy as jnp
from jax import lax
from jax.sharding import PartitionSpec as P


def send(x, size, mask):
    return lax.ppermute(x, "blk", [(i, i ^ mask) for i in range(size)])


def split(size):
    inner = 1
    while inner * inner * 4 <= size:
        inner *= 2
    return size // inner, inner


def per_device(doc_grads, val_grads, inv_hessian, topic_mask, membership, owner_slot, *, size):
    outer, inner = split(size)
    me = lax.axis_index("blk")
    docs = doc_grads.shape[0]
    val_local, width = val_grads.shape
    rows = inv_hessian.shape[0]
    clusters = owner_slot.shape[0]
    kept = clusters // size
    order = me ^ jnp.arange(size)

    def gather(x):
        far = jnp.stack([x] + [send(x, size, s * inner) for s in range(1, outer)])
        near = jnp.stack([far] + [send(far, size, t) for t in range(1, inner)], axis=1)
        return near.reshape((size,) + x.shape)

    vals = gather(val_grads)
    vals = vals.reshape(size * val_local, width)
    panel = lax.dot_general(
        vals, inv_hessian, (((1,), (1,)), ((), ())), preferred_element_type=jnp.float32
    ).astype(jnp.bfloat16)
    panel = panel.reshape(size, val_local, rows)[order].reshape(size * val_local, rows)
    panels = gather(panel)[order]
    precond = jnp.moveaxis(panels, 0, 1).reshape(size * val_local, width)
    scores = lax.dot_general(
        precond, doc_grads, (((1,), (1,)), ((), ())), preferred_element_type=jnp.float32
    )
    block_rows = docs // topic_mask.shape[0]
    mask = jnp.repeat(topic_mask.T.astype(jnp.float32), block_rows, axis=1)
    mask = jnp.repeat(mask, val_local, axis=0)
    masked = scores * mask
    slot_of = (order[:, None] * kept + jnp.arange(kept)[None, :]).reshape(-1)
    by_slot = (slot_of[:, None] == owner_slot[None, :]).astype(jnp.bfloat16)
    by_doc = (jnp.arange(clusters)[:, None] == membership[None, :]).astype(jnp.bfloat16)
    one_hot = jnp.dot(by_slot, by_doc, preferred_element_type=jnp.float32).astype(jnp.bfloat16)
    high = masked.astype(jnp.bfloat16)
    low = (masked - high.astype(jnp.float32)).astype(jnp.bfloat16)
    dims = (((1,), (1,)), ((), ()))
    sums = lax.dot_general(one_hot, high, dims, preferred_element_type=jnp.float32)
    sums = sums + lax.dot_general(one_hot, low, dims, preferred_element_type=jnp.float32)
    sums = 0.125 * sums
    sums = sums.reshape(outer, inner * kept, -1)
    near = sums[0]
    for s in range(1, outer):
        near = near + send(sums[s], size, s * inner)
    near = near.reshape(inner, kept, -1)
    total = near[0]
    for t in range(1, inner):
        total = total + send(near[t], size, t)
    return total


def solution(mesh):
    size = mesh.shape["blk"]

    def run(*args):
        return per_device(*args, size=size)

    in_specs = (
        P(("grp", "blk"), None),
        P("blk", None),
        P("blk", None),
        P(("grp", "blk"), None),
        P(("grp", "blk")),
        P(),
    )
    out_specs = P(("grp", "blk"), None)
    return jax.shard_map(run, mesh=mesh, in_specs=in_specs, out_specs=out_specs, check_vma=False)
```

time: 175 us -> 58.9 us (0.34)
  blocking collectives: 146 us -> 0 us
  waiting for transfers between devices: 0.01 us -> 21.6 us
  starting transfers between devices: 7.36 us -> 20.3 us
  local copies, waits for them, and re-layouts: 7.16 us -> 2.55 us
    unnamed x2 -> x0, blocking collectives: 127 us -> none
    ppermute x0 -> x18, waiting for transfers between devices: none -> 21.6 us  [send(): return lax.ppermute(x, 'blk', [(i, i ^ mask) for i in range(size)])]
    ppermute x0 -> x18, starting transfers between devices: none -> 20.3 us  [send(): return lax.ppermute(x, 'blk', [(i, i ^ mask) for i in range(size)])]
    all_gather x1 -> x0, blocking collectives: 18.7 us -> none  [per_device(): lax.all_gather(panel, 'blk', axis=0, tiled=True)]
    all_to_all x1 -> x0, starting transfers between devices: 7.36 us -> none  [per_device(): lax.all_to_all(val_grads, 'blk', split_axis=1, concat_axis=0, tiled=True)]
    unnamed x8 -> x6, local copies, waits for them, and re-layouts: 3.66 us -> 0.01 us
    gather x1 -> x2, local copies, waits for them, and re-layouts: 3.34 us -> 1.17 us  [the longest x1 0.61 us: per_device(): panel.reshape(size, val_local, rows)[order].reshape(size * val_local, rows)]
    another operation x0 -> x5, other arithmetic: none -> 2.12 us  [the longest x4 1.2 us: gather(): jnp.stack([far] + [send(far, size, t) for t in range(1, inner)], axis=1)]
  transfers between devices with their start and end apart: 1 -> 18, of which waited for: 0 -> 12; matrix products, arithmetic and copies ran while one was open for 3% -> 2% of each run, Pallas kernels for 0% -> 0%
where the time goes in v1:
time: 58.9 us; the launch traced here: 58.6 us
  waiting for transfers between devices  21.6 us (37%)
  starting transfers between devices  20.3 us (34%)
  matrix products  11.8 us (20%)
  local copies, waits for them, and re-layouts  2.55 us (4%)
  other arithmetic  2.22 us (4%)
    ppermute x18, waiting for transfers between devices, send(): return lax.ppermute(x, 'blk', [(i, i ^ mask) for i in range(size)])  21.6 us
    ppermute x18, starting transfers between devices, send(): return lax.ppermute(x, 'blk', [(i, i ^ mask) for i in range(size)])  20.3 us
    dot_general x1, matrix products, per_device(): lax.dot_general(precond, doc_grads, (((1,), (1,)), ((), ())), preferred_e...  5.65 us
    dot_general x1, matrix products, per_device(): lax.dot_general(vals, inv_hessian, (((1,), (1,)), ((), ())), preferred_el...  5.64 us
    another operation x4, other arithmetic, gather(): jnp.stack([far] + [send(far, size, t) for t in range(1, inner)], axis=1)  1.2 us
  transfers between devices with their start and end apart: 18, of which 12 were waited for; matrix products, arithmetic and copies ran while one was open for 2% of the time, Pallas kernels for 0%

profile of v1, /device:TPU:0, one launch (start us, length us, event | category | flops | bytes accessed | tf_op | source)
XLA Modules:
  0.0 58.6 jit_solution(14484544575097329741)
XLA Ops:
  0.0 0.0 copy-start
  0.0 0.0 copy-start.2
  0.0 0.0 copy-start.1
  0.0 3.1 %collective-permute-start = (bf16[1,8192]{1,0:T(2,128)(2,1)}, bf16[1,8192]{1,0:T(2,128)(2,1)S(1)}, u32[]{:S(2)}, u32[]{:S(2)}) collective-permute-start(bf16[1,8192]{1,0:T(2,128)(2,1)} %param.7), channel_id=1, source_target_pairs={{0,4},{1,5},{2,6},{3,7},{4,0},{5,1},{6,2},{7,3},{8,12},{9,13},{10,... | collective-permute-start | bytes 49160 | tf_op jit(solution)/shard_map/ppermute | solution.py:8
  3.1 2.6 %collective-permute-start.1 = (bf16[1,8192]{1,0:T(2,128)(2,1)}, bf16[1,8192]{1,0:T(2,128)(2,1)S(1)}, u32[]{:S(2)}, u32[]{:S(2)}) collective-permute-start(bf16[1,8192]{1,0:T(2,128)(2,1)} %param.7), channel_id=1, source_target_pairs={{0,8},{1,9},{2,10},{3,11},{4,12},{5,13},{6,14},{7,15},{8,0},{9,1},... | collective-permute-start | bytes 49160 | tf_op jit(solution)/shard_map/ppermute | solution.py:8
  5.7 0.0 collective-permute-start.2
  5.7 0.1 iota_add_fusion
  5.8 0.1 add.55
  5.9 0.0 collective-permute-done
  5.9 2.8 %collective-permute-done.1 = bf16[1,8192]{1,0:T(2,128)(2,1)S(1)} collective-permute-done((bf16[1,8192]{1,0:T(2,128)(2,1)}, bf16[1,8192]{1,0:T(2,128)(2,1)S(1)}, u32[]{:S(2)}, u32[]{:S(2)}) %collective-permute-start.1) | collective-permute-done | bytes 16416 | tf_op jit(solution)/shard_map/ppermute | solution.py:8
  8.7 2.9 %collective-permute-done.2 = bf16[1,8192]{1,0:T(2,128)(2,1)S(1)} collective-permute-done((bf16[1,8192]{1,0:T(2,128)(2,1)}, bf16[1,8192]{1,0:T(2,128)(2,1)S(1)}, u32[]{:S(2)}, u32[]{:S(2)}) %collective-permute-start.2) | collective-permute-done | bytes 16416 | tf_op jit(solution)/shard_map/ppermute | solution.py:8
  11.6 0.9 %pad_maximum_fusion.2 = bf16[4,1,8192]{2,0,1:T(4,128)(2,1)S(1)} fusion(bf16[1,1,8192]{2,0,1:T(2,128)(2,1)S(1)} %bitcast.47, bf16[1,1,8192]{2,0,1:T(2,128)(2,1)S(1)} %bitcast.45, bf16[1,1,8192]{2,0,1:T(2,128)(2,1)S(1)} %bitcast.43, bf16[1,1,8192]{2,0,1:T(2,128)(2,1)} %bitcast.41), kind=kLoop, calls=%fused_computation.11 | loop fusion | flops 262144 | bytes 131072 | tf_op jit(solution)/shard_map/stack | solution.py:29
  12.5 0.1 collective-permute-start.3
  12.6 1.6 %collective-permute-start.4 = (bf16[4,1,8192]{2,0,1:T(4,128)(2,1)S(1)}, bf16[4,1,8192]{2,0,1:T(4,128)(2,1)S(1)}, u32[]{:S(2)}, u32[]{:S(2)}) collective-permute-start(bf16[4,1,8192]{2,0,1:T(4,128)(2,1)S(1)} %pad_maximum_fusion.2), channel_id=1, source_target_pairs={{0,2},{1,3},{2,0},{3,1},{4,6},{5,7},{6,4},{7,5},{8,10},{9,11},{10,... | collective-permute-start | bytes 196616 | tf_op jit(solution)/shard_map/ppermute | solution.py:8
  14.2 0.3 collective-permute-start.5
  14.5 0.9 %fusion.22 = bf16[4,1,1,8192]{3,0,2,1:T(4,128)(2,1)S(1)} fusion(bf16[1,1,8192]{2,0,1:T(2,128)(2,1)S(1)} %bitcast.48, bf16[1,1,8192]{2,0,1:T(2,128)(2,1)S(1)} %bitcast.46, bf16[1,1,8192]{2,0,1:T(2,128)(2,1)S(1)} %bitcast.44, bf16[1,1,8192]{2,0,1:T(2,128)(2,1)} %bitcast.42), kind=kLoop, calls=%fused_computation.35 | loop fusion | flops 262144 | bytes 131072 | tf_op jit(solution)/shard_map/stack | solution.py:30
  15.4 0.0 collective-permute-done.3
  15.4 1.7 %collective-permute-done.4 = bf16[4,1,8192]{2,0,1:T(4,128)(2,1)S(1)} collective-permute-done((bf16[4,1,8192]{2,0,1:T(4,128)(2,1)S(1)}, bf16[4,1,8192]{2,0,1:T(4,128)(2,1)S(1)}, u32[]{:S(2)}, u32[]{:S(2)}) %collective-permute-start.4) | collective-permute-done | bytes 65568 | tf_op jit(solution)/shard_map/ppermute | solution.py:8
  17.1 1.1 %collective-permute-done.5 = bf16[4,1,8192]{2,0,1:T(4,128)(2,1)S(1)} collective-permute-done((bf16[4,1,8192]{2,0,1:T(4,128)(2,1)S(1)}, bf16[4,1,8192]{2,0,1:T(4,128)(2,1)S(1)}, u32[]{:S(2)}, u32[]{:S(2)}) %collective-permute-start.5) | collective-permute-done | bytes 65568 | tf_op jit(solution)/shard_map/ppermute | solution.py:8
  18.2 0.2 pad_maximum_fusion
  18.5 0.2 copy.11
  18.7 0.1 reshape_reshape.3
  18.7 5.6 %convolution_convert_fusion.1 = bf16[16,512]{1,0:T(8,128)(2,1)S(1)} fusion(bf16[16,8192]{1,0:T(8,128)(2,1)S(1)} %reshape_reshape.3, bf16[512,8192]{1,0:T(8,128)(2,1)} %param.8), kind=kOutput, calls=%fused_computation.4 | convolution fusion | flops 134225920 | bytes 8667136 | tf_op jit(solution)/shard_map/dot_general | solution.py:35
  24.4 0.6 %gather_fusion = bf16[16,512]{1,0:T(8,128)(2,1)S(1)} fusion(bf16[16,512]{1,0:T(8,128)(2,1)S(1)} %convolution_convert_fusion.1, s32[1024]{0:T(1024)S(1)} %pad_clamp_fusion), kind=kCustom, calls=%fused_computation | custom fusion | bytes 32832 | tf_op jit(solution)/shard_map/gather | solution.py:38
  25.0 0.1 collective-permute-start.6
  25.1 0.9 %collective-permute-start.7 = (bf16[16,512]{1,0:T(8,128)(2,1)S(1)}, bf16[16,512]{1,0:T(8,128)(2,1)S(1)}, u32[]{:S(2)}, u32[]{:S(2)}) collective-permute-start(bf16[16,512]{1,0:T(8,128)(2,1)S(1)} %gather_fusion), channel_id=1, source_target_pairs={{0,8},{1,9},{2,10},{3,11},{4,12},{5,13},{6,14},{7,15},{8,0},{9,1},... | collective-permute-start | bytes 49160 | tf_op jit(solution)/shard_map/ppermute | solution.py:8
  26.0 3.5 %collective-permute-start.8 = (bf16[16,512]{1,0:T(8,128)(2,1)S(1)}, bf16[16,512]{1,0:T(8,128)(2,1)S(1)}, u32[]{:S(2)}, u32[]{:S(2)}) collective-permute-start(bf16[16,512]{1,0:T(8,128)(2,1)S(1)} %gather_fusion), channel_id=1, source_target_pairs={{0,12},{1,13},{2,14},{3,15},{4,8},{5,9},{6,10},{7,11},{8,4},{9,5},... | collective-permute-start | bytes 49160 | tf_op jit(solution)/shard_map/ppermute | solution.py:8
  29.4 0.0 copy-done
  29.4 0.0 copy-done.2
  29.4 0.2 convolution_convert_fusion
  29.7 0.0 collective-permute-done.6
  29.7 0.1 collective-permute-done.7
  29.8 1.7 %collective-permute-done.8 = bf16[16,512]{1,0:T(8,128)(2,1)S(1)} collective-permute-done((bf16[16,512]{1,0:T(8,128)(2,1)S(1)}, bf16[16,512]{1,0:T(8,128)(2,1)S(1)}, u32[]{:S(2)}, u32[]{:S(2)}) %collective-permute-start.8) | collective-permute-done | bytes 16416 | tf_op jit(solution)/shard_map/ppermute | solution.py:8
  31.5 0.1 collective-permute-start.9
  31.6 1.4 %collective-permute-start.10 = (bf16[4,16,512]{2,1,0:T(8,128)(2,1)S(1)}, bf16[4,16,512]{2,1,0:T(8,128)(2,1)S(1)}, u32[]{:S(2)}, u32[]{:S(2)}) collective-permute-start(bf16[4,16,512]{2,1,0:T(8,128)(2,1)S(1)} %get-tuple-element.6), channel_id=1, source_target_pairs={{0,2},{1,3},{2,0},{3,1},{4,6},{5,7},{6,4},{7,5},{8,10},{9,11},{10,... | collective-permute-start | bytes 196616 | tf_op jit(solution)/shard_map/ppermute | solution.py:8
  33.0 0.5 collective-permute-start.11
  33.5 0.0 copy-done.1
  33.5 0.1 copy.14
  33.6 0.0 collective-permute-done.9
  33.6 2.7 %collective-permute-done.10 = bf16[4,16,512]{2,1,0:T(8,128)(2,1)S(1)} collective-permute-done((bf16[4,16,512]{2,1,0:T(8,128)(2,1)S(1)}, bf16[4,16,512]{2,1,0:T(8,128)(2,1)S(1)}, u32[]{:S(2)}, u32[]{:S(2)}) %collective-permute-start.10) | collective-permute-done | bytes 65568 | tf_op jit(solution)/shard_map/ppermute | solution.py:8
  36.2 1.0 %collective-permute-done.11 = bf16[4,16,512]{2,1,0:T(8,128)(2,1)S(1)} collective-permute-done((bf16[4,16,512]{2,1,0:T(8,128)(2,1)S(1)}, bf16[4,16,512]{2,1,0:T(8,128)(2,1)S(1)}, u32[]{:S(2)}, u32[]{:S(2)}) %collective-permute-start.11) | collective-permute-done | bytes 65568 | tf_op jit(solution)/shard_map/ppermute | solution.py:8
  37.3 0.6 gather_fusion.1
  37.9 0.1 broadcast_in_dim.2
  38.0 5.7 %convolution_multiply_fusion = f32[16,512]{1,0:T(8,128)S(1)} fusion(bf16[16,8192]{1,0:T(8,128)(2,1)S(1)} %bitcast.37, bf16[512,8192]{1,0:T(8,128)(2,1)} %param.6, f32[2,8,4,128]{3,2,1,0:T(4,128)S(1)} %bitcast.40), kind=kOutput, calls=%fused_computation.3 | convolution fusion | flops 134225920 | bytes 8716288 | tf_op jit(solution)/shard_map/dot_general | solution.py:41
  43.7 0.1 fusion.10
  43.8 0.2 fusion
  44.0 0.1 fusion.15
  44.0 0.2 collective-permute-start.12
  44.3 3.8 %collective-permute-start.13 = (f32[32,16]{0,1:T(8,128)S(1)}, f32[32,16]{0,1:T(8,128)S(1)}, u32[]{:S(2)}, u32[]{:S(2)}) collective-permute-start(f32[32,16]{0,1:T(8,128)S(1)} %get-tuple-element.12), channel_id=1, source_target_pairs={{0,8},{1,9},{2,10},{3,11},{4,12},{5,13},{6,14},{7,15},{8,0},{9,1},... | collective-permute-start | bytes 6152 | tf_op jit(solution)/shard_map/ppermute | solution.py:8
  48.1 0.4 collective-permute-start.14
  48.5 0.0 collective-permute-done.12
  48.5 1.3 %collective-permute-done.13 = f32[32,16]{0,1:T(8,128)S(1)} collective-permute-done((f32[32,16]{0,1:T(8,128)S(1)}, f32[32,16]{0,1:T(8,128)S(1)}, u32[]{:S(2)}, u32[]{:S(2)}) %collective-permute-start.13) | collective-permute-done | bytes 2080 | tf_op jit(solution)/shard_map/ppermute | solution.py:8
  49.7 3.8 %collective-permute-done.14 = f32[32,16]{0,1:T(8,128)S(1)} collective-permute-done((f32[32,16]{0,1:T(8,128)S(1)}, f32[32,16]{0,1:T(8,128)S(1)}, u32[]{:S(2)}, u32[]{:S(2)}) %collective-permute-start.14) | collective-permute-done | bytes 2080 | tf_op jit(solution)/shard_map/ppermute | solution.py:8
  53.6 0.1 fusion.14
  53.6 0.0 collective-permute-start.15
  53.7 1.2 %collective-permute-start.16 = (f32[8,16]{0,1:T(8,128)S(1)}, f32[8,16]{0,1:T(8,128)S(1)}, u32[]{:S(2)}, u32[]{:S(2)}) collective-permute-start(f32[8,16]{0,1:T(8,128)S(1)} %get-tuple-element.9), channel_id=1, source_target_pairs={{0,2},{1,3},{2,0},{3,1},{4,6},{5,7},{6,4},{7,5},{8,10},{9,11},{10,... | collective-permute-start | bytes 1544 | tf_op jit(solution)/shard_map/ppermute | solution.py:8
  54.8 0.7 %collective-permute-start.17 = (f32[8,16]{0,1:T(8,128)S(1)}, f32[8,16]{0,1:T(8,128)S(1)}, u32[]{:S(2)}, u32[]{:S(2)}) collective-permute-start(f32[8,16]{0,1:T(8,128)S(1)} %get-tuple-element.8), channel_id=1, source_target_pairs={{0,3},{1,2},{2,1},{3,0},{4,7},{5,6},{6,5},{7,4},{8,11},{9,10},{10,... | collective-permute-start | bytes 1544 | tf_op jit(solution)/shard_map/ppermute | solution.py:8
  55.5 0.0 collective-permute-done.15
  55.5 1.9 %collective-permute-done.16 = f32[8,16]{0,1:T(8,128)S(1)} collective-permute-done((f32[8,16]{0,1:T(8,128)S(1)}, f32[8,16]{0,1:T(8,128)S(1)}, u32[]{:S(2)}, u32[]{:S(2)}) %collective-permute-start.16) | collective-permute-done | bytes 544 | tf_op jit(solution)/shard_map/ppermute | solution.py:8
  57.4 0.6 collective-permute-done.17
  57.9 0.7 %copy.15 = f32[8,16]{1,0:T(8,128)} copy(f32[8,16]{0,1:T(8,128)S(1)} %fusion.6) | data formatting | bytes 1024 | tf_op jit(solution)/shard_map/add | solution.py:65
  (10 shorter events, 0.1 us)
Async XLA Ops:
  0.0 29.4 %copy-start = (s32[512]{0:T(512)S(1)}, s32[512]{0:T(512)}, u32[]{:S(2)}) copy-start(s32[512]{0:T(512)} %param.10) | copy-start | bytes 6148
  0.0 29.4 %copy-start.2 = (s32[128]{0:T(128)S(1)}, s32[128]{0:T(128)}, u32[]{:S(2)}) copy-start(s32[128]{0:T(128)} %param.11) | copy-start | bytes 1540
  0.0 33.5 %copy-start.1 = (s32[4,16]{1,0:T(4,128)S(1)}, s32[4,16]{1,0:T(4,128)}, u32[]{:S(2)}) copy-start(s32[4,16]{1,0:T(4,128)} %param.9) | copy-start | bytes 772
  0.0 5.9 %collective-permute-start = (bf16[1,8192]{1,0:T(2,128)(2,1)}, bf16[1,8192]{1,0:T(2,128)(2,1)S(1)}, u32[]{:S(2)}, u32[]{:S(2)}) collective-permute-start(bf16[1,8192]{1,0:T(2,128)(2,1)} %param.7), channel_id=1, source_target_pairs={{0,4},{1,5},{2,6},{3,7},{4,0},{5,1},{6,2},{7,3},{8,12},{9,13},{10,... | collective-permute-start | bytes 49160 | tf_op jit(solution)/shard_map/ppermute | solution.py:8
  3.1 5.6 %collective-permute-start.1 = (bf16[1,8192]{1,0:T(2,128)(2,1)}, bf16[1,8192]{1,0:T(2,128)(2,1)S(1)}, u32[]{:S(2)}, u32[]{:S(2)}) collective-permute-start(bf16[1,8192]{1,0:T(2,128)(2,1)} %param.7), channel_id=1, source_target_pairs={{0,8},{1,9},{2,10},{3,11},{4,12},{5,13},{6,14},{7,15},{8,0},{9,1},... | collective-permute-start | bytes 49160 | tf_op jit(solution)/shard_map/ppermute | solution.py:8
  5.7 5.9 %collective-permute-start.2 = (bf16[1,8192]{1,0:T(2,128)(2,1)}, bf16[1,8192]{1,0:T(2,128)(2,1)S(1)}, u32[]{:S(2)}, u32[]{:S(2)}) collective-permute-start(bf16[1,8192]{1,0:T(2,128)(2,1)} %param.7), channel_id=1, source_target_pairs={{0,12},{1,13},{2,14},{3,15},{4,8},{5,9},{6,10},{7,11},{8,4},{9,5},... | collective-permute-start | bytes 49160 | tf_op jit(solution)/shard_map/ppermute | solution.py:8
  12.5 2.9 %collective-permute-start.3 = (bf16[4,1,8192]{2,0,1:T(4,128)(2,1)S(1)}, bf16[4,1,8192]{2,0,1:T(4,128)(2,1)S(1)}, u32[]{:S(2)}, u32[]{:S(2)}) collective-permute-start(bf16[4,1,8192]{2,0,1:T(4,128)(2,1)S(1)} %pad_maximum_fusion.2), channel_id=1, source_target_pairs={{0,1},{1,0},{2,3},{3,2},{4,5},{5,4},{6,7},{7,6},{8,9},{9,8},{10,11... | collective-permute-start | bytes 196616 | tf_op jit(solution)/shard_map/ppermute | solution.py:8
  12.6 4.5 %collective-permute-start.4 = (bf16[4,1,8192]{2,0,1:T(4,128)(2,1)S(1)}, bf16[4,1,8192]{2,0,1:T(4,128)(2,1)S(1)}, u32[]{:S(2)}, u32[]{:S(2)}) collective-permute-start(bf16[4,1,8192]{2,0,1:T(4,128)(2,1)S(1)} %pad_maximum_fusion.2), channel_id=1, source_target_pairs={{0,2},{1,3},{2,0},{3,1},{4,6},{5,7},{6,4},{7,5},{8,10},{9,11},{10,... | collective-permute-start | bytes 196616 | tf_op jit(solution)/shard_map/ppermute | solution.py:8
  14.2 4.0 %collective-permute-start.5 = (bf16[4,1,8192]{2,0,1:T(4,128)(2,1)S(1)}, bf16[4,1,8192]{2,0,1:T(4,128)(2,1)S(1)}, u32[]{:S(2)}, u32[]{:S(2)}) collective-permute-start(bf16[4,1,8192]{2,0,1:T(4,128)(2,1)S(1)} %pad_maximum_fusion.2), channel_id=1, source_target_pairs={{0,3},{1,2},{2,1},{3,0},{4,7},{5,6},{6,5},{7,4},{8,11},{9,10},{10,... | collective-permute-start | bytes 196616 | tf_op jit(solution)/shard_map/ppermute | solution.py:8
  25.0 4.7 %collective-permute-start.6 = (bf16[16,512]{1,0:T(8,128)(2,1)S(1)}, bf16[16,512]{1,0:T(8,128)(2,1)S(1)}, u32[]{:S(2)}, u32[]{:S(2)}) collective-permute-start(bf16[16,512]{1,0:T(8,128)(2,1)S(1)} %gather_fusion), channel_id=1, source_target_pairs={{0,4},{1,5},{2,6},{3,7},{4,0},{5,1},{6,2},{7,3},{8,12},{9,13},{10,... | collective-permute-start | bytes 49160 | tf_op jit(solution)/shard_map/ppermute | solution.py:8
  25.1 4.7 %collective-permute-start.7 = (bf16[16,512]{1,0:T(8,128)(2,1)S(1)}, bf16[16,512]{1,0:T(8,128)(2,1)S(1)}, u32[]{:S(2)}, u32[]{:S(2)}) collective-permute-start(bf16[16,512]{1,0:T(8,128)(2,1)S(1)} %gather_fusion), channel_id=1, source_target_pairs={{0,8},{1,9},{2,10},{3,11},{4,12},{5,13},{6,14},{7,15},{8,0},{9,1},... | collective-permute-start | bytes 49160 | tf_op jit(solution)/shard_map/ppermute | solution.py:8
  26.0 5.5 %collective-permute-start.8 = (bf16[16,512]{1,0:T(8,128)(2,1)S(1)}, bf16[16,512]{1,0:T(8,128)(2,1)S(1)}, u32[]{:S(2)}, u32[]{:S(2)}) collective-permute-start(bf16[16,512]{1,0:T(8,128)(2,1)S(1)} %gather_fusion), channel_id=1, source_target_pairs={{0,12},{1,13},{2,14},{3,15},{4,8},{5,9},{6,10},{7,11},{8,4},{9,5},... | collective-permute-start | bytes 49160 | tf_op jit(solution)/shard_map/ppermute | solution.py:8
  31.5 2.0 %collective-permute-start.9 = (bf16[4,16,512]{2,1,0:T(8,128)(2,1)S(1)}, bf16[4,16,512]{2,1,0:T(8,128)(2,1)S(1)}, u32[]{:S(2)}, u32[]{:S(2)}) collective-permute-start(bf16[4,16,512]{2,1,0:T(8,128)(2,1)S(1)} %get-tuple-element.6), channel_id=1, source_target_pairs={{0,1},{1,0},{2,3},{3,2},{4,5},{5,4},{6,7},{7,6},{8,9},{9,8},{10,11... | collective-permute-start | bytes 196616 | tf_op jit(solution)/shard_map/ppermute | solution.py:8
  31.6 4.6 %collective-permute-start.10 = (bf16[4,16,512]{2,1,0:T(8,128)(2,1)S(1)}, bf16[4,16,512]{2,1,0:T(8,128)(2,1)S(1)}, u32[]{:S(2)}, u32[]{:S(2)}) collective-permute-start(bf16[4,16,512]{2,1,0:T(8,128)(2,1)S(1)} %get-tuple-element.6), channel_id=1, source_target_pairs={{0,2},{1,3},{2,0},{3,1},{4,6},{5,7},{6,4},{7,5},{8,10},{9,11},{10,... | collective-permute-start | bytes 196616 | tf_op jit(solution)/shard_map/ppermute | solution.py:8
  33.0 4.3 %collective-permute-start.11 = (bf16[4,16,512]{2,1,0:T(8,128)(2,1)S(1)}, bf16[4,16,512]{2,1,0:T(8,128)(2,1)S(1)}, u32[]{:S(2)}, u32[]{:S(2)}) collective-permute-start(bf16[4,16,512]{2,1,0:T(8,128)(2,1)S(1)} %get-tuple-element.6), channel_id=1, source_target_pairs={{0,3},{1,2},{2,1},{3,0},{4,7},{5,6},{6,5},{7,4},{8,11},{9,10},{10,... | collective-permute-start | bytes 196616 | tf_op jit(solution)/shard_map/ppermute | solution.py:8
  44.0 4.4 %collective-permute-start.12 = (f32[32,16]{0,1:T(8,128)S(1)}, f32[32,16]{0,1:T(8,128)S(1)}, u32[]{:S(2)}, u32[]{:S(2)}) collective-permute-start(f32[32,16]{0,1:T(8,128)S(1)} %get-tuple-element.10), channel_id=1, source_target_pairs={{0,4},{1,5},{2,6},{3,7},{4,0},{5,1},{6,2},{7,3},{8,12},{9,13},{10,... | collective-permute-start | bytes 6152 | tf_op jit(solution)/shard_map/ppermute | solution.py:8
  44.3 5.4 %collective-permute-start.13 = (f32[32,16]{0,1:T(8,128)S(1)}, f32[32,16]{0,1:T(8,128)S(1)}, u32[]{:S(2)}, u32[]{:S(2)}) collective-permute-start(f32[32,16]{0,1:T(8,128)S(1)} %get-tuple-element.12), channel_id=1, source_target_pairs={{0,8},{1,9},{2,10},{3,11},{4,12},{5,13},{6,14},{7,15},{8,0},{9,1},... | collective-permute-start | bytes 6152 | tf_op jit(solution)/shard_map/ppermute | solution.py:8
  48.1 5.4 %collective-permute-start.14 = (f32[32,16]{0,1:T(8,128)S(1)}, f32[32,16]{0,1:T(8,128)S(1)}, u32[]{:S(2)}, u32[]{:S(2)}) collective-permute-start(f32[32,16]{0,1:T(8,128)S(1)} %get-tuple-element.11), channel_id=1, source_target_pairs={{0,12},{1,13},{2,14},{3,15},{4,8},{5,9},{6,10},{7,11},{8,4},{9,5},... | collective-permute-start | bytes 6152 | tf_op jit(solution)/shard_map/ppermute | solution.py:8
  53.6 1.9 %collective-permute-start.15 = (f32[8,16]{0,1:T(8,128)S(1)}, f32[8,16]{0,1:T(8,128)S(1)}, u32[]{:S(2)}, u32[]{:S(2)}) collective-permute-start(f32[8,16]{0,1:T(8,128)S(1)} %get-tuple-element.7), channel_id=1, source_target_pairs={{0,1},{1,0},{2,3},{3,2},{4,5},{5,4},{6,7},{7,6},{8,9},{9,8},{10,11... | collective-permute-start | bytes 1544 | tf_op jit(solution)/shard_map/ppermute | solution.py:8
  53.7 3.7 %collective-permute-start.16 = (f32[8,16]{0,1:T(8,128)S(1)}, f32[8,16]{0,1:T(8,128)S(1)}, u32[]{:S(2)}, u32[]{:S(2)}) collective-permute-start(f32[8,16]{0,1:T(8,128)S(1)} %get-tuple-element.9), channel_id=1, source_target_pairs={{0,2},{1,3},{2,0},{3,1},{4,6},{5,7},{6,4},{7,5},{8,10},{9,11},{10,... | collective-permute-start | bytes 1544 | tf_op jit(solution)/shard_map/ppermute | solution.py:8
  54.8 3.1 %collective-permute-start.17 = (f32[8,16]{0,1:T(8,128)S(1)}, f32[8,16]{0,1:T(8,128)S(1)}, u32[]{:S(2)}, u32[]{:S(2)}) collective-permute-start(f32[8,16]{0,1:T(8,128)S(1)} %get-tuple-element.8), channel_id=1, source_target_pairs={{0,3},{1,2},{2,1},{3,0},{4,7},{5,6},{6,5},{7,4},{8,11},{9,10},{10,... | collective-permute-start | bytes 1544 | tf_op jit(solution)/shard_map/ppermute | solution.py:8

commit v2 on v1

v2 whole, which is shorter than its diff:
```python
import functools

import jax
import jax.numpy as jnp
from jax import lax
from jax.experimental import pallas as pl
from jax.experimental.pallas import tpu as pltpu
from jax.sharding import PartitionSpec as P

ROWS_BY_ROWS = (((1,), (1,)), ((), ()))
VMEM = pl.BlockSpec(memory_space=pltpu.VMEM)
HBM = pl.BlockSpec(memory_space=pltpu.HBM)
SMEM = pl.BlockSpec(memory_space=pltpu.SMEM)


def dot(a, b, dims=ROWS_BY_ROWS):
    return lax.dot_general(a, b, dims, preferred_element_type=jnp.float32)


def near_memory(x):
    return pltpu.with_memory_space_constraint(x, pltpu.VMEM)


def far_memory(x):
    return pltpu.with_memory_space_constraint(x, pltpu.HBM)


def call(body, name, out_shape, flops, moved, limit=12):
    return functools.partial(
        pl.pallas_call,
        body,
        out_shape=out_shape,
        compiler_params=pltpu.CompilerParams(vmem_limit_bytes=limit << 20),
        cost_estimate=pl.CostEstimate(flops=flops, bytes_accessed=moved, transcendentals=0),
        name=name,
    )


def send(x, size, mask):
    return lax.ppermute(x, "blk", [(i, i ^ mask) for i in range(size)])


def start_copies(ref, start, out, sems):
    pieces = sems.shape[0]
    rows = out.shape[0] // pieces
    copies = []
    for i in range(pieces):
        here, there = pl.ds(start + i * rows, rows), pl.ds(i * rows, rows)
        copies.append(pltpu.make_async_copy(ref.at[here], out.at[there], sems.at[i]))
        copies[-1].start()
    return copies


def fetch(x, after):
    def body(x_ref, _, out_ref, sems):
        for copy in start_copies(x_ref, 0, out_ref, sems):
            copy.wait()

    run = call(body, "fetch", pltpu.VMEM(x.shape, x.dtype), 0, 2 * x.size * x.dtype.itemsize, 1)(
        in_specs=[HBM, pl.BlockSpec(memory_space=pl.ANY)], out_specs=VMEM, scratch_shapes=[pltpu.SemaphoreType.DMA((1,))]
    )
    return near_memory(run(far_memory(x), after))


def split(size):
    inner = 1
    while inner * inner * 4 <= size:
        inner *= 2
    return size // inner, inner


def far_masks(size):
    outer, inner = split(size)
    return [s * inner + (s > 0 and inner > 1) for s in range(outer)]


def pack_body(*refs):
    out = refs[-1]
    out[...] = jnp.concatenate([r[...].astype(jnp.float32) for r in refs[:-1]], axis=0).astype(out.dtype)


def panel_body(me_ref, *refs, outer, inner):
    parts, hess_ref, docs_ref = refs[:inner], refs[inner], refs[inner + 1]
    out_ref, docs_out, sems = refs[inner + 2 :]
    copies = start_copies(docs_ref, 0, docs_out, sems)
    vals = jnp.concatenate([r[...].astype(jnp.float32) for r in parts], axis=0).astype(jnp.bfloat16)
    count = vals.shape[0]
    each = count // (outer * inner)
    to = lax.broadcasted_iota(jnp.int32, (count, count), 0)
    at = lax.broadcasted_iota(jnp.int32, (count, count), 1)
    block = at // each
    s = block % outer
    origin = me_ref[0] ^ (s * inner + jnp.where(s > 0, int(inner > 1), 0)) ^ (block // outer)
    place = (to == origin * each + at % each).astype(jnp.float32).astype(jnp.bfloat16)
    out_ref[...] = dot(place, dot(hess_ref[...], vals).astype(jnp.bfloat16)).astype(out_ref.dtype)
    for copy in copies:
        copy.wait()


def scores_of(me, docs_ref, slices_ref, step, inner):
    outer, _, rows = slices_ref.shape
    total = None
    for s, mask in enumerate(far_masks(outer * inner)):
        column = pl.multiple_of((me ^ mask ^ step) * rows, rows)
        part = dot(slices_ref[s], docs_ref[:, pl.ds(column, rows)])
        total = part if total is None else total + part
    return total


def add_scores(me, docs_refs, slices_ref, step, inner):
    return jnp.concatenate([scores_of(me, r, slices_ref, step, inner) for r in docs_refs], axis=1)


def first_body(
    me_ref, low_ref, docs_ref, slices_ref, mask_ref, member_ref, slot_ref, out_ref, hot_ref, wide_ref, high_ref, sems, *, inner
):
    split_at = low_ref.shape[0]
    copies = start_copies(docs_ref, split_at, high_ref, sems)
    out_ref[:, :split_at] = scores_of(me_ref[0], low_ref, slices_ref, 0, inner)
    clusters, docs = hot_ref.shape
    row = lax.broadcasted_iota(jnp.int32, (clusters, clusters), 0)
    by_slot = (row == slot_ref[...]).astype(jnp.float32).astype(jnp.bfloat16)
    cluster = lax.broadcasted_iota(jnp.int32, (clusters, docs), 0)
    by_doc = (cluster == member_ref[...]).astype(jnp.float32).astype(jnp.bfloat16)
    hot_ref[...] = dot(by_slot, by_doc, (((1,), (0,)), ((), ()))).astype(jnp.bfloat16)
    blocks = mask_ref.shape[0]
    doc = lax.broadcasted_iota(jnp.int32, (blocks, docs), 1)
    spread = (doc // (docs // blocks) == lax.broadcasted_iota(jnp.int32, (blocks, docs), 0)).astype(jnp.float32)
    narrow = mask_ref[...].astype(jnp.float32)
    wide_ref[...] = dot(narrow.astype(jnp.bfloat16), spread.astype(jnp.bfloat16), (((0,), (0,)), ((), ())))
    for copy in copies:
        copy.wait()
    out_ref[:, split_at:] = scores_of(me_ref[0], high_ref, slices_ref, 0, inner)


def next_body(me_ref, low_ref, high_ref, slices_ref, sum_ref, out_ref, *, step, inner):
    out_ref[...] = sum_ref[...] + add_scores(me_ref[0], (low_ref, high_ref), slices_ref, step, inner)


def last_body(me_ref, low_ref, high_ref, slices_ref, sum_ref, hot_ref, wide_ref, out_ref, *, step, inner):
    scores = sum_ref[...] + add_scores(me_ref[0], (low_ref, high_ref), slices_ref, step, inner)
    masked = 0.125 * (scores * wide_ref[...])
    high = masked.astype(jnp.bfloat16)
    low = (masked - high.astype(jnp.float32)).astype(jnp.bfloat16)
    out_ref[...] = dot(hot_ref[...], high) + dot(hot_ref[...], low)


def total_body(parts_ref, out_ref):
    kept, count = out_ref.shape
    total = jnp.sum(parts_ref[...], axis=0, keepdims=True)
    out_ref[...] = jnp.concatenate([total[:, r * count : (r + 1) * count] for r in range(kept)], axis=0)


def wide_sums(me, near, docs_in, topic_mask, membership, owner_slot, *, size):
    outer, inner = split(size)
    docs, width = docs_in.shape
    clusters = owner_slot.shape[0]
    order = jnp.argsort((me ^ (jnp.array(far_masks(size))[:, None] ^ jnp.arange(inner))).reshape(-1))
    slices = jnp.stack(near, axis=1).reshape((size,) + near[0].shape[1:])[order]
    precond = jnp.moveaxis(slices, 0, 1).reshape(-1, width)
    blocks = topic_mask.shape[0]
    mask = jnp.repeat(topic_mask.T.astype(jnp.float32), docs // blocks, axis=1)
    mask = jnp.repeat(mask, precond.shape[0] // mask.shape[0], axis=0)
    masked = 0.125 * (dot(precond, docs_in) * mask)
    by_slot = (jnp.arange(clusters)[:, None] == owner_slot[None, :]).astype(jnp.bfloat16)
    by_doc = (jnp.arange(clusters)[:, None] == membership[None, :]).astype(jnp.bfloat16)
    hot = jnp.dot(by_slot, by_doc, preferred_element_type=jnp.float32).astype(jnp.bfloat16)
    return dot(hot, masked.astype(jnp.bfloat16))


def tiled_sums(me, near, docs_low, doc_grads, topic_mask, membership, owner_slot, *, size):
    outer, inner = split(size)
    docs, width = doc_grads.shape
    clusters = owner_slot.shape[0]
    count = near[0].shape[1]
    work = dict(flops=2 * count * docs * width // inner, moved=2 * docs * width // inner)
    sums, hot, wide, docs_high = call(
        functools.partial(first_body, inner=inner),
        "scores_0",
        (
            jax.ShapeDtypeStruct((count, docs), jnp.float32),
            jax.ShapeDtypeStruct((clusters, docs), jnp.bfloat16),
            jax.ShapeDtypeStruct((count, docs), jnp.float32),
            pltpu.VMEM((docs - docs_low.shape[0], width), doc_grads.dtype),
        ),
        **work,
    )(
        in_specs=[SMEM, VMEM, HBM] + [VMEM] * 4,
        out_specs=(VMEM,) * 4,
        scratch_shapes=[pltpu.SemaphoreType.DMA((1,))],
    )(
        me,
        docs_low,
        far_memory(doc_grads),
        near[0],
        topic_mask,
        membership.reshape(1, docs),
        owner_slot.reshape(1, clusters),
    )
    near_docs = (docs_low, near_memory(docs_high))
    for t in range(1, inner - 1):
        sums = call(
            functools.partial(next_body, step=t, inner=inner),
            f"scores_{t}",
            jax.ShapeDtypeStruct((count, docs), jnp.float32),
            **work,
        )(in_specs=[SMEM] + [VMEM] * 4, out_specs=VMEM)(me, *near_docs, near[t], sums)
    return call(
        functools.partial(last_body, step=inner - 1, inner=inner),
        "sums",
        jax.ShapeDtypeStruct((clusters, count), jnp.float32),
        **work,
    )(in_specs=[SMEM] + [VMEM] * 6, out_specs=VMEM)(me, *near_docs, near[inner - 1], sums, hot, wide)


def per_device(doc_grads, val_grads, inv_hessian, topic_mask, membership, owner_slot, *, size):
    outer, inner = split(size)
    me = lax.axis_index("blk").astype(jnp.int32).reshape(1)
    docs = doc_grads.shape[0]
    val_local, width = val_grads.shape
    rows = inv_hessian.shape[0]
    clusters = owner_slot.shape[0]
    kept = clusters // size
    count = size * val_local
    masks = far_masks(size)[1:]

    far = [val_grads] + [send(val_grads, size, mask) for mask in masks]
    far[0] = fetch(val_grads, far[1])
    far = call(
        pack_body, "pack", jax.ShapeDtypeStruct((outer * val_local, width), jnp.bfloat16), 0, 4 * outer * width
    )(in_specs=[VMEM] * outer, out_specs=VMEM)(*far)
    near = [far] + [send(far, size, t) for t in range(1, inner)]
    near_hess = fetch(inv_hessian, far)
    early = docs * 3 // 4
    panel, docs_low = call(
        functools.partial(panel_body, outer=outer, inner=inner),
        "panel",
        (jax.ShapeDtypeStruct((count, rows), jnp.bfloat16), pltpu.VMEM((early, width), doc_grads.dtype)),
        2 * count * rows * width,
        2 * rows * width,
        16,
    )(
        in_specs=[SMEM] + [VMEM] * (inner + 1) + [HBM],
        out_specs=(VMEM, VMEM),
        scratch_shapes=[pltpu.SemaphoreType.DMA((1,))],
    )(me, *near, near_hess, far_memory(doc_grads))

    far = jnp.stack([panel] + [send(panel, size, mask) for mask in masks])
    near = [far] + [send(far, size, t) for t in range(1, inner)]
    if rows % 128 == 0:
        sums = tiled_sums(me, near, near_memory(docs_low), doc_grads, topic_mask, membership, owner_slot, size=size)
    else:
        sums = wide_sums(me, near, doc_grads, topic_mask, membership, owner_slot, size=size)

    sums = lax.all_to_all(sums.reshape(size, kept * count), "blk", 0, 0, tiled=True)
    return call(total_body, "total", jax.ShapeDtypeStruct((kept, count), jnp.float32), 0, 8 * size * kept * count)(
        in_specs=[VMEM], out_specs=VMEM
    )(sums)


def solution(mesh):
    size = mesh.shape["blk"]

    def run(*args):
        return per_device(*args, size=size)

    in_specs = (
        P(("grp", "blk"), None),
        P("blk", None),
        P("blk", None),
        P(("grp", "blk"), None),
        P(("grp", "blk")),
        P(),
    )
    out_specs = P(("grp", "blk"), None)
    return jax.shard_map(run, mesh=mesh, in_specs=in_specs, out_specs=out_specs, check_vma=False)
```

time: 58.9 us -> 43.7 us (0.74)
  waiting for transfers between devices: 21.6 us -> 7.33 us
  Pallas kernels: 0 us -> 12.3 us
  matrix products: 11.8 us -> 0 us
  blocking collectives: 0 us -> 10.6 us
  starting transfers between devices: 20.3 us -> 12.9 us
  local copies, waits for them, and re-layouts: 2.55 us -> 0.09 us
  other arithmetic: 2.22 us -> 0.01 us
    ppermute x18 -> x12, waiting for transfers between devices: 21.6 us -> 7.33 us  [send(): return lax.ppermute(x, 'blk', [(i, i ^ mask) for i in range(size)])]
    pallas_call x0 -> x9, Pallas kernels: none -> 12.3 us  [the longest x2 4.19 us: fetch(): return near_memory(run(far_memory(x), after))]
    dot_general x5 -> x0, matrix products: 11.8 us -> none  [the longest x1 5.65 us: per_device(): lax.dot_general(precond, doc_grads, (((1,), (1,)), ((), ())), preferred_e...]
    all_to_all x0 -> x1, blocking collectives: none -> 10.6 us  [per_device(): lax.all_to_all(sums.reshape(size, kept * count), 'blk', 0, 0, tiled=True)]
    ppermute x18 -> x12, starting transfers between devices: 20.3 us -> 12.9 us  [send(): return lax.ppermute(x, 'blk', [(i, i ^ mask) for i in range(size)])]
    another operation x5 -> x1, other arithmetic: 2.12 us -> 0.01 us  [per_device(): far = jnp.stack([panel] + [send(panel, size, mask) for mask in masks])]
    gather x2 -> x0, local copies, waits for them, and re-layouts: 1.17 us -> none  [the longest x1 0.61 us: per_device(): panel.reshape(size, val_local, rows)[order].reshape(size * val_local, rows)]
    add x2 -> x0, local copies, waits for them, and re-layouts: 0.75 us -> none  [the longest x1 0.66 us: per_device(): total = total + send(near[t], size, t)]
  transfers between devices with their start and end apart: 18 -> 12, of which waited for: 12 -> 6; matrix products, arithmetic and copies ran while one was open for 2% -> 0% of each run, Pallas kernels for 0% -> 18%
where the time goes in v2:
time: 43.7 us; the launch traced here: 43.4 us
  starting transfers between devices  12.9 us (30%)
  Pallas kernels  12.3 us (28%)
  blocking collectives  10.6 us (24%)
  waiting for transfers between devices  7.33 us (17%)
    ppermute x12, starting transfers between devices, send(): return lax.ppermute(x, 'blk', [(i, i ^ mask) for i in range(size)])  12.9 us
    all_to_all x1, blocking collectives, per_device(): lax.all_to_all(sums.reshape(size, kept * count), 'blk', 0, 0, tiled=True)  10.6 us
    ppermute x12, waiting for transfers between devices, send(): return lax.ppermute(x, 'blk', [(i, i ^ mask) for i in range(size)])  7.33 us
    pallas_call x2, Pallas kernels, fetch(): return near_memory(run(far_memory(x), after))  4.19 us
    pallas_call x1, Pallas kernels, per_device(): call(functools.partial(panel_body, outer=outer, inner=inner), 'panel', (j...  2.83 us
    pallas_call x1, Pallas kernels, tiled_sums(): call(functools.partial(first_body, inner=inner), 'scores_0', (jax.ShapeDt...  2.36 us
    pallas_call x2, Pallas kernels, tiled_sums(): call(functools.partial(next_body, step=t, inner=inner), f'scores_{t}', ja...  1.26 us
    pallas_call x1, Pallas kernels, tiled_sums(): call(functools.partial(last_body, step=inner - 1, inner=inner), 'sums', j...  0.94 us
  transfers between devices with their start and end apart: 12, of which 6 were waited for; matrix products, arithmetic and copies ran while one was open for 0% of the time, Pallas kernels for 18%

profile of v2, /device:TPU:0, one launch (start us, length us, event | category | flops | bytes accessed | tf_op | source)
XLA Modules:
  0.0 43.4 jit_solution(6446138315800154226)
XLA Ops:
  0.0 2.5 %collective-permute-start = (bf16[1,8192]{1,0:T(2,128)(2,1)}, bf16[1,8192]{1,0:T(2,128)(2,1)S(1)}, u32[]{:S(2)}, u32[]{:S(2)}) collective-permute-start(bf16[1,8192]{1,0:T(2,128)(2,1)} %x_ref.2), channel_id=1, source_target_pairs={{0,5},{1,4},{2,7},{3,6},{4,1},{5,0},{6,3},{7,2},{8,13},{9,12},{10,... | collective-permute-start | bytes 49160 | tf_op jit(solution)/shard_map/ppermute | solution.py:40
  2.5 2.8 %collective-permute-start.2 = (bf16[1,8192]{1,0:T(2,128)(2,1)}, bf16[1,8192]{1,0:T(2,128)(2,1)S(1)}, u32[]{:S(2)}, u32[]{:S(2)}) collective-permute-start(bf16[1,8192]{1,0:T(2,128)(2,1)} %x_ref.2), channel_id=1, source_target_pairs={{0,13},{1,12},{2,15},{3,14},{4,9},{5,8},{6,11},{7,10},{8,5},{9,4},... | collective-permute-start | bytes 49160 | tf_op jit(solution)/shard_map/ppermute | solution.py:40
  5.2 0.1 collective-permute-start.1
  5.3 0.0 collective-permute-done._.refs_1_
  5.3 0.8 %fetch.2.refs_0_ = bf16[1,8192]{1,0:T(2,128)(2,1)S(1)} custom-call(bf16[1,8192]{1,0:T(2,128)(2,1)} %x_ref.2, bf16[1,8192]{1,0:T(2,128)(2,1)S(1)} %collective-permute-done._.refs_1_), custom_call_target="tpu_custom_call" | custom-call | bytes 32768 | tf_op jit(solution)/shard_map/fetch/pallas_call | solution.py:62
  6.1 1.7 %collective-permute-done.2.refs_3_ = bf16[1,8192]{1,0:T(2,128)(2,1)S(1)} collective-permute-done((bf16[1,8192]{1,0:T(2,128)(2,1)}, bf16[1,8192]{1,0:T(2,128)(2,1)S(1)}, u32[]{:S(2)}, u32[]{:S(2)}) %collective-permute-start.2) | collective-permute-done | bytes 16416 | tf_op jit(solution)/shard_map/ppermute | solution.py:40
  7.9 2.7 %collective-permute-done.1.refs_2_ = bf16[1,8192]{1,0:T(2,128)(2,1)S(1)} collective-permute-done((bf16[1,8192]{1,0:T(2,128)(2,1)}, bf16[1,8192]{1,0:T(2,128)(2,1)S(1)}, u32[]{:S(2)}, u32[]{:S(2)}) %collective-permute-start.1) | collective-permute-done | bytes 16416 | tf_op jit(solution)/shard_map/ppermute | solution.py:40
  10.6 0.1 pack.1._.refs_0_
  10.7 1.3 %collective-permute-start.5 = (bf16[4,8192]{1,0:T(4,128)(2,1)S(1)}, bf16[4,8192]{1,0:T(4,128)(2,1)S(1)}, u32[]{:S(2)}, u32[]{:S(2)}) collective-permute-start(bf16[4,8192]{1,0:T(4,128)(2,1)S(1)} %pack.1._.refs_0_), channel_id=1, source_target_pairs={{0,3},{1,2},{2,1},{3,0},{4,7},{5,6},{6,5},{7,4},{8,11},{9,10},{10,... | collective-permute-start | bytes 196616 | tf_op jit(solution)/shard_map/ppermute | solution.py:40
  12.0 0.5 %collective-permute-start.4 = (bf16[4,8192]{1,0:T(4,128)(2,1)S(1)}, bf16[4,8192]{1,0:T(4,128)(2,1)S(1)}, u32[]{:S(2)}, u32[]{:S(2)}) collective-permute-start(bf16[4,8192]{1,0:T(4,128)(2,1)S(1)} %pack.1._.refs_0_), channel_id=1, source_target_pairs={{0,2},{1,3},{2,0},{3,1},{4,6},{5,7},{6,4},{7,5},{8,10},{9,11},{10,... | collective-permute-start | bytes 196616 | tf_op jit(solution)/shard_map/ppermute | solution.py:40
  12.5 0.1 collective-permute-start.3
  12.6 3.4 %fetch.3.refs_4_ = bf16[512,8192]{1,0:T(8,128)(2,1)S(1)} custom-call(bf16[512,8192]{1,0:T(8,128)(2,1)} %x_ref.3, bf16[4,8192]{1,0:T(4,128)(2,1)S(1)} %pack.1._.refs_0_), custom_call_target="tpu_custom_call" | custom-call | bytes 16777216 | tf_op jit(solution)/shard_map/fetch/pallas_call | solution.py:62
  16.0 0.0 collective-permute-done.5.refs_3_
  16.1 0.5 %collective-permute-done.4.refs_2_ = bf16[4,8192]{1,0:T(4,128)(2,1)S(1)} collective-permute-done((bf16[4,8192]{1,0:T(4,128)(2,1)S(1)}, bf16[4,8192]{1,0:T(4,128)(2,1)S(1)}, u32[]{:S(2)}, u32[]{:S(2)}) %collective-permute-start.4) | collective-permute-done | bytes 65568 | tf_op jit(solution)/shard_map/ppermute | solution.py:40
  16.6 0.0 collective-permute-done.3.refs_1_
  16.6 0.0 copy-start
  16.6 0.0 copy-start.1
  16.6 0.0 copy-start.2
  16.6 2.8 %panel.1 = (bf16[16,512]{1,0:T(8,128)(2,1)S(1)}, bf16[384,8192]{1,0:T(8,128)(2,1)S(1)}) custom-call(s32[1]{0:T(128)} %bitcast.me_ref, bf16[4,8192]{1,0:T(4,128)(2,1)S(1)} %pack.1._.refs_0_, bf16[4,8192]{1,0:T(4,128)(2,1)S(1)} %collective-permute-done.3.refs_1_, bf16[4,8192]{1,0:T(4,128)(2,1)S(1)} %collective-permute-done.4.refs_2_, ...), custom_call_target="tpu_custom_call" | custom-call | flops 134217728 | bytes 8388608 | tf_op jit(solution)/shard_map/panel/pallas_call | solution.py:235
  19.4 1.2 %collective-permute-start.8 = (bf16[16,512]{1,0:T(8,128)(2,1)S(1)}, bf16[16,512]{1,0:T(8,128)(2,1)S(1)}, u32[]{:S(2)}, u32[]{:S(2)}) collective-permute-start(bf16[16,512]{1,0:T(8,128)(2,1)S(1)} %get-tuple-element.12), channel_id=1, source_target_pairs={{0,13},{1,12},{2,15},{3,14},{4,9},{5,8},{6,11},{7,10},{8,5},{9,4},... | collective-permute-start | bytes 49160 | tf_op jit(solution)/shard_map/ppermute | solution.py:40
  20.6 0.2 collective-permute-start.7
  20.8 2.2 %collective-permute-start.6 = (bf16[16,512]{1,0:T(8,128)(2,1)S(1)}, bf16[16,512]{1,0:T(8,128)(2,1)S(1)}, u32[]{:S(2)}, u32[]{:S(2)}) collective-permute-start(bf16[16,512]{1,0:T(8,128)(2,1)S(1)} %get-tuple-element.12), channel_id=1, source_target_pairs={{0,5},{1,4},{2,7},{3,6},{4,1},{5,0},{6,3},{7,2},{8,13},{9,12},{10,... | collective-permute-start | bytes 49160 | tf_op jit(solution)/shard_map/ppermute | solution.py:40
  23.1 1.5 %collective-permute-done.8 = bf16[16,512]{1,0:T(8,128)(2,1)S(1)} collective-permute-done((bf16[16,512]{1,0:T(8,128)(2,1)S(1)}, bf16[16,512]{1,0:T(8,128)(2,1)S(1)}, u32[]{:S(2)}, u32[]{:S(2)}) %collective-permute-start.8) | collective-permute-done | bytes 16416 | tf_op jit(solution)/shard_map/ppermute | solution.py:40
  24.6 0.6 %collective-permute-done.7 = bf16[16,512]{1,0:T(8,128)(2,1)S(1)} collective-permute-done((bf16[16,512]{1,0:T(8,128)(2,1)S(1)}, bf16[16,512]{1,0:T(8,128)(2,1)S(1)}, u32[]{:S(2)}, u32[]{:S(2)}) %collective-permute-start.7) | collective-permute-done | bytes 16416 | tf_op jit(solution)/shard_map/ppermute | solution.py:40
  25.1 0.0 collective-permute-done.6
  25.2 0.2 collective-permute-start.11
  25.4 1.5 %collective-permute-start.10 = (bf16[4,16,512]{2,1,0:T(8,128)(2,1)S(1)}, bf16[4,16,512]{2,1,0:T(8,128)(2,1)S(1)}, u32[]{:S(2)}, u32[]{:S(2)}) collective-permute-start(bf16[4,16,512]{2,1,0:T(8,128)(2,1)S(1)} %pad_maximum_fusion.slices_ref), channel_id=1, source_target_pairs={{0,2},{1,3},{2,0},{3,1},{4,6},{5,7},{6,4},{7,5},{8,10},{9,11},{10,... | collective-permute-start | bytes 196616 | tf_op jit(solution)/shard_map/ppermute | solution.py:40
  26.9 0.2 collective-permute-start.9
  27.1 0.0 copy-done
  27.1 0.0 copy-done.1
  27.1 0.0 copy-done.2
  27.1 2.4 %scores_0.1 = (f32[16,512]{1,0:T(8,128)S(1)}, bf16[128,512]{1,0:T(8,128)(2,1)S(1)}, f32[16,512]{1,0:T(8,128)S(1)}, bf16[128,8192]{1,0:T(8,128)(2,1)S(1)}) custom-call(s32[1]{0:T(128)} %bitcast.me_ref, bf16[384,8192]{1,0:T(8,128)(2,1)S(1)} %get-tuple-element.11.low_ref, bf16[512,8192]{1,0:T(8,128)(2,1)} %docs_ref.1, ...), custom_call_target="tpu_custom_call" | custom-call | flops 33554432 | bytes 2097152 | tf_op jit(solution)/shard_map/scores_0/pallas_call | solution.py:177
  29.5 0.0 collective-permute-done.11.slices_ref
  29.5 0.6 %scores_1.1.sum_ref = f32[16,512]{1,0:T(8,128)S(1)} custom-call(s32[1]{0:T(128)} %bitcast.me_ref, bf16[384,8192]{1,0:T(8,128)(2,1)S(1)} %get-tuple-element.11.low_ref, bf16[128,8192]{1,0:T(8,128)(2,1)S(1)} %get-tuple-element.13.high_ref, bf16[4,16,512]{2,1,0:T(8,128)(2,1)S(1)} %collective-permute-done.11.slices_ref, f32[16,512]{1,0:T(8,128)S(1)} %get-tuple-element.14.sum_ref), custom_call_target="tpu_custom_call" | custom-call | flops 33554432 | bytes 2097152 | tf_op jit(solution)/shard_map/scores_1/pallas_call | solution.py:202
  30.1 0.0 collective-permute-done.10.slices_ref
  30.1 0.6 %scores_2.1.sum_ref = f32[16,512]{1,0:T(8,128)S(1)} custom-call(s32[1]{0:T(128)} %bitcast.me_ref, bf16[384,8192]{1,0:T(8,128)(2,1)S(1)} %get-tuple-element.11.low_ref, bf16[128,8192]{1,0:T(8,128)(2,1)S(1)} %get-tuple-element.13.high_ref, bf16[4,16,512]{2,1,0:T(8,128)(2,1)S(1)} %collective-permute-done.10.slices_ref, f32[16,512]{1,0:T(8,128)S(1)} %scores_1.1.sum_ref), custom_call_target="tpu_custom_call" | custom-call | flops 33554432 | bytes 2097152 | tf_op jit(solution)/shard_map/scores_2/pallas_call | solution.py:202
  30.8 0.3 collective-permute-done.9.slices_ref
  31.0 0.9 %sums.1 = f32[128,16]{1,0:T(8,128)S(1)} custom-call(s32[1]{0:T(128)} %bitcast.me_ref, bf16[384,8192]{1,0:T(8,128)(2,1)S(1)} %get-tuple-element.11.low_ref, bf16[128,8192]{1,0:T(8,128)(2,1)S(1)} %get-tuple-element.13.high_ref, bf16[4,16,512]{2,1,0:T(8,128)(2,1)S(1)} %collective-permute-done.9.slices_ref, f32[16,512]{1,0:T(8,128)S(1)} %scores_2.1.sum_ref, ...), custom_call_target="tpu_custom_call" | custom-call | flops 33554432 | bytes 2097152 | tf_op jit(solution)/shard_map/sums/pallas_call | solution.py:208
  32.0 0.1 all_to_all.7
  32.1 10.6 %all_to_all.11 = f32[16,1,128]{2,1,0:T(1,128)S(1)} all-to-all(f32[16,1,128]{2,1,0:T(1,128)S(1)} %bitcast.13), channel_id=1, replica_groups=mesh['grp'=2,'blk'=16] {'blk'}, dimensions={0} | all-to-all | bytes 16384 | tf_op jit(solution)/shard_map/all_to_all | solution.py:255
  42.7 0.7 %total.1 = f32[8,16]{1,0:T(8,128)} custom-call(f32[16,128]{1,0:T(8,128)S(1)} %bitcast.9), custom_call_target="tpu_custom_call" | custom-call | bytes 16384 | tf_op jit(solution)/shard_map/total/pallas_call | solution.py:256
  (1 shorter events, 0.0 us)
Async XLA Ops:
  0.0 5.3 %collective-permute-start = (bf16[1,8192]{1,0:T(2,128)(2,1)}, bf16[1,8192]{1,0:T(2,128)(2,1)S(1)}, u32[]{:S(2)}, u32[]{:S(2)}) collective-permute-start(bf16[1,8192]{1,0:T(2,128)(2,1)} %x_ref.2), channel_id=1, source_target_pairs={{0,5},{1,4},{2,7},{3,6},{4,1},{5,0},{6,3},{7,2},{8,13},{9,12},{10,... | collective-permute-start | bytes 49160 | tf_op jit(solution)/shard_map/ppermute | solution.py:40
  2.5 5.4 %collective-permute-start.2 = (bf16[1,8192]{1,0:T(2,128)(2,1)}, bf16[1,8192]{1,0:T(2,128)(2,1)S(1)}, u32[]{:S(2)}, u32[]{:S(2)}) collective-permute-start(bf16[1,8192]{1,0:T(2,128)(2,1)} %x_ref.2), channel_id=1, source_target_pairs={{0,13},{1,12},{2,15},{3,14},{4,9},{5,8},{6,11},{7,10},{8,5},{9,4},... | collective-permute-start | bytes 49160 | tf_op jit(solution)/shard_map/ppermute | solution.py:40
  5.2 5.4 %collective-permute-start.1 = (bf16[1,8192]{1,0:T(2,128)(2,1)}, bf16[1,8192]{1,0:T(2,128)(2,1)S(1)}, u32[]{:S(2)}, u32[]{:S(2)}) collective-permute-start(bf16[1,8192]{1,0:T(2,128)(2,1)} %x_ref.2), channel_id=1, source_target_pairs={{0,9},{1,8},{2,11},{3,10},{4,13},{5,12},{6,15},{7,14},{8,1},{9,0},... | collective-permute-start | bytes 49160 | tf_op jit(solution)/shard_map/ppermute | solution.py:40
  10.7 5.4 %collective-permute-start.5 = (bf16[4,8192]{1,0:T(4,128)(2,1)S(1)}, bf16[4,8192]{1,0:T(4,128)(2,1)S(1)}, u32[]{:S(2)}, u32[]{:S(2)}) collective-permute-start(bf16[4,8192]{1,0:T(4,128)(2,1)S(1)} %pack.1._.refs_0_), channel_id=1, source_target_pairs={{0,3},{1,2},{2,1},{3,0},{4,7},{5,6},{6,5},{7,4},{8,11},{9,10},{10,... | collective-permute-start | bytes 196616 | tf_op jit(solution)/shard_map/ppermute | solution.py:40
  12.0 4.6 %collective-permute-start.4 = (bf16[4,8192]{1,0:T(4,128)(2,1)S(1)}, bf16[4,8192]{1,0:T(4,128)(2,1)S(1)}, u32[]{:S(2)}, u32[]{:S(2)}) collective-permute-start(bf16[4,8192]{1,0:T(4,128)(2,1)S(1)} %pack.1._.refs_0_), channel_id=1, source_target_pairs={{0,2},{1,3},{2,0},{3,1},{4,6},{5,7},{6,4},{7,5},{8,10},{9,11},{10,... | collective-permute-start | bytes 196616 | tf_op jit(solution)/shard_map/ppermute | solution.py:40
  12.5 4.1 %collective-permute-start.3 = (bf16[4,8192]{1,0:T(4,128)(2,1)S(1)}, bf16[4,8192]{1,0:T(4,128)(2,1)S(1)}, u32[]{:S(2)}, u32[]{:S(2)}) collective-permute-start(bf16[4,8192]{1,0:T(4,128)(2,1)S(1)} %pack.1._.refs_0_), channel_id=1, source_target_pairs={{0,1},{1,0},{2,3},{3,2},{4,5},{5,4},{6,7},{7,6},{8,9},{9,8},{10,11... | collective-permute-start | bytes 196616 | tf_op jit(solution)/shard_map/ppermute | solution.py:40
  16.6 10.5 %copy-start = (s32[4,16]{1,0:T(4,128)S(1)}, s32[4,16]{1,0:T(4,128)}, u32[]{:S(2)}) copy-start(s32[4,16]{1,0:T(4,128)} %mask_ref.1) | copy-start | bytes 772
  16.6 10.5 %copy-start.1 = (s32[512]{0:T(512)S(1)}, s32[512]{0:T(512)}, u32[]{:S(2)}) copy-start(s32[512]{0:T(512)} %param.10) | copy-start | bytes 6148
  16.6 10.5 %copy-start.2 = (s32[128]{0:T(128)S(1)}, s32[128]{0:T(128)}, u32[]{:S(2)}) copy-start(s32[128]{0:T(128)} %param.11) | copy-start | bytes 1540
  19.4 5.2 %collective-permute-start.8 = (bf16[16,512]{1,0:T(8,128)(2,1)S(1)}, bf16[16,512]{1,0:T(8,128)(2,1)S(1)}, u32[]{:S(2)}, u32[]{:S(2)}) collective-permute-start(bf16[16,512]{1,0:T(8,128)(2,1)S(1)} %get-tuple-element.12), channel_id=1, source_target_pairs={{0,13},{1,12},{2,15},{3,14},{4,9},{5,8},{6,11},{7,10},{8,5},{9,4},... | collective-permute-start | bytes 49160 | tf_op jit(solution)/shard_map/ppermute | solution.py:40
  20.6 4.5 %collective-permute-start.7 = (bf16[16,512]{1,0:T(8,128)(2,1)S(1)}, bf16[16,512]{1,0:T(8,128)(2,1)S(1)}, u32[]{:S(2)}, u32[]{:S(2)}) collective-permute-start(bf16[16,512]{1,0:T(8,128)(2,1)S(1)} %get-tuple-element.12), channel_id=1, source_target_pairs={{0,9},{1,8},{2,11},{3,10},{4,13},{5,12},{6,15},{7,14},{8,1},{9,0},... | collective-permute-start | bytes 49160 | tf_op jit(solution)/shard_map/ppermute | solution.py:40
  20.8 4.3 %collective-permute-start.6 = (bf16[16,512]{1,0:T(8,128)(2,1)S(1)}, bf16[16,512]{1,0:T(8,128)(2,1)S(1)}, u32[]{:S(2)}, u32[]{:S(2)}) collective-permute-start(bf16[16,512]{1,0:T(8,128)(2,1)S(1)} %get-tuple-element.12), channel_id=1, source_target_pairs={{0,5},{1,4},{2,7},{3,6},{4,1},{5,0},{6,3},{7,2},{8,13},{9,12},{10,... | collective-permute-start | bytes 49160 | tf_op jit(solution)/shard_map/ppermute | solution.py:40
  25.2 4.3 %collective-permute-start.11 = (bf16[4,16,512]{2,1,0:T(8,128)(2,1)S(1)}, bf16[4,16,512]{2,1,0:T(8,128)(2,1)S(1)}, u32[]{:S(2)}, u32[]{:S(2)}) collective-permute-start(bf16[4,16,512]{2,1,0:T(8,128)(2,1)S(1)} %pad_maximum_fusion.slices_ref), channel_id=1, source_target_pairs={{0,1},{1,0},{2,3},{3,2},{4,5},{5,4},{6,7},{7,6},{8,9},{9,8},{10,11... | collective-permute-start | bytes 196616 | tf_op jit(solution)/shard_map/ppermute | solution.py:40
  25.4 4.7 %collective-permute-start.10 = (bf16[4,16,512]{2,1,0:T(8,128)(2,1)S(1)}, bf16[4,16,512]{2,1,0:T(8,128)(2,1)S(1)}, u32[]{:S(2)}, u32[]{:S(2)}) collective-permute-start(bf16[4,16,512]{2,1,0:T(8,128)(2,1)S(1)} %pad_maximum_fusion.slices_ref), channel_id=1, source_target_pairs={{0,2},{1,3},{2,0},{3,1},{4,6},{5,7},{6,4},{7,5},{8,10},{9,11},{10,... | collective-permute-start | bytes 196616 | tf_op jit(solution)/shard_map/ppermute | solution.py:40
  26.9 4.2 %collective-permute-start.9 = (bf16[4,16,512]{2,1,0:T(8,128)(2,1)S(1)}, bf16[4,16,512]{2,1,0:T(8,128)(2,1)S(1)}, u32[]{:S(2)}, u32[]{:S(2)}) collective-permute-start(bf16[4,16,512]{2,1,0:T(8,128)(2,1)S(1)} %pad_maximum_fusion.slices_ref), channel_id=1, source_target_pairs={{0,3},{1,2},{2,1},{3,0},{4,7},{5,6},{6,5},{7,4},{8,11},{9,10},{10,... | collective-permute-start | bytes 196616 | tf_op jit(solution)/shard_map/ppermute | solution.py:40

commit v3 on v2

--- a/solution.py
+++ b/solution.py
@@ -74,24 +74,34 @@
     return [s * inner + (s > 0 and inner > 1) for s in range(outer)]
 
 
+def gather_stages(size):
+    outer, inner = split(size)
+    if inner < 2:
+        return [[s * inner for s in range(1, outer)]]
+    near = [2 * a + 1 for a in range(1, inner // 2)]
+    far = [s * inner + 1 for s in range(1, outer)]
+    if len(far) == 3:
+        far = [far[0], far[2], far[1]]
+    return [stage for stage in (near, far, [1]) if stage]
+
+
 def pack_body(*refs):
-    out = refs[-1]
-    out[...] = jnp.concatenate([r[...].astype(jnp.float32) for r in refs[:-1]], axis=0).astype(out.dtype)
-
-
-def panel_body(me_ref, *refs, outer, inner):
-    parts, hess_ref, docs_ref = refs[:inner], refs[inner], refs[inner + 1]
-    out_ref, docs_out, sems = refs[inner + 2 :]
+    parts, out = refs[:-2], refs[-1]
+    out[...] = jnp.concatenate([r[...].astype(jnp.float32) for r in parts], axis=0).astype(out.dtype)
+
+
+def panel_body(me_ref, *refs, order):
+    parts, hess_ref, docs_ref, out_ref, docs_out, sems = refs[:-5], *refs[-5:]
     copies = start_copies(docs_ref, 0, docs_out, sems)
     vals = jnp.concatenate([r[...].astype(jnp.float32) for r in parts], axis=0).astype(jnp.bfloat16)
     count = vals.shape[0]
-    each = count // (outer * inner)
+    each = count // len(order)
     to = lax.broadcasted_iota(jnp.int32, (count, count), 0)
     at = lax.broadcasted_iota(jnp.int32, (count, count), 1)
-    block = at // each
-    s = block % outer
-    origin = me_ref[0] ^ (s * inner + jnp.where(s > 0, int(inner > 1), 0)) ^ (block // outer)
-    place = (to == origin * each + at % each).astype(jnp.float32).astype(jnp.bfloat16)
+    origin = jnp.zeros_like(at)
+    for i, mask in enumerate(order):
+        origin = jnp.where(at // each == i, mask, origin)
+    place = (to == (me_ref[0] ^ origin) * each + at % each).astype(jnp.float32).astype(jnp.bfloat16)
     out_ref[...] = dot(place, dot(hess_ref[...], vals).astype(jnp.bfloat16)).astype(out_ref.dtype)
     for copy in copies:
         copy.wait()
@@ -224,23 +234,31 @@
     count = size * val_local
     masks = far_masks(size)[1:]
 
-    far = [val_grads] + [send(val_grads, size, mask) for mask in masks]
-    far[0] = fetch(val_grads, far[1])
-    far = call(
-        pack_body, "pack", jax.ShapeDtypeStruct((outer * val_local, width), jnp.bfloat16), 0, 4 * outer * width
-    )(in_specs=[VMEM] * outer, out_specs=VMEM)(*far)
-    near = [far] + [send(far, size, t) for t in range(1, inner)]
-    near_hess = fetch(inv_hessian, far)
+    order, held = [0], fetch(val_grads, me)
+    outgoing, near_hess = val_grads, None
+    stages = gather_stages(size)
+    for stage in stages:
+        came = [send(outgoing, size, mask) for mask in stage]
+        order += [mask ^ o for mask in stage for o in order]
+        if stage is stages[-2]:
+            near_hess = fetch(inv_hessian, held)
+        if stage is not stages[-1]:
+            shape = ((len(came) + 1) * held.shape[0], width)
+            held = call(pack_body, "pack", jax.ShapeDtypeStruct(shape, held.dtype), 0, 4 * shape[0] * width)(
+                in_specs=[VMEM] * (len(came) + 1) + [pl.BlockSpec(memory_space=pl.ANY)], out_specs=VMEM
+            )(held, *came, me if near_hess is None else near_hess)
+            outgoing = held
+    near = [held] + came
     early = docs * 3 // 4
     panel, docs_low = call(
-        functools.partial(panel_body, outer=outer, inner=inner),
+        functools.partial(panel_body, order=order),
         "panel",
         (jax.ShapeDtypeStruct((count, rows), jnp.bfloat16), pltpu.VMEM((early, width), doc_grads.dtype)),
         2 * count * rows * width,
         2 * rows * width,
         16,
     )(
-        in_specs=[SMEM] + [VMEM] * (inner + 1) + [HBM],
+        in_specs=[SMEM] + [VMEM] * (len(near) + 1) + [HBM],
         out_specs=(VMEM, VMEM),
         scratch_shapes=[pltpu.SemaphoreType.DMA((1,))],
     )(me, *near, near_hess, far_memory(doc_grads))

time: 43.7 us -> 42.3 us (0.968)
  waiting for transfers between devices: 7.33 us -> 5.27 us
  starting transfers between devices: 12.9 us -> 13.9 us
    ppermute x12 -> x11, waiting for transfers between devices: 7.33 us -> 5.27 us  [send(): return lax.ppermute(x, 'blk', [(i, i ^ mask) for i in range(size)])]
    ppermute x12 -> x11, starting transfers between devices: 12.9 us -> 13.9 us  [send(): return lax.ppermute(x, 'blk', [(i, i ^ mask) for i in range(size)])]
    pallas_call x2 -> x3, Pallas kernels: 2.91 us -> 2.93 us  [the longest x1 2.79 us: per_device(): call(functools.partial(panel_body, order=order), 'panel', (jax.ShapeDtype...]
  transfers between devices with their start and end apart: 12 -> 11, of which waited for: 6 -> 6; matrix products, arithmetic and copies ran while one was open for 0% -> 0% of each run, Pallas kernels for 18% -> 19%
where the time goes in v3:
time: 42.3 us; the launch traced here: 42 us
  starting transfers between devices  13.9 us (33%)
  Pallas kernels  12.4 us (29%)
  blocking collectives  10.2 us (24%)
  waiting for transfers between devices  5.27 us (12%)
    ppermute x11, starting transfers between devices, send(): return lax.ppermute(x, 'blk', [(i, i ^ mask) for i in range(size)])  13.9 us
    all_to_all x1, blocking collectives, per_device(): lax.all_to_all(sums.reshape(size, kept * count), 'blk', 0, 0, tiled=True)  10.2 us
    ppermute x11, waiting for transfers between devices, send(): return lax.ppermute(x, 'blk', [(i, i ^ mask) for i in range(size)])  5.27 us
    pallas_call x2, Pallas kernels, fetch(): return near_memory(run(far_memory(x), after))  4.19 us
    pallas_call x1, Pallas kernels, per_device(): call(functools.partial(panel_body, order=order), 'panel', (jax.ShapeDtype...  2.79 us
    pallas_call x1, Pallas kernels, tiled_sums(): call(functools.partial(first_body, inner=inner), 'scores_0', (jax.ShapeDt...  2.36 us
    pallas_call x2, Pallas kernels, tiled_sums(): call(functools.partial(next_body, step=t, inner=inner), f'scores_{t}', ja...  1.26 us
    pallas_call x1, Pallas kernels, tiled_sums(): call(functools.partial(last_body, step=inner - 1, inner=inner), 'sums', j...  0.94 us
  transfers between devices with their start and end apart: 11, of which 6 were waited for; matrix products, arithmetic and copies ran while one was open for 0% of the time, Pallas kernels for 19%

profile of v3, /device:TPU:0, one launch (start us, length us, event | category | flops | bytes accessed | tf_op | source)
XLA Modules:
  0.0 42.0 jit_solution(12003902629085858643)
XLA Ops:
  0.0 2.4 %collective-permute-start = (bf16[1,8192]{1,0:T(2,128)(2,1)}, bf16[1,8192]{1,0:T(2,128)(2,1)S(1)}, u32[]{:S(2)}, u32[]{:S(2)}) collective-permute-start(bf16[1,8192]{1,0:T(2,128)(2,1)} %x_ref.2), channel_id=1, source_target_pairs={{0,3},{1,2},{2,1},{3,0},{4,7},{5,6},{6,5},{7,4},{8,11},{9,10},{10,... | collective-permute-start | bytes 49160 | tf_op jit(solution)/shard_map/ppermute | solution.py:40
  2.4 0.8 %fetch.2.refs_0_ = bf16[1,8192]{1,0:T(2,128)(2,1)S(1)} custom-call(bf16[1,8192]{1,0:T(2,128)(2,1)} %x_ref.2, s32[1]{0:T(128)} %bitcast._.refs_2_.me_ref), custom_call_target="tpu_custom_call" | custom-call | bytes 32768 | tf_op jit(solution)/shard_map/fetch/pallas_call | solution.py:62
  3.2 1.3 %collective-permute-done.refs_1_ = bf16[1,8192]{1,0:T(2,128)(2,1)S(1)} collective-permute-done((bf16[1,8192]{1,0:T(2,128)(2,1)}, bf16[1,8192]{1,0:T(2,128)(2,1)S(1)}, u32[]{:S(2)}, u32[]{:S(2)}) %collective-permute-start) | collective-permute-done | bytes 16416 | tf_op jit(solution)/shard_map/ppermute | solution.py:40
  4.5 3.2 %collective-permute-start.3 = (bf16[2,8192]{1,0:T(2,128)(2,1)S(1)}, bf16[2,8192]{1,0:T(2,128)(2,1)S(1)}, u32[]{:S(2)}, u32[]{:S(2)}) collective-permute-start(bf16[2,8192]{1,0:T(2,128)(2,1)S(1)} %pack.2._.refs_0_), channel_id=1, source_target_pairs={{0,9},{1,8},{2,11},{3,10},{4,13},{5,12},{6,15},{7,14},{8,1},{9,0},... | collective-permute-start | bytes 98312 | tf_op jit(solution)/shard_map/ppermute | solution.py:40
  7.7 1.3 %collective-permute-start.2 = (bf16[2,8192]{1,0:T(2,128)(2,1)S(1)}, bf16[2,8192]{1,0:T(2,128)(2,1)S(1)}, u32[]{:S(2)}, u32[]{:S(2)}) collective-permute-start(bf16[2,8192]{1,0:T(2,128)(2,1)S(1)} %pack.2._.refs_0_), channel_id=1, source_target_pairs={{0,13},{1,12},{2,15},{3,14},{4,9},{5,8},{6,11},{7,10},{8,5},{9,4},... | collective-permute-start | bytes 98312 | tf_op jit(solution)/shard_map/ppermute | solution.py:40
  9.1 0.3 collective-permute-start.1
  9.3 3.4 %fetch.3.refs_4_.refs_2_ = bf16[512,8192]{1,0:T(8,128)(2,1)S(1)} custom-call(bf16[512,8192]{1,0:T(8,128)(2,1)} %x_ref.3, bf16[2,8192]{1,0:T(2,128)(2,1)S(1)} %pack.2._.refs_0_), custom_call_target="tpu_custom_call" | custom-call | bytes 16777216 | tf_op jit(solution)/shard_map/fetch/pallas_call | solution.py:62
  12.7 0.0 collective-permute-done.3.refs_3_
  12.8 0.3 collective-permute-done.2.refs_2_
  13.0 0.0 collective-permute-done.1.refs_1_
  13.0 0.1 pack.3.refs_0_
  13.1 0.0 copy-start
  13.1 0.0 copy-start.1
  13.1 0.0 copy-start.2
  13.1 0.6 %collective-permute-start.4 = (bf16[8,8192]{1,0:T(8,128)(2,1)S(1)}, bf16[8,8192]{1,0:T(8,128)(2,1)S(1)}, u32[]{:S(2)}, u32[]{:S(2)}) collective-permute-start(bf16[8,8192]{1,0:T(8,128)(2,1)S(1)} %pack.3.refs_0_), channel_id=1, source_target_pairs={{0,1},{1,0},{2,3},{3,2},{4,5},{5,4},{6,7},{7,6},{8,9},{9,8},{10,11... | collective-permute-start | bytes 393224 | tf_op jit(solution)/shard_map/ppermute | solution.py:40
  13.7 1.0 %collective-permute-done.4.refs_1_ = bf16[8,8192]{1,0:T(8,128)(2,1)S(1)} collective-permute-done((bf16[8,8192]{1,0:T(8,128)(2,1)S(1)}, bf16[8,8192]{1,0:T(8,128)(2,1)S(1)}, u32[]{:S(2)}, u32[]{:S(2)}) %collective-permute-start.4) | collective-permute-done | bytes 131104 | tf_op jit(solution)/shard_map/ppermute | solution.py:40
  14.7 2.8 %panel.1 = (bf16[16,512]{1,0:T(8,128)(2,1)S(1)}, bf16[384,8192]{1,0:T(8,128)(2,1)S(1)}) custom-call(s32[1]{0:T(128)} %bitcast._.refs_2_.me_ref, bf16[8,8192]{1,0:T(8,128)(2,1)S(1)} %pack.3.refs_0_, bf16[8,8192]{1,0:T(8,128)(2,1)S(1)} %collective-permute-done.4.refs_1_, bf16[512,8192]{1,0:T(8,128)(2,1)S(1)} %fetch.3.refs_4_.refs_2_, bf16[512,8192]{1,0:T(8,128)(2,1)} %docs_ref.1), custom_call_target="tpu_custom_call" | custom-call | flops 134217728 | bytes 8388608 | tf_op jit(solution)/shard_map/panel/pallas_call | solution.py:253
  17.5 2.3 %collective-permute-start.7 = (bf16[16,512]{1,0:T(8,128)(2,1)S(1)}, bf16[16,512]{1,0:T(8,128)(2,1)S(1)}, u32[]{:S(2)}, u32[]{:S(2)}) collective-permute-start(bf16[16,512]{1,0:T(8,128)(2,1)S(1)} %get-tuple-element.12), channel_id=1, source_target_pairs={{0,13},{1,12},{2,15},{3,14},{4,9},{5,8},{6,11},{7,10},{8,5},{9,4},... | collective-permute-start | bytes 49160 | tf_op jit(solution)/shard_map/ppermute | solution.py:40
  19.8 0.1 collective-permute-start.6
  19.9 1.8 %collective-permute-start.5 = (bf16[16,512]{1,0:T(8,128)(2,1)S(1)}, bf16[16,512]{1,0:T(8,128)(2,1)S(1)}, u32[]{:S(2)}, u32[]{:S(2)}) collective-permute-start(bf16[16,512]{1,0:T(8,128)(2,1)S(1)} %get-tuple-element.12), channel_id=1, source_target_pairs={{0,5},{1,4},{2,7},{3,6},{4,1},{5,0},{6,3},{7,2},{8,13},{9,12},{10,... | collective-permute-start | bytes 49160 | tf_op jit(solution)/shard_map/ppermute | solution.py:40
  21.7 0.9 %collective-permute-done.7 = bf16[16,512]{1,0:T(8,128)(2,1)S(1)} collective-permute-done((bf16[16,512]{1,0:T(8,128)(2,1)S(1)}, bf16[16,512]{1,0:T(8,128)(2,1)S(1)}, u32[]{:S(2)}, u32[]{:S(2)}) %collective-permute-start.7) | collective-permute-done | bytes 16416 | tf_op jit(solution)/shard_map/ppermute | solution.py:40
  22.6 1.6 %collective-permute-done.6 = bf16[16,512]{1,0:T(8,128)(2,1)S(1)} collective-permute-done((bf16[16,512]{1,0:T(8,128)(2,1)S(1)}, bf16[16,512]{1,0:T(8,128)(2,1)S(1)}, u32[]{:S(2)}, u32[]{:S(2)}) %collective-permute-start.6) | collective-permute-done | bytes 16416 | tf_op jit(solution)/shard_map/ppermute | solution.py:40
  24.1 0.0 collective-permute-done.5
  24.1 0.2 collective-permute-start.10
  24.3 1.6 %collective-permute-start.9 = (bf16[4,16,512]{2,1,0:T(8,128)(2,1)S(1)}, bf16[4,16,512]{2,1,0:T(8,128)(2,1)S(1)}, u32[]{:S(2)}, u32[]{:S(2)}) collective-permute-start(bf16[4,16,512]{2,1,0:T(8,128)(2,1)S(1)} %pad_maximum_fusion.slices_ref), channel_id=1, source_target_pairs={{0,2},{1,3},{2,0},{3,1},{4,6},{5,7},{6,4},{7,5},{8,10},{9,11},{10,... | collective-permute-start | bytes 196616 | tf_op jit(solution)/shard_map/ppermute | solution.py:40
  25.9 0.2 collective-permute-start.8
  26.1 0.0 copy-done
  26.1 0.0 copy-done.1
  26.1 0.0 copy-done.2
  26.1 2.4 %scores_0.1 = (f32[16,512]{1,0:T(8,128)S(1)}, bf16[128,512]{1,0:T(8,128)(2,1)S(1)}, f32[16,512]{1,0:T(8,128)S(1)}, bf16[128,8192]{1,0:T(8,128)(2,1)S(1)}) custom-call(s32[1]{0:T(128)} %bitcast._.refs_2_.me_ref, bf16[384,8192]{1,0:T(8,128)(2,1)S(1)} %get-tuple-element.11.low_ref, bf16[512,8192]{1,0:T(8,128)(2,1)} %docs_ref.1, ...), custom_call_target="tpu_custom_call" | custom-call | flops 33554432 | bytes 2097152 | tf_op jit(solution)/shard_map/scores_0/pallas_call | solution.py:187
  28.4 0.0 collective-permute-done.10.slices_ref
  28.5 0.6 %scores_1.1.sum_ref = f32[16,512]{1,0:T(8,128)S(1)} custom-call(s32[1]{0:T(128)} %bitcast._.refs_2_.me_ref, bf16[384,8192]{1,0:T(8,128)(2,1)S(1)} %get-tuple-element.11.low_ref, bf16[128,8192]{1,0:T(8,128)(2,1)S(1)} %get-tuple-element.13.high_ref, bf16[4,16,512]{2,1,0:T(8,128)(2,1)S(1)} %collective-permute-done.10.slices_ref, ...), custom_call_target="tpu_custom_call" | custom-call | flops 33554432 | bytes 2097152 | tf_op jit(solution)/shard_map/scores_1/pallas_call | solution.py:212
  29.1 0.0 collective-permute-done.9.slices_ref
  29.1 0.6 %scores_2.1.sum_ref = f32[16,512]{1,0:T(8,128)S(1)} custom-call(s32[1]{0:T(128)} %bitcast._.refs_2_.me_ref, bf16[384,8192]{1,0:T(8,128)(2,1)S(1)} %get-tuple-element.11.low_ref, bf16[128,8192]{1,0:T(8,128)(2,1)S(1)} %get-tuple-element.13.high_ref, bf16[4,16,512]{2,1,0:T(8,128)(2,1)S(1)} %collective-permute-done.9.slices_ref, f32[16,512]{1,0:T(8,128)S(1)} %scores_1.1.sum_ref), custom_call_target="tpu_custom_call" | custom-call | flops 33554432 | bytes 2097152 | tf_op jit(solution)/shard_map/scores_2/pallas_call | solution.py:212
  29.7 0.3 collective-permute-done.8.slices_ref
  30.0 0.9 %sums.1 = f32[128,16]{1,0:T(8,128)S(1)} custom-call(s32[1]{0:T(128)} %bitcast._.refs_2_.me_ref, bf16[384,8192]{1,0:T(8,128)(2,1)S(1)} %get-tuple-element.11.low_ref, bf16[128,8192]{1,0:T(8,128)(2,1)S(1)} %get-tuple-element.13.high_ref, bf16[4,16,512]{2,1,0:T(8,128)(2,1)S(1)} %collective-permute-done.8.slices_ref, f32[16,512]{1,0:T(8,128)S(1)} %scores_2.1.sum_ref, ...), custom_call_target="tpu_custom_call" | custom-call | flops 33554432 | bytes 2097152 | tf_op jit(solution)/shard_map/sums/pallas_call | solution.py:218
  31.0 0.1 all_to_all.7
  31.0 10.2 %all_to_all.11 = f32[16,1,128]{2,1,0:T(1,128)S(1)} all-to-all(f32[16,1,128]{2,1,0:T(1,128)S(1)} %bitcast.13), channel_id=1, replica_groups=mesh['grp'=2,'blk'=16] {'blk'}, dimensions={0} | all-to-all | bytes 16384 | tf_op jit(solution)/shard_map/all_to_all | solution.py:273
  41.3 0.7 %total.1 = f32[8,16]{1,0:T(8,128)} custom-call(f32[16,128]{1,0:T(8,128)S(1)} %bitcast.9), custom_call_target="tpu_custom_call" | custom-call | bytes 16384 | tf_op jit(solution)/shard_map/total/pallas_call | solution.py:274
  (2 shorter events, 0.1 us)
Async XLA Ops:
  0.0 4.5 %collective-permute-start = (bf16[1,8192]{1,0:T(2,128)(2,1)}, bf16[1,8192]{1,0:T(2,128)(2,1)S(1)}, u32[]{:S(2)}, u32[]{:S(2)}) collective-permute-start(bf16[1,8192]{1,0:T(2,128)(2,1)} %x_ref.2), channel_id=1, source_target_pairs={{0,3},{1,2},{2,1},{3,0},{4,7},{5,6},{6,5},{7,4},{8,11},{9,10},{10,... | collective-permute-start | bytes 49160 | tf_op jit(solution)/shard_map/ppermute | solution.py:40
  4.5 8.2 %collective-permute-start.3 = (bf16[2,8192]{1,0:T(2,128)(2,1)S(1)}, bf16[2,8192]{1,0:T(2,128)(2,1)S(1)}, u32[]{:S(2)}, u32[]{:S(2)}) collective-permute-start(bf16[2,8192]{1,0:T(2,128)(2,1)S(1)} %pack.2._.refs_0_), channel_id=1, source_target_pairs={{0,9},{1,8},{2,11},{3,10},{4,13},{5,12},{6,15},{7,14},{8,1},{9,0},... | collective-permute-start | bytes 98312 | tf_op jit(solution)/shard_map/ppermute | solution.py:40
  7.7 5.3 %collective-permute-start.2 = (bf16[2,8192]{1,0:T(2,128)(2,1)S(1)}, bf16[2,8192]{1,0:T(2,128)(2,1)S(1)}, u32[]{:S(2)}, u32[]{:S(2)}) collective-permute-start(bf16[2,8192]{1,0:T(2,128)(2,1)S(1)} %pack.2._.refs_0_), channel_id=1, source_target_pairs={{0,13},{1,12},{2,15},{3,14},{4,9},{5,8},{6,11},{7,10},{8,5},{9,4},... | collective-permute-start | bytes 98312 | tf_op jit(solution)/shard_map/ppermute | solution.py:40
  9.1 3.9 %collective-permute-start.1 = (bf16[2,8192]{1,0:T(2,128)(2,1)S(1)}, bf16[2,8192]{1,0:T(2,128)(2,1)S(1)}, u32[]{:S(2)}, u32[]{:S(2)}) collective-permute-start(bf16[2,8192]{1,0:T(2,128)(2,1)S(1)} %pack.2._.refs_0_), channel_id=1, source_target_pairs={{0,5},{1,4},{2,7},{3,6},{4,1},{5,0},{6,3},{7,2},{8,13},{9,12},{10,... | collective-permute-start | bytes 98312 | tf_op jit(solution)/shard_map/ppermute | solution.py:40
  13.1 13.0 %copy-start = (s32[4,16]{1,0:T(4,128)S(1)}, s32[4,16]{1,0:T(4,128)}, u32[]{:S(2)}) copy-start(s32[4,16]{1,0:T(4,128)} %mask_ref.1) | copy-start | bytes 772
  13.1 13.0 %copy-start.1 = (s32[512]{0:T(512)S(1)}, s32[512]{0:T(512)}, u32[]{:S(2)}) copy-start(s32[512]{0:T(512)} %param.10) | copy-start | bytes 6148
  13.1 13.0 %copy-start.2 = (s32[128]{0:T(128)S(1)}, s32[128]{0:T(128)}, u32[]{:S(2)}) copy-start(s32[128]{0:T(128)} %param.11) | copy-start | bytes 1540
  13.1 1.6 %collective-permute-start.4 = (bf16[8,8192]{1,0:T(8,128)(2,1)S(1)}, bf16[8,8192]{1,0:T(8,128)(2,1)S(1)}, u32[]{:S(2)}, u32[]{:S(2)}) collective-permute-start(bf16[8,8192]{1,0:T(8,128)(2,1)S(1)} %pack.3.refs_0_), channel_id=1, source_target_pairs={{0,1},{1,0},{2,3},{3,2},{4,5},{5,4},{6,7},{7,6},{8,9},{9,8},{10,11... | collective-permute-start | bytes 393224 | tf_op jit(solution)/shard_map/ppermute | solution.py:40
  17.5 5.0 %collective-permute-start.7 = (bf16[16,512]{1,0:T(8,128)(2,1)S(1)}, bf16[16,512]{1,0:T(8,128)(2,1)S(1)}, u32[]{:S(2)}, u32[]{:S(2)}) collective-permute-start(bf16[16,512]{1,0:T(8,128)(2,1)S(1)} %get-tuple-element.12), channel_id=1, source_target_pairs={{0,13},{1,12},{2,15},{3,14},{4,9},{5,8},{6,11},{7,10},{8,5},{9,4},... | collective-permute-start | bytes 49160 | tf_op jit(solution)/shard_map/ppermute | solution.py:40
  19.8 4.3 %collective-permute-start.6 = (bf16[16,512]{1,0:T(8,128)(2,1)S(1)}, bf16[16,512]{1,0:T(8,128)(2,1)S(1)}, u32[]{:S(2)}, u32[]{:S(2)}) collective-permute-start(bf16[16,512]{1,0:T(8,128)(2,1)S(1)} %get-tuple-element.12), channel_id=1, source_target_pairs={{0,9},{1,8},{2,11},{3,10},{4,13},{5,12},{6,15},{7,14},{8,1},{9,0},... | collective-permute-start | bytes 49160 | tf_op jit(solution)/shard_map/ppermute | solution.py:40
  19.9 4.2 %collective-permute-start.5 = (bf16[16,512]{1,0:T(8,128)(2,1)S(1)}, bf16[16,512]{1,0:T(8,128)(2,1)S(1)}, u32[]{:S(2)}, u32[]{:S(2)}) collective-permute-start(bf16[16,512]{1,0:T(8,128)(2,1)S(1)} %get-tuple-element.12), channel_id=1, source_target_pairs={{0,5},{1,4},{2,7},{3,6},{4,1},{5,0},{6,3},{7,2},{8,13},{9,12},{10,... | collective-permute-start | bytes 49160 | tf_op jit(solution)/shard_map/ppermute | solution.py:40
  24.1 4.3 %collective-permute-start.10 = (bf16[4,16,512]{2,1,0:T(8,128)(2,1)S(1)}, bf16[4,16,512]{2,1,0:T(8,128)(2,1)S(1)}, u32[]{:S(2)}, u32[]{:S(2)}) collective-permute-start(bf16[4,16,512]{2,1,0:T(8,128)(2,1)S(1)} %pad_maximum_fusion.slices_ref), channel_id=1, source_target_pairs={{0,1},{1,0},{2,3},{3,2},{4,5},{5,4},{6,7},{7,6},{8,9},{9,8},{10,11... | collective-permute-start | bytes 196616 | tf_op jit(solution)/shard_map/ppermute | solution.py:40
  24.3 4.8 %collective-permute-start.9 = (bf16[4,16,512]{2,1,0:T(8,128)(2,1)S(1)}, bf16[4,16,512]{2,1,0:T(8,128)(2,1)S(1)}, u32[]{:S(2)}, u32[]{:S(2)}) collective-permute-start(bf16[4,16,512]{2,1,0:T(8,128)(2,1)S(1)} %pad_maximum_fusion.slices_ref), channel_id=1, source_target_pairs={{0,2},{1,3},{2,0},{3,1},{4,6},{5,7},{6,4},{7,5},{8,10},{9,11},{10,... | collective-permute-start | bytes 196616 | tf_op jit(solution)/shard_map/ppermute | solution.py:40
  25.9 4.1 %collective-permute-start.8 = (bf16[4,16,512]{2,1,0:T(8,128)(2,1)S(1)}, bf16[4,16,512]{2,1,0:T(8,128)(2,1)S(1)}, u32[]{:S(2)}, u32[]{:S(2)}) collective-permute-start(bf16[4,16,512]{2,1,0:T(8,128)(2,1)S(1)} %pad_maximum_fusion.slices_ref), channel_id=1, source_target_pairs={{0,3},{1,2},{2,1},{3,0},{4,7},{5,6},{6,5},{7,4},{8,11},{9,10},{10,... | collective-permute-start | bytes 196616 | tf_op jit(solution)/shard_map/ppermute | solution.py:40

commit v4 on v3

v4 whole, which is shorter than its diff:
```python
import functools
import math

import jax
import jax.numpy as jnp
from jax import lax
from jax.experimental import pallas as pl
from jax.experimental.pallas import tpu as pltpu
from jax.sharding import PartitionSpec as P

ROWS_BY_ROWS = (((1,), (1,)), ((), ()))
VMEM = pl.BlockSpec(memory_space=pltpu.VMEM)
HBM = pl.BlockSpec(memory_space=pltpu.HBM)
SMEM = pl.BlockSpec(memory_space=pltpu.SMEM)


def dot(a, b, dims=ROWS_BY_ROWS):
    return lax.dot_general(a, b, dims, preferred_element_type=jnp.float32)


def near_memory(x):
    return pltpu.with_memory_space_constraint(x, pltpu.VMEM)


def far_memory(x):
    return pltpu.with_memory_space_constraint(x, pltpu.HBM)


def call(body, name, out_shape, flops, moved, limit=12):
    return functools.partial(
        pl.pallas_call,
        body,
        out_shape=out_shape,
        compiler_params=pltpu.CompilerParams(vmem_limit_bytes=limit << 20),
        cost_estimate=pl.CostEstimate(flops=flops, bytes_accessed=moved, transcendentals=0),
        name=name,
    )


def send(x, size, mask):
    return lax.ppermute(x, "blk", [(i, i ^ mask) for i in range(size)])


def start_copies(ref, start, out, sems):
    pieces = sems.shape[0]
    rows = out.shape[0] // pieces
    copies = []
    for i in range(pieces):
        here, there = ref, out
        if ref.shape[0] != rows:
            here, there = ref.at[pl.ds(start + i * rows, rows)], out.at[pl.ds(i * rows, rows)]
        copies.append(pltpu.make_async_copy(here, there, sems.at[i]))
        copies[-1].start()
    return copies


def fetch(x, after, first=0, count=None, into=None):
    count = x.shape[0] - first if count is None else count

    def body(x_ref, *refs):
        out_ref, sems = refs[-2:]
        part = out_ref if count == out_ref.shape[0] else out_ref.at[pl.ds(first, count)]
        for copy in start_copies(x_ref, first, part, sems):
            copy.wait()

    run = call(body, "fetch", pltpu.VMEM(x.shape, x.dtype), 0, 2 * count * x.shape[1] * x.dtype.itemsize, 1)(
        in_specs=[HBM, pl.BlockSpec(memory_space=pl.ANY)] + [VMEM] * (into is not None),
        out_specs=VMEM,
        scratch_shapes=[pltpu.SemaphoreType.DMA((1,))],
        input_output_aliases={} if into is None else {2: 0},
    )
    return near_memory(run(far_memory(x), after, *([] if into is None else [into])))


def split(size):
    inner = 1
    while inner * inner * 4 <= size:
        inner *= 2
    return size // inner, inner


def stack_body(*refs):
    parts, out = refs[:-2], refs[-1]
    for i, part in enumerate(parts):
        n = part.shape[0]
        out[i * n : (i + 1) * n] = part[...]


def gather_stages(size):
    outer, inner = split(size)
    if inner < 2:
        return [[s * inner for s in range(1, outer)]]
    near = [2 * a + 1 for a in range(1, inner // 2)]
    far = [s * inner + 1 for s in range(1, outer)]
    if len(far) == 3:
        far = [far[0], far[2], far[1]]
    return [stage for stage in (near, far, [1]) if stage]


def pack_body(*refs):
    parts, out = refs[:-2], refs[-1]
    out[...] = jnp.concatenate([r[...].astype(jnp.float32) for r in parts], axis=0).astype(out.dtype)


def panel_body(me_ref, *refs, order):
    parts, hess_ref, docs_ref, out_ref, docs_out, sems = refs[:-5], *refs[-5:]
    copies = start_copies(docs_ref, 0, docs_out, sems)
    vals = jnp.concatenate([r[...].astype(jnp.float32) for r in parts], axis=0).astype(jnp.bfloat16)
    count = vals.shape[0]
    each = count // len(order)
    to = lax.broadcasted_iota(jnp.int32, (count, count), 0)
    at = lax.broadcasted_iota(jnp.int32, (count, count), 1)
    origin = jnp.zeros_like(at)
    for i, mask in enumerate(order):
        origin = jnp.where(at // each == i, mask, origin)
    place = (to == (me_ref[0] ^ origin) * each + at % each).astype(jnp.float32).astype(jnp.bfloat16)
    out_ref[...] = dot(place, dot(hess_ref[...], vals).astype(jnp.bfloat16)).astype(out_ref.dtype)
    for copy in copies:
        copy.wait()


def scores_of(me, docs_ref, parts):
    total = None
    for slices_ref, masks in parts:
        rows = slices_ref.shape[-1]
        for s, mask in enumerate(masks):
            column = pl.multiple_of((me ^ mask) * rows, rows)
            part = dot(slices_ref[s], docs_ref[:, pl.ds(column, rows)])
            total = part if total is None else total + part
    return total


def add_scores(me, docs_refs, parts):
    return jnp.concatenate([scores_of(me, r, parts) for r in docs_refs], axis=1)


def first_body(me_ref, low_ref, docs_ref, mask_ref, member_ref, slot_ref, *refs, masks, size):
    parts = list(zip(refs[: len(masks)], masks))
    out_ref, hot_ref, wide_ref, high_ref, sems = refs[len(masks) :]
    split_at = low_ref.shape[0]
    copies = start_copies(docs_ref, split_at, high_ref, sems)
    out_ref[:, :split_at] = scores_of(me_ref[0], low_ref, parts)
    clusters, docs = hot_ref.shape
    row = lax.broadcasted_iota(jnp.int32, (clusters, clusters), 0)
    kept = clusters // size
    slot = (size - 1 - row // kept) * kept + row % kept
    by_slot = (slot == slot_ref[...]).astype(jnp.float32).astype(jnp.bfloat16)
    cluster = lax.broadcasted_iota(jnp.int32, (clusters, docs), 0)
    by_doc = (cluster == member_ref[...]).astype(jnp.float32).astype(jnp.bfloat16)
    hot_ref[...] = dot(by_slot, by_doc, (((1,), (0,)), ((), ()))).astype(jnp.bfloat16)
    blocks = mask_ref.shape[0]
    doc = lax.broadcasted_iota(jnp.int32, (blocks, docs), 1)
    spread = (doc // (docs // blocks) == lax.broadcasted_iota(jnp.int32, (blocks, docs), 0)).astype(jnp.float32)
    narrow = mask_ref[...].astype(jnp.float32)
    wide_ref[...] = dot(narrow.astype(jnp.bfloat16), spread.astype(jnp.bfloat16), (((0,), (0,)), ((), ())))
    for copy in copies:
        copy.wait()
    out_ref[:, split_at:] = scores_of(me_ref[0], high_ref, parts)


def next_body(me_ref, low_ref, high_ref, sum_ref, *refs, masks):
    parts = list(zip(refs, masks))
    refs[-1][...] = sum_ref[...] + add_scores(me_ref[0], (low_ref, high_ref), parts)


def last_body(me_ref, low_ref, high_ref, sum_ref, hot_ref, wide_ref, *refs, masks):
    parts, out_ref = list(zip(refs, masks)), refs[-1]
    scores = sum_ref[...] + add_scores(me_ref[0], (low_ref, high_ref), parts)
    masked = 0.125 * (scores * wide_ref[...])
    high = masked.astype(jnp.bfloat16)
    low = (masked - high.astype(jnp.float32)).astype(jnp.bfloat16)
    out_ref[...] = dot(hot_ref[...], high) + dot(hot_ref[...], low)


def total_body(parts_ref, out_ref):
    kept, count = out_ref.shape
    total = jnp.sum(parts_ref[...], axis=0, keepdims=True)
    out_ref[...] = jnp.concatenate([total[:, r * count : (r + 1) * count] for r in range(kept)], axis=0)


def wide_sums(me, own, came, docs_in, topic_mask, membership, owner_slot, *, size):
    docs, width = docs_in.shape
    clusters = owner_slot.shape[0]
    arrays, masks = zip(own, *came)
    held, masks = jnp.concatenate(arrays), sum(masks, [])
    slices = jnp.concatenate([held, send(held, size, 1)])
    origins = me ^ jnp.array(masks + [mask ^ 1 for mask in masks])
    precond = jnp.moveaxis(slices[jnp.argsort(origins)], 0, 1).reshape(-1, width)
    blocks = topic_mask.shape[0]
    mask = jnp.repeat(topic_mask.T.astype(jnp.float32), docs // blocks, axis=1)
    mask = jnp.repeat(mask, precond.shape[0] // mask.shape[0], axis=0)
    masked = 0.125 * (dot(precond, docs_in) * mask)
    slot = jnp.arange(clusters).reshape(size, -1)[::-1].reshape(-1)
    by_slot = (slot[:, None] == owner_slot[None, :]).astype(jnp.bfloat16)
    by_doc = (jnp.arange(clusters)[:, None] == membership[None, :]).astype(jnp.bfloat16)
    hot = jnp.dot(by_slot, by_doc, preferred_element_type=jnp.float32).astype(jnp.bfloat16)
    return dot(hot, masked.astype(jnp.bfloat16))


def tiled_sums(me, own, came, docs_low, doc_grads, topic_mask, membership, owner_slot, *, size):
    docs, width = doc_grads.shape
    clusters = owner_slot.shape[0]
    count = own[0].shape[1]

    def run(body, name, out_shape, step, operands, in_specs, **more):
        arrays, masks = zip(*step)
        share = sum(len(m) for m in masks) * docs * width // size
        out_specs = (VMEM,) * len(out_shape) if isinstance(out_shape, tuple) else VMEM
        return call(functools.partial(body, masks=masks), name, out_shape, 2 * count * share, 2 * share)(
            in_specs=in_specs + [VMEM] * len(arrays), out_specs=out_specs, **more
        )(*operands, *arrays)

    total = jax.ShapeDtypeStruct((count, docs), jnp.float32)
    sums, hot, wide, docs_high = run(
        functools.partial(first_body, size=size),
        "scores_first",
        (
            total,
            jax.ShapeDtypeStruct((clusters, docs), jnp.bfloat16),
            total,
            pltpu.VMEM((docs - docs_low.shape[0], width), doc_grads.dtype),
        ),
        [own],
        (me, docs_low, far_memory(doc_grads), topic_mask, membership.reshape(1, docs), owner_slot.reshape(1, clusters)),
        [SMEM, VMEM, HBM] + [VMEM] * 3,
        scratch_shapes=[pltpu.SemaphoreType.DMA((1,))],
    )
    both = (docs_low, near_memory(docs_high))
    arrays, masks = zip(own, *came)
    shape = (sum(a.shape[0] for a in arrays),) + arrays[0].shape[1:]
    held = call(stack_body, "stack", jax.ShapeDtypeStruct(shape, arrays[0].dtype), 0, 4 * math.prod(shape))(
        in_specs=[VMEM] * len(arrays) + [pl.BlockSpec(memory_space=pl.ANY)], out_specs=VMEM
    )(*arrays, sums)
    other = (send(held, size, 1), [mask ^ 1 for mask in sum(masks, [])])
    sums = run(next_body, "scores_next", total, came, (me, *both, sums), [SMEM] + [VMEM] * 3)
    shape = jax.ShapeDtypeStruct((clusters, count), jnp.float32)
    return run(last_body, "sums", shape, [other], (me, *both, sums, hot, wide), [SMEM] + [VMEM] * 5)


def per_device(doc_grads, val_grads, inv_hessian, topic_mask, membership, owner_slot, *, size):
    outer, inner = split(size)
    me = lax.axis_index("blk").astype(jnp.int32).reshape(1)
    docs = doc_grads.shape[0]
    val_local, width = val_grads.shape
    rows = inv_hessian.shape[0]
    clusters = owner_slot.shape[0]
    kept = clusters // size
    count = size * val_local
    order, held = [0], fetch(val_grads, me)
    outgoing, near_hess = val_grads, None
    stages = gather_stages(size)
    for k, stage in enumerate(stages):
        came = [send(outgoing, size, mask) for mask in stage]
        order += [mask ^ o for mask in stage for o in order]
        if k < 2:
            near_hess = fetch(inv_hessian, held, k * (rows // 2), rows // 2, into=near_hess)
        if stage is not stages[-1]:
            shape = ((len(came) + 1) * held.shape[0], width)
            held = call(pack_body, "pack", jax.ShapeDtypeStruct(shape, held.dtype), 0, 4 * shape[0] * width)(
                in_specs=[VMEM] * (len(came) + 1) + [pl.BlockSpec(memory_space=pl.ANY)], out_specs=VMEM
            )(held, *came, me if near_hess is None else near_hess)
            outgoing = held
    near = [held] + came
    early = docs * 5 // 8
    panel, docs_low = call(
        functools.partial(panel_body, order=order),
        "panel",
        (jax.ShapeDtypeStruct((count, rows), jnp.bfloat16), pltpu.VMEM((early, width), doc_grads.dtype)),
        2 * count * rows * width,
        2 * rows * width,
        16,
    )(
        in_specs=[SMEM] + [VMEM] * (len(near) + 1) + [HBM],
        out_specs=(VMEM, VMEM),
        scratch_shapes=[pltpu.SemaphoreType.DMA((1,))],
    )(me, *near, near_hess, far_memory(doc_grads))

    near, far, _ = stages
    own = jnp.stack([panel] + [send(panel, size, mask) for mask in near])
    own_masks = [0] + near
    came = [(send(own, size, mask), [mask ^ m for m in own_masks]) for mask in far]

    find = tiled_sums if rows % 128 == 0 else wide_sums
    given = (near_memory(docs_low), doc_grads) if rows % 128 == 0 else (doc_grads,)
    sums = find(me, (own, own_masks), came, *given, topic_mask, membership, owner_slot, size=size)

    backwards = list(range(size - 1, -1, -1))
    sums = lax.all_to_all(sums.reshape(size, kept * count), "blk", 0, 0, tiled=True, axis_index_groups=[backwards])
    return call(total_body, "total", jax.ShapeDtypeStruct((kept, count), jnp.float32), 0, 8 * size * kept * count)(
        in_specs=[VMEM], out_specs=VMEM
    )(sums)


def solution(mesh):
    size = mesh.shape["blk"]

    def run(*args):
        return per_device(*args, size=size)

    in_specs = (
        P(("grp", "blk"), None),
        P("blk", None),
        P("blk", None),
        P(("grp", "blk"), None),
        P(("grp", "blk")),
        P(),
    )
    out_specs = P(("grp", "blk"), None)
    return jax.shard_map(run, mesh=mesh, in_specs=in_specs, out_specs=out_specs, check_vma=False)
```

time: 42.3 us -> 39.3 us (0.929)
  starting transfers between devices: 13.9 us -> 10.7 us
  blocking collectives: 10.2 us -> 7.9 us
  waiting for transfers between devices: 5.27 us -> 6.79 us
  Pallas kernels: 12.4 us -> 13.3 us
    ppermute x11 -> x10, starting transfers between devices: 13.9 us -> 10.7 us  [send(): return lax.ppermute(x, 'blk', [(i, i ^ mask) for i in range(size)])]
    all_to_all x1, blocking collectives: 10.2 us -> 7.9 us  [per_device(): lax.all_to_all(sums.reshape(size, kept * count), 'blk', 0, 0, tiled=True,...]
    ppermute x11 -> x10, waiting for transfers between devices: 5.27 us -> 6.79 us  [send(): return lax.ppermute(x, 'blk', [(i, i ^ mask) for i in range(size)])]
    pallas_call x6 -> x7, Pallas kernels: 8.75 us -> 10 us  [the longest x3 5.19 us: fetch(): run(far_memory(x), after, *([] if into is None else [into]))]
  transfers between devices with their start and end apart: 11 -> 10, of which waited for: 6 -> 4; matrix products, arithmetic and copies ran while one was open for 0% -> 0% of each run, Pallas kernels for 19% -> 22%
where the time goes in v4:
time: 39.3 us; the launch traced here: 39 us
  Pallas kernels  13.3 us (34%)
  starting transfers between devices  10.7 us (27%)
  blocking collectives  7.9 us (20%)
  waiting for transfers between devices  6.79 us (17%)
    ppermute x10, starting transfers between devices, send(): return lax.ppermute(x, 'blk', [(i, i ^ mask) for i in range(size)])  10.7 us
    all_to_all x1, blocking collectives, per_device(): lax.all_to_all(sums.reshape(size, kept * count), 'blk', 0, 0, tiled=True,...  7.9 us
    ppermute x10, waiting for transfers between devices, send(): return lax.ppermute(x, 'blk', [(i, i ^ mask) for i in range(size)])  6.79 us
    pallas_call x3, Pallas kernels, fetch(): run(far_memory(x), after, *([] if into is None else [into]))  5.19 us
    pallas_call x3, Pallas kernels, run(): call(functools.partial(body, masks=masks), name, out_shape, 2 * count * s...  4.79 us
    pallas_call x1, Pallas kernels, per_device(): call(functools.partial(panel_body, order=order), 'panel', (jax.ShapeDtype...  2.49 us
  transfers between devices with their start and end apart: 10, of which 4 were waited for; matrix products, arithmetic and copies ran while one was open for 0% of the time, Pallas kernels for 22%

profile of v4, /device:TPU:0, one launch (start us, length us, event | category | flops | bytes accessed | tf_op | source)
XLA Modules:
  0.0 39.0 jit_solution(7903412665344542570)
XLA Ops:
  0.0 2.4 %collective-permute-start = (bf16[1,8192]{1,0:T(2,128)(2,1)}, bf16[1,8192]{1,0:T(2,128)(2,1)S(1)}, u32[]{:S(2)}, u32[]{:S(2)}) collective-permute-start(bf16[1,8192]{1,0:T(2,128)(2,1)} %x_ref.3), channel_id=1, source_target_pairs={{0,3},{1,2},{2,1},{3,0},{4,7},{5,6},{6,5},{7,4},{8,11},{9,10},{10,... | collective-permute-start | bytes 49160 | tf_op jit(solution)/shard_map/ppermute | solution.py:41
  2.4 0.8 %fetch.3.refs_0_ = bf16[1,8192]{1,0:T(2,128)(2,1)S(1)} custom-call(bf16[1,8192]{1,0:T(2,128)(2,1)} %x_ref.3, s32[1]{0:T(128)} %bitcast.refs_0_.me_ref), custom_call_target="tpu_custom_call" | custom-call | bytes 32768 | tf_op jit(solution)/shard_map/fetch/pallas_call | solution.py:72
  3.2 2.2 %fetch.4.refs_2_.refs_1_ = bf16[512,8192]{1,0:T(8,128)(2,1)S(1)} custom-call(bf16[512,8192]{1,0:T(8,128)(2,1)} %x_ref.5, bf16[1,8192]{1,0:T(2,128)(2,1)S(1)} %fetch.3.refs_0_), custom_call_target="tpu_custom_call" | custom-call | bytes 8388608 | tf_op jit(solution)/shard_map/fetch/pallas_call | solution.py:72
  5.4 0.0 collective-permute-done.refs_1_
  5.4 0.1 pack.2.refs_0_
  5.5 2.9 %collective-permute-start.3 = (bf16[2,8192]{1,0:T(2,128)(2,1)S(1)}, bf16[2,8192]{1,0:T(2,128)(2,1)S(1)}, u32[]{:S(2)}, u32[]{:S(2)}) collective-permute-start(bf16[2,8192]{1,0:T(2,128)(2,1)S(1)} %pack.2.refs_0_), channel_id=1, source_target_pairs={{0,9},{1,8},{2,11},{3,10},{4,13},{5,12},{6,15},{7,14},{8,1},{9,0},... | collective-permute-start | bytes 98312 | tf_op jit(solution)/shard_map/ppermute | solution.py:41
  8.4 1.1 %collective-permute-start.2 = (bf16[2,8192]{1,0:T(2,128)(2,1)S(1)}, bf16[2,8192]{1,0:T(2,128)(2,1)S(1)}, u32[]{:S(2)}, u32[]{:S(2)}) collective-permute-start(bf16[2,8192]{1,0:T(2,128)(2,1)S(1)} %pack.2.refs_0_), channel_id=1, source_target_pairs={{0,13},{1,12},{2,15},{3,14},{4,9},{5,8},{6,11},{7,10},{8,5},{9,4},... | collective-permute-start | bytes 98312 | tf_op jit(solution)/shard_map/ppermute | solution.py:41
  9.5 0.0 collective-permute-start.1
  9.5 2.2 %fetch.5.refs_4_.refs_2_ = bf16[512,8192]{1,0:T(8,128)(2,1)S(1)} custom-call(bf16[512,8192]{1,0:T(8,128)(2,1)} %x_ref.5, bf16[2,8192]{1,0:T(2,128)(2,1)S(1)} %pack.2.refs_0_, bf16[512,8192]{1,0:T(8,128)(2,1)S(1)} %fetch.4.refs_2_.refs_1_), custom_call_target="tpu_custom_call", output_to_operand_aliasing={{}: (2, {})} | custom-call | bytes 8388608 | tf_op jit(solution)/shard_map/fetch/pallas_call | solution.py:72
  11.7 0.0 collective-permute-done.3.refs_3_
  11.7 2.3 %collective-permute-done.2.refs_2_ = bf16[2,8192]{1,0:T(2,128)(2,1)S(1)} collective-permute-done((bf16[2,8192]{1,0:T(2,128)(2,1)S(1)}, bf16[2,8192]{1,0:T(2,128)(2,1)S(1)}, u32[]{:S(2)}, u32[]{:S(2)}) %collective-permute-start.2) | collective-permute-done | bytes 32800 | tf_op jit(solution)/shard_map/ppermute | solution.py:41
  14.0 0.0 collective-permute-done.1.refs_1_
  14.0 0.1 pack.3.refs_0_
  14.1 0.0 copy-start
  14.1 0.0 copy-start.1
  14.1 0.0 copy-start.2
  14.1 0.1 collective-permute-start.4
  14.2 1.3 %collective-permute-done.4.refs_1_ = bf16[8,8192]{1,0:T(8,128)(2,1)S(1)} collective-permute-done((bf16[8,8192]{1,0:T(8,128)(2,1)S(1)}, bf16[8,8192]{1,0:T(8,128)(2,1)S(1)}, u32[]{:S(2)}, u32[]{:S(2)}) %collective-permute-start.4) | collective-permute-done | bytes 131104 | tf_op jit(solution)/shard_map/ppermute | solution.py:41
  15.5 2.5 %panel.1 = (bf16[16,512]{1,0:T(8,128)(2,1)S(1)}, bf16[320,8192]{1,0:T(8,128)(2,1)S(1)}) custom-call(s32[1]{0:T(128)} %bitcast.refs_0_.me_ref, bf16[8,8192]{1,0:T(8,128)(2,1)S(1)} %pack.3.refs_0_, bf16[8,8192]{1,0:T(8,128)(2,1)S(1)} %collective-permute-done.4.refs_1_, bf16[512,8192]{1,0:T(8,128)(2,1)S(1)} %fetch.5.refs_4_.refs_2_, bf16[512,8192]{1,0:T(8,128)(2,1)} %docs_ref.1), custom_call_target="tpu_custom_call" | custom-call | flops 134217728 | bytes 8388608 | tf_op jit(solution)/shard_map/panel/pallas_call | solution.py:265
  18.0 0.8 %collective-permute-start.5 = (bf16[16,512]{1,0:T(8,128)(2,1)S(1)}, bf16[16,512]{1,0:T(8,128)(2,1)S(1)}, u32[]{:S(2)}, u32[]{:S(2)}) collective-permute-start(bf16[16,512]{1,0:T(8,128)(2,1)S(1)} %get-tuple-element.12), channel_id=1, source_target_pairs={{0,3},{1,2},{2,1},{3,0},{4,7},{5,6},{6,5},{7,4},{8,11},{9,10},{10,... | collective-permute-start | bytes 49160 | tf_op jit(solution)/shard_map/ppermute | solution.py:41
  18.8 2.5 %collective-permute-done.5 = bf16[16,512]{1,0:T(8,128)(2,1)S(1)} collective-permute-done((bf16[16,512]{1,0:T(8,128)(2,1)S(1)}, bf16[16,512]{1,0:T(8,128)(2,1)S(1)}, u32[]{:S(2)}, u32[]{:S(2)}) %collective-permute-start.5) | collective-permute-done | bytes 16416 | tf_op jit(solution)/shard_map/ppermute | solution.py:41
  21.3 0.7 %collective-permute-start.8 = (bf16[2,16,512]{2,1,0:T(8,128)(2,1)S(1)}, bf16[2,16,512]{2,1,0:T(8,128)(2,1)S(1)}, u32[]{:S(2)}, u32[]{:S(2)}) collective-permute-start(bf16[2,16,512]{2,1,0:T(8,128)(2,1)S(1)} %pad_maximum_fusion.refs_0_), channel_id=1, source_target_pairs={{0,9},{1,8},{2,11},{3,10},{4,13},{5,12},{6,15},{7,14},{8,1},{9,0},... | collective-permute-start | bytes 98312 | tf_op jit(solution)/shard_map/ppermute | solution.py:41
  21.9 1.3 %collective-permute-start.7 = (bf16[2,16,512]{2,1,0:T(8,128)(2,1)S(1)}, bf16[2,16,512]{2,1,0:T(8,128)(2,1)S(1)}, u32[]{:S(2)}, u32[]{:S(2)}) collective-permute-start(bf16[2,16,512]{2,1,0:T(8,128)(2,1)S(1)} %pad_maximum_fusion.refs_0_), channel_id=1, source_target_pairs={{0,13},{1,12},{2,15},{3,14},{4,9},{5,8},{6,11},{7,10},{8,5},{9,4},... | collective-permute-start | bytes 98312 | tf_op jit(solution)/shard_map/ppermute | solution.py:41
  23.2 1.1 %collective-permute-start.6 = (bf16[2,16,512]{2,1,0:T(8,128)(2,1)S(1)}, bf16[2,16,512]{2,1,0:T(8,128)(2,1)S(1)}, u32[]{:S(2)}, u32[]{:S(2)}) collective-permute-start(bf16[2,16,512]{2,1,0:T(8,128)(2,1)S(1)} %pad_maximum_fusion.refs_0_), channel_id=1, source_target_pairs={{0,5},{1,4},{2,7},{3,6},{4,1},{5,0},{6,3},{7,2},{8,13},{9,12},{10,... | collective-permute-start | bytes 98312 | tf_op jit(solution)/shard_map/ppermute | solution.py:41
  24.2 0.0 copy-done
  24.2 0.0 copy-done.1
  24.2 0.0 copy-done.2
  24.2 2.2 %scores_first.1 = (f32[16,512]{1,0:T(8,128)S(1)}, bf16[128,512]{1,0:T(8,128)(2,1)S(1)}, f32[16,512]{1,0:T(8,128)S(1)}, bf16[192,8192]{1,0:T(8,128)(2,1)S(1)}) custom-call(s32[1]{0:T(128)} %bitcast.refs_0_.me_ref, bf16[320,8192]{1,0:T(8,128)(2,1)S(1)} %get-tuple-element.11.low_ref, bf16[512,8192]{1,0:T(8,128)(2,1)} %docs_ref.1, s32[4,16]{1,0:T(4,128)S(1)} %copy-done, ...), custom_call_target="tpu_custom_call" | custom-call | flops 16777216 | bytes 1048576 | tf_op jit(solution)/shard_map/scores_first/pallas_call | solution.py:209
  26.5 0.0 collective-permute-done.8.refs_2_.refs_3_
  26.5 0.7 %collective-permute-done.7.refs_1_.refs_2_ = bf16[2,16,512]{2,1,0:T(8,128)(2,1)S(1)} collective-permute-done((bf16[2,16,512]{2,1,0:T(8,128)(2,1)S(1)}, bf16[2,16,512]{2,1,0:T(8,128)(2,1)S(1)}, u32[]{:S(2)}, u32[]{:S(2)}) %collective-permute-start.7) | collective-permute-done | bytes 32800 | tf_op jit(solution)/shard_map/ppermute | solution.py:41
  27.2 0.0 collective-permute-done.6.refs_0_.refs_1_
  27.2 0.5 %collective-permute-start.9 = (bf16[8,16,512]{2,1,0:T(8,128)(2,1)S(1)}, bf16[8,16,512]{2,1,0:T(8,128)(2,1)S(1)}, u32[]{:S(2)}, u32[]{:S(2)}) collective-permute-start(bf16[8,16,512]{2,1,0:T(8,128)(2,1)S(1)} %stack.13), channel_id=1, source_target_pairs={{0,1},{1,0},{2,3},{3,2},{4,5},{5,4},{6,7},{7,6},{8,9},{9,8},{10,11... | collective-permute-start | bytes 393224 | tf_op jit(solution)/shard_map/ppermute | solution.py:41
  27.7 1.0 %scores_next.1.sum_ref = f32[16,512]{1,0:T(8,128)S(1)} custom-call(s32[1]{0:T(128)} %bitcast.refs_0_.me_ref, bf16[320,8192]{1,0:T(8,128)(2,1)S(1)} %get-tuple-element.11.low_ref, bf16[192,8192]{1,0:T(8,128)(2,1)S(1)} %get-tuple-element.13.high_ref, f32[16,512]{1,0:T(8,128)S(1)} %get-tuple-element.14.sum_ref.refs_4_, ...), custom_call_target="tpu_custom_call" | custom-call | flops 50331648 | bytes 3145728 | tf_op jit(solution)/shard_map/scores_next/pallas_call | solution.py:209
  28.7 0.0 collective-permute-done.9.refs_0_
  28.7 1.6 %sums.1 = f32[128,16]{1,0:T(8,128)S(1)} custom-call(s32[1]{0:T(128)} %bitcast.refs_0_.me_ref, bf16[320,8192]{1,0:T(8,128)(2,1)S(1)} %get-tuple-element.11.low_ref, bf16[192,8192]{1,0:T(8,128)(2,1)S(1)} %get-tuple-element.13.high_ref, f32[16,512]{1,0:T(8,128)S(1)} %scores_next.1.sum_ref, bf16[128,512]{1,0:T(8,128)(2,1)S(1)} %get-tuple-element.15.hot_ref, ...), custom_call_target="tpu_custom_call" | custom-call | flops 67108864 | bytes 4194304 | tf_op jit(solution)/shard_map/sums/pallas_call | solution.py:209
  30.3 0.1 all_to_all.7
  30.4 7.9 %all_to_all.11 = f32[16,1,128]{2,1,0:T(1,128)S(1)} all-to-all(f32[16,1,128]{2,1,0:T(1,128)S(1)} %bitcast.11), channel_id=1, replica_groups={{15,14,13,12,11,10,9,8,7,6,5,4,3,2,1,0},{31,30,29,28,27,26,25,24,23,22,..., dimensions={0} | all-to-all | bytes 16384 | tf_op jit(solution)/shard_map/all_to_all | solution.py:288
  38.3 0.7 %total.1 = f32[8,16]{1,0:T(8,128)} custom-call(f32[16,128]{1,0:T(8,128)S(1)} %bitcast.7), custom_call_target="tpu_custom_call" | custom-call | bytes 16384 | tf_op jit(solution)/shard_map/total/pallas_call | solution.py:289
  (2 shorter events, 0.0 us)
Async XLA Ops:
  0.0 5.4 %collective-permute-start = (bf16[1,8192]{1,0:T(2,128)(2,1)}, bf16[1,8192]{1,0:T(2,128)(2,1)S(1)}, u32[]{:S(2)}, u32[]{:S(2)}) collective-permute-start(bf16[1,8192]{1,0:T(2,128)(2,1)} %x_ref.3), channel_id=1, source_target_pairs={{0,3},{1,2},{2,1},{3,0},{4,7},{5,6},{6,5},{7,4},{8,11},{9,10},{10,... | collective-permute-start | bytes 49160 | tf_op jit(solution)/shard_map/ppermute | solution.py:41
  5.5 6.2 %collective-permute-start.3 = (bf16[2,8192]{1,0:T(2,128)(2,1)S(1)}, bf16[2,8192]{1,0:T(2,128)(2,1)S(1)}, u32[]{:S(2)}, u32[]{:S(2)}) collective-permute-start(bf16[2,8192]{1,0:T(2,128)(2,1)S(1)} %pack.2.refs_0_), channel_id=1, source_target_pairs={{0,9},{1,8},{2,11},{3,10},{4,13},{5,12},{6,15},{7,14},{8,1},{9,0},... | collective-permute-start | bytes 98312 | tf_op jit(solution)/shard_map/ppermute | solution.py:41
  8.4 5.6 %collective-permute-start.2 = (bf16[2,8192]{1,0:T(2,128)(2,1)S(1)}, bf16[2,8192]{1,0:T(2,128)(2,1)S(1)}, u32[]{:S(2)}, u32[]{:S(2)}) collective-permute-start(bf16[2,8192]{1,0:T(2,128)(2,1)S(1)} %pack.2.refs_0_), channel_id=1, source_target_pairs={{0,13},{1,12},{2,15},{3,14},{4,9},{5,8},{6,11},{7,10},{8,5},{9,4},... | collective-permute-start | bytes 98312 | tf_op jit(solution)/shard_map/ppermute | solution.py:41
  9.5 4.5 %collective-permute-start.1 = (bf16[2,8192]{1,0:T(2,128)(2,1)S(1)}, bf16[2,8192]{1,0:T(2,128)(2,1)S(1)}, u32[]{:S(2)}, u32[]{:S(2)}) collective-permute-start(bf16[2,8192]{1,0:T(2,128)(2,1)S(1)} %pack.2.refs_0_), channel_id=1, source_target_pairs={{0,5},{1,4},{2,7},{3,6},{4,1},{5,0},{6,3},{7,2},{8,13},{9,12},{10,... | collective-permute-start | bytes 98312 | tf_op jit(solution)/shard_map/ppermute | solution.py:41
  14.1 10.2 %copy-start = (s32[4,16]{1,0:T(4,128)S(1)}, s32[4,16]{1,0:T(4,128)}, u32[]{:S(2)}) copy-start(s32[4,16]{1,0:T(4,128)} %mask_ref.1) | copy-start | bytes 772
  14.1 10.2 %copy-start.1 = (s32[512]{0:T(512)S(1)}, s32[512]{0:T(512)}, u32[]{:S(2)}) copy-start(s32[512]{0:T(512)} %param.10) | copy-start | bytes 6148
  14.1 10.1 %copy-start.2 = (s32[128]{0:T(128)S(1)}, s32[128]{0:T(128)}, u32[]{:S(2)}) copy-start(s32[128]{0:T(128)} %param.11) | copy-start | bytes 1540
  14.1 1.4 %collective-permute-start.4 = (bf16[8,8192]{1,0:T(8,128)(2,1)S(1)}, bf16[8,8192]{1,0:T(8,128)(2,1)S(1)}, u32[]{:S(2)}, u32[]{:S(2)}) collective-permute-start(bf16[8,8192]{1,0:T(8,128)(2,1)S(1)} %pack.3.refs_0_), channel_id=1, source_target_pairs={{0,1},{1,0},{2,3},{3,2},{4,5},{5,4},{6,7},{7,6},{8,9},{9,8},{10,11... | collective-permute-start | bytes 393224 | tf_op jit(solution)/shard_map/ppermute | solution.py:41
  18.0 3.2 %collective-permute-start.5 = (bf16[16,512]{1,0:T(8,128)(2,1)S(1)}, bf16[16,512]{1,0:T(8,128)(2,1)S(1)}, u32[]{:S(2)}, u32[]{:S(2)}) collective-permute-start(bf16[16,512]{1,0:T(8,128)(2,1)S(1)} %get-tuple-element.12), channel_id=1, source_target_pairs={{0,3},{1,2},{2,1},{3,0},{4,7},{5,6},{6,5},{7,4},{8,11},{9,10},{10,... | collective-permute-start | bytes 49160 | tf_op jit(solution)/shard_map/ppermute | solution.py:41
  21.3 5.2 %collective-permute-start.8 = (bf16[2,16,512]{2,1,0:T(8,128)(2,1)S(1)}, bf16[2,16,512]{2,1,0:T(8,128)(2,1)S(1)}, u32[]{:S(2)}, u32[]{:S(2)}) collective-permute-start(bf16[2,16,512]{2,1,0:T(8,128)(2,1)S(1)} %pad_maximum_fusion.refs_0_), channel_id=1, source_target_pairs={{0,9},{1,8},{2,11},{3,10},{4,13},{5,12},{6,15},{7,14},{8,1},{9,0},... | collective-permute-start | bytes 98312 | tf_op jit(solution)/shard_map/ppermute | solution.py:41
  21.9 5.3 %collective-permute-start.7 = (bf16[2,16,512]{2,1,0:T(8,128)(2,1)S(1)}, bf16[2,16,512]{2,1,0:T(8,128)(2,1)S(1)}, u32[]{:S(2)}, u32[]{:S(2)}) collective-permute-start(bf16[2,16,512]{2,1,0:T(8,128)(2,1)S(1)} %pad_maximum_fusion.refs_0_), channel_id=1, source_target_pairs={{0,13},{1,12},{2,15},{3,14},{4,9},{5,8},{6,11},{7,10},{8,5},{9,4},... | collective-permute-start | bytes 98312 | tf_op jit(solution)/shard_map/ppermute | solution.py:41
  23.2 4.0 %collective-permute-start.6 = (bf16[2,16,512]{2,1,0:T(8,128)(2,1)S(1)}, bf16[2,16,512]{2,1,0:T(8,128)(2,1)S(1)}, u32[]{:S(2)}, u32[]{:S(2)}) collective-permute-start(bf16[2,16,512]{2,1,0:T(8,128)(2,1)S(1)} %pad_maximum_fusion.refs_0_), channel_id=1, source_target_pairs={{0,5},{1,4},{2,7},{3,6},{4,1},{5,0},{6,3},{7,2},{8,13},{9,12},{10,... | collective-permute-start | bytes 98312 | tf_op jit(solution)/shard_map/ppermute | solution.py:41
  27.2 1.5 %collective-permute-start.9 = (bf16[8,16,512]{2,1,0:T(8,128)(2,1)S(1)}, bf16[8,16,512]{2,1,0:T(8,128)(2,1)S(1)}, u32[]{:S(2)}, u32[]{:S(2)}) collective-permute-start(bf16[8,16,512]{2,1,0:T(8,128)(2,1)S(1)} %stack.13), channel_id=1, source_target_pairs={{0,1},{1,0},{2,3},{3,2},{4,5},{5,4},{6,7},{7,6},{8,9},{9,8},{10,11... | collective-permute-start | bytes 393224 | tf_op jit(solution)/shard_map/ppermute | solution.py:41

commit v5 on v4

--- a/solution.py
+++ b/solution.py
@@ -134,6 +134,12 @@
     return jnp.concatenate([scores_of(me, r, parts) for r in docs_refs], axis=1)
 
 
+def kept_by(size):
+    outer, inner = split(size)
+    groups = [*range(outer - 2, 0, -1), outer - 1, 0]
+    return [g * inner + i for g in groups for i in range(inner - 1, -1, -1)]
+
+
 def first_body(me_ref, low_ref, docs_ref, mask_ref, member_ref, slot_ref, *refs, masks, size):
     parts = list(zip(refs[: len(masks)], masks))
     out_ref, hot_ref, wide_ref, high_ref, sems = refs[len(masks) :]
@@ -143,7 +149,10 @@
     clusters, docs = hot_ref.shape
     row = lax.broadcasted_iota(jnp.int32, (clusters, clusters), 0)
     kept = clusters // size
-    slot = (size - 1 - row // kept) * kept + row % kept
+    owner = jnp.zeros_like(row)
+    for i, device in enumerate(kept_by(size)):
+        owner = jnp.where(row // kept == i, device, owner)
+    slot = owner * kept + row % kept
     by_slot = (slot == slot_ref[...]).astype(jnp.float32).astype(jnp.bfloat16)
     cluster = lax.broadcasted_iota(jnp.int32, (clusters, docs), 0)
     by_doc = (cluster == member_ref[...]).astype(jnp.float32).astype(jnp.bfloat16)
@@ -190,7 +199,7 @@
     mask = jnp.repeat(topic_mask.T.astype(jnp.float32), docs // blocks, axis=1)
     mask = jnp.repeat(mask, precond.shape[0] // mask.shape[0], axis=0)
     masked = 0.125 * (dot(precond, docs_in) * mask)
-    slot = jnp.arange(clusters).reshape(size, -1)[::-1].reshape(-1)
+    slot = jnp.arange(clusters).reshape(size, -1)[jnp.array(kept_by(size))].reshape(-1)
     by_slot = (slot[:, None] == owner_slot[None, :]).astype(jnp.bfloat16)
     by_doc = (jnp.arange(clusters)[:, None] == membership[None, :]).astype(jnp.bfloat16)
     hot = jnp.dot(by_slot, by_doc, preferred_element_type=jnp.float32).astype(jnp.bfloat16)
@@ -220,13 +229,13 @@
             total,
             pltpu.VMEM((docs - docs_low.shape[0], width), doc_grads.dtype),
         ),
-        [own],
+        [own, (send(own[0], size, 1), [mask ^ 1 for mask in own[1]])],
         (me, docs_low, far_memory(doc_grads), topic_mask, membership.reshape(1, docs), owner_slot.reshape(1, clusters)),
         [SMEM, VMEM, HBM] + [VMEM] * 3,
         scratch_shapes=[pltpu.SemaphoreType.DMA((1,))],
     )
     both = (docs_low, near_memory(docs_high))
-    arrays, masks = zip(own, *came)
+    arrays, masks = zip(*came)
     shape = (sum(a.shape[0] for a in arrays),) + arrays[0].shape[1:]
     held = call(stack_body, "stack", jax.ShapeDtypeStruct(shape, arrays[0].dtype), 0, 4 * math.prod(shape))(
         in_specs=[VMEM] * len(arrays) + [pl.BlockSpec(memory_space=pl.ANY)], out_specs=VMEM
@@ -246,14 +255,33 @@
     clusters = owner_slot.shape[0]
     kept = clusters // size
     count = size * val_local
-    order, held = [0], fetch(val_grads, me)
-    outgoing, near_hess = val_grads, None
+    half = rows // 2
+
+    def both_body(val_ref, hess_ref, _, val_out, hess_out, sems):
+        part = pl.ds(0, half)
+        copies = [
+            pltpu.make_async_copy(val_ref, val_out, sems.at[0]),
+            pltpu.make_async_copy(hess_ref.at[part], hess_out.at[part], sems.at[1]),
+        ]
+        for copy in copies:
+            copy.start()
+        for copy in copies:
+            copy.wait()
+
+    shapes = tuple(pltpu.VMEM(x.shape, x.dtype) for x in (val_grads, inv_hessian))
+    held, near_hess = call(both_body, "fetch", shapes, 0, 2 * rows * width, 1)(
+        in_specs=[HBM, HBM, pl.BlockSpec(memory_space=pl.ANY)],
+        out_specs=(VMEM, VMEM),
+        scratch_shapes=[pltpu.SemaphoreType.DMA((2,))],
+    )(far_memory(val_grads), far_memory(inv_hessian), me)
+    held, near_hess = near_memory(held), near_memory(near_hess)
+    order, outgoing = [0], val_grads
     stages = gather_stages(size)
     for k, stage in enumerate(stages):
         came = [send(outgoing, size, mask) for mask in stage]
         order += [mask ^ o for mask in stage for o in order]
-        if k < 2:
-            near_hess = fetch(inv_hessian, held, k * (rows // 2), rows // 2, into=near_hess)
+        if k == 1:
+            near_hess = fetch(inv_hessian, held, half, rows - half, into=near_hess)
         if stage is not stages[-1]:
             shape = ((len(came) + 1) * held.shape[0], width)
             held = call(pack_body, "pack", jax.ShapeDtypeStruct(shape, held.dtype), 0, 4 * shape[0] * width)(
@@ -284,8 +312,7 @@
     given = (near_memory(docs_low), doc_grads) if rows % 128 == 0 else (doc_grads,)
     sums = find(me, (own, own_masks), came, *given, topic_mask, membership, owner_slot, size=size)
 
-    backwards = list(range(size - 1, -1, -1))
-    sums = lax.all_to_all(sums.reshape(size, kept * count), "blk", 0, 0, tiled=True, axis_index_groups=[backwards])
+    sums = lax.all_to_all(sums.reshape(size, kept * count), "blk", 0, 0, tiled=True, axis_index_groups=[kept_by(size)])
     return call(total_body, "total", jax.ShapeDtypeStruct((kept, count), jnp.float32), 0, 8 * size * kept * count)(
         in_specs=[VMEM], out_specs=VMEM
     )(sums)

time: 39.3 us -> 39 us (level)
  starting transfers between devices: 10.7 us -> 13.1 us
  waiting for transfers between devices: 6.79 us -> 5.07 us
  Pallas kernels: 13.3 us -> 12.5 us
    pallas_call x3 -> x1, Pallas kernels: 5.19 us -> 2.2 us  [fetch(): run(far_memory(x), after, *([] if into is None else [into]))]
    ppermute x10 -> x11, starting transfers between devices: 10.7 us -> 13.1 us  [send(): return lax.ppermute(x, 'blk', [(i, i ^ mask) for i in range(size)])]
    pallas_call x0 -> x1, Pallas kernels: none -> 2.22 us  [per_device(): call(both_body, 'fetch', shapes, 0, 2 * rows * width, 1)]
    ppermute x10 -> x11, waiting for transfers between devices: 6.79 us -> 5.07 us  [send(): return lax.ppermute(x, 'blk', [(i, i ^ mask) for i in range(size)])]
  transfers between devices with their start and end apart: 10 -> 11, of which waited for: 4 -> 4; matrix products, arithmetic and copies ran while one was open for 0% -> 0% of each run, Pallas kernels for 22% -> 20%
where the time goes in v5:
time: 39 us; the launch traced here: 38.8 us
  starting transfers between devices  13.1 us (34%)
  Pallas kernels  12.5 us (32%)
  blocking collectives  7.9 us (20%)
  waiting for transfers between devices  5.07 us (13%)
    ppermute x11, starting transfers between devices, send(): return lax.ppermute(x, 'blk', [(i, i ^ mask) for i in range(size)])  13.1 us
    all_to_all x1, blocking collectives, per_device(): lax.all_to_all(sums.reshape(size, kept * count), 'blk', 0, 0, tiled=True,...  7.9 us
    ppermute x11, waiting for transfers between devices, send(): return lax.ppermute(x, 'blk', [(i, i ^ mask) for i in range(size)])  5.07 us
    pallas_call x3, Pallas kernels, run(): call(functools.partial(body, masks=masks), name, out_shape, 2 * count * s...  4.74 us
    pallas_call x1, Pallas kernels, per_device(): call(functools.partial(panel_body, order=order), 'panel', (jax.ShapeDtype...  2.49 us
    pallas_call x1, Pallas kernels, per_device(): call(both_body, 'fetch', shapes, 0, 2 * rows * width, 1)  2.22 us
    pallas_call x1, Pallas kernels, fetch(): run(far_memory(x), after, *([] if into is None else [into]))  2.2 us
  transfers between devices with their start and end apart: 11, of which 4 were waited for; matrix products, arithmetic and copies ran while one was open for 0% of the time, Pallas kernels for 20%

profile of v5, /device:TPU:0, one launch (start us, length us, event | category | flops | bytes accessed | tf_op | source)
XLA Modules:
  0.0 38.8 jit_solution(5775788038371006103)
XLA Ops:
  0.0 2.4 %collective-permute-start = (bf16[1,8192]{1,0:T(2,128)(2,1)}, bf16[1,8192]{1,0:T(2,128)(2,1)S(1)}, u32[]{:S(2)}, u32[]{:S(2)}) collective-permute-start(bf16[1,8192]{1,0:T(2,128)(2,1)} %val_ref.1), channel_id=1, source_target_pairs={{0,3},{1,2},{2,1},{3,0},{4,7},{5,6},{6,5},{7,4},{8,11},{9,10},{10,... | collective-permute-start | bytes 49160 | tf_op jit(solution)/shard_map/ppermute | solution.py:41
  2.4 2.2 %fetch.2 = (bf16[1,8192]{1,0:T(2,128)(2,1)S(1)}, bf16[512,8192]{1,0:T(8,128)(2,1)S(1)}) custom-call(bf16[1,8192]{1,0:T(2,128)(2,1)} %val_ref.1, bf16[512,8192]{1,0:T(8,128)(2,1)} %x_ref.1, s32[1]{0:T(128)} %bitcast._.me_ref), custom_call_target="tpu_custom_call" | custom-call | bytes 8388608 | tf_op jit(solution)/shard_map/fetch/pallas_call | solution.py:272
  4.6 0.0 collective-permute-done.refs_1_
  4.6 0.1 pack.2.refs_0_
  4.7 3.1 %collective-permute-start.3 = (bf16[2,8192]{1,0:T(2,128)(2,1)S(1)}, bf16[2,8192]{1,0:T(2,128)(2,1)S(1)}, u32[]{:S(2)}, u32[]{:S(2)}) collective-permute-start(bf16[2,8192]{1,0:T(2,128)(2,1)S(1)} %pack.2.refs_0_), channel_id=1, source_target_pairs={{0,9},{1,8},{2,11},{3,10},{4,13},{5,12},{6,15},{7,14},{8,1},{9,0},... | collective-permute-start | bytes 98312 | tf_op jit(solution)/shard_map/ppermute | solution.py:41
  7.7 1.3 %collective-permute-start.2 = (bf16[2,8192]{1,0:T(2,128)(2,1)S(1)}, bf16[2,8192]{1,0:T(2,128)(2,1)S(1)}, u32[]{:S(2)}, u32[]{:S(2)}) collective-permute-start(bf16[2,8192]{1,0:T(2,128)(2,1)S(1)} %pack.2.refs_0_), channel_id=1, source_target_pairs={{0,13},{1,12},{2,15},{3,14},{4,9},{5,8},{6,11},{7,10},{8,5},{9,4},... | collective-permute-start | bytes 98312 | tf_op jit(solution)/shard_map/ppermute | solution.py:41
  9.1 0.3 collective-permute-start.1
  9.3 2.2 %fetch.3.refs_4_.refs_2_ = bf16[512,8192]{1,0:T(8,128)(2,1)S(1)} custom-call(bf16[512,8192]{1,0:T(8,128)(2,1)} %x_ref.1, bf16[2,8192]{1,0:T(2,128)(2,1)S(1)} %pack.2.refs_0_, bf16[512,8192]{1,0:T(8,128)(2,1)S(1)} %get-tuple-element.14.refs_2_.refs_1_), custom_call_target="tpu_custom_call", output_to_operand_aliasing={{}: (2, {})} | custom-call | bytes 8388608 | tf_op jit(solution)/shard_map/fetch/pallas_call | solution.py:72
  11.5 0.0 collective-permute-done.3.refs_3_
  11.6 1.4 %collective-permute-done.2.refs_2_ = bf16[2,8192]{1,0:T(2,128)(2,1)S(1)} collective-permute-done((bf16[2,8192]{1,0:T(2,128)(2,1)S(1)}, bf16[2,8192]{1,0:T(2,128)(2,1)S(1)}, u32[]{:S(2)}, u32[]{:S(2)}) %collective-permute-start.2) | collective-permute-done | bytes 32800 | tf_op jit(solution)/shard_map/ppermute | solution.py:41
  13.0 0.0 collective-permute-done.1.refs_1_
  13.0 0.1 pack.3.refs_0_
  13.1 0.0 copy-start
  13.1 0.0 copy-start.1
  13.1 0.0 copy-start.2
  13.1 0.6 %collective-permute-start.4 = (bf16[8,8192]{1,0:T(8,128)(2,1)S(1)}, bf16[8,8192]{1,0:T(8,128)(2,1)S(1)}, u32[]{:S(2)}, u32[]{:S(2)}) collective-permute-start(bf16[8,8192]{1,0:T(8,128)(2,1)S(1)} %pack.3.refs_0_), channel_id=1, source_target_pairs={{0,1},{1,0},{2,3},{3,2},{4,5},{5,4},{6,7},{7,6},{8,9},{9,8},{10,11... | collective-permute-start | bytes 393224 | tf_op jit(solution)/shard_map/ppermute | solution.py:41
  13.7 1.0 %collective-permute-done.4.refs_1_ = bf16[8,8192]{1,0:T(8,128)(2,1)S(1)} collective-permute-done((bf16[8,8192]{1,0:T(8,128)(2,1)S(1)}, bf16[8,8192]{1,0:T(8,128)(2,1)S(1)}, u32[]{:S(2)}, u32[]{:S(2)}) %collective-permute-start.4) | collective-permute-done | bytes 131104 | tf_op jit(solution)/shard_map/ppermute | solution.py:41
  14.7 2.5 %panel.1 = (bf16[16,512]{1,0:T(8,128)(2,1)S(1)}, bf16[320,8192]{1,0:T(8,128)(2,1)S(1)}) custom-call(s32[1]{0:T(128)} %bitcast._.me_ref, bf16[8,8192]{1,0:T(8,128)(2,1)S(1)} %pack.3.refs_0_, bf16[8,8192]{1,0:T(8,128)(2,1)S(1)} %collective-permute-done.4.refs_1_, bf16[512,8192]{1,0:T(8,128)(2,1)S(1)} %fetch.3.refs_4_.refs_2_, bf16[512,8192]{1,0:T(8,128)(2,1)} %docs_ref.1), custom_call_target="tpu_custom_call" | custom-call | flops 134217728 | bytes 8388608 | tf_op jit(solution)/shard_map/panel/pallas_call | solution.py:293
  17.2 1.6 %collective-permute-start.5 = (bf16[16,512]{1,0:T(8,128)(2,1)S(1)}, bf16[16,512]{1,0:T(8,128)(2,1)S(1)}, u32[]{:S(2)}, u32[]{:S(2)}) collective-permute-start(bf16[16,512]{1,0:T(8,128)(2,1)S(1)} %get-tuple-element.16), channel_id=1, source_target_pairs={{0,3},{1,2},{2,1},{3,0},{4,7},{5,6},{6,5},{7,4},{8,11},{9,10},{10,... | collective-permute-start | bytes 49160 | tf_op jit(solution)/shard_map/ppermute | solution.py:41
  18.8 1.7 %collective-permute-done.5 = bf16[16,512]{1,0:T(8,128)(2,1)S(1)} collective-permute-done((bf16[16,512]{1,0:T(8,128)(2,1)S(1)}, bf16[16,512]{1,0:T(8,128)(2,1)S(1)}, u32[]{:S(2)}, u32[]{:S(2)}) %collective-permute-start.5) | collective-permute-done | bytes 16416 | tf_op jit(solution)/shard_map/ppermute | solution.py:41
  20.5 0.3 collective-permute-start.6
  20.8 1.2 %collective-permute-start.9 = (bf16[2,16,512]{2,1,0:T(8,128)(2,1)S(1)}, bf16[2,16,512]{2,1,0:T(8,128)(2,1)S(1)}, u32[]{:S(2)}, u32[]{:S(2)}) collective-permute-start(bf16[2,16,512]{2,1,0:T(8,128)(2,1)S(1)} %pad_maximum_fusion.refs_0_), channel_id=1, source_target_pairs={{0,9},{1,8},{2,11},{3,10},{4,13},{5,12},{6,15},{7,14},{8,1},{9,0},... | collective-permute-start | bytes 98312 | tf_op jit(solution)/shard_map/ppermute | solution.py:41
  22.1 0.9 %collective-permute-start.8 = (bf16[2,16,512]{2,1,0:T(8,128)(2,1)S(1)}, bf16[2,16,512]{2,1,0:T(8,128)(2,1)S(1)}, u32[]{:S(2)}, u32[]{:S(2)}) collective-permute-start(bf16[2,16,512]{2,1,0:T(8,128)(2,1)S(1)} %pad_maximum_fusion.refs_0_), channel_id=1, source_target_pairs={{0,13},{1,12},{2,15},{3,14},{4,9},{5,8},{6,11},{7,10},{8,5},{9,4},... | collective-permute-start | bytes 98312 | tf_op jit(solution)/shard_map/ppermute | solution.py:41
  22.9 0.9 %collective-permute-start.7 = (bf16[2,16,512]{2,1,0:T(8,128)(2,1)S(1)}, bf16[2,16,512]{2,1,0:T(8,128)(2,1)S(1)}, u32[]{:S(2)}, u32[]{:S(2)}) collective-permute-start(bf16[2,16,512]{2,1,0:T(8,128)(2,1)S(1)} %pad_maximum_fusion.refs_0_), channel_id=1, source_target_pairs={{0,5},{1,4},{2,7},{3,6},{4,1},{5,0},{6,3},{7,2},{8,13},{9,12},{10,... | collective-permute-start | bytes 98312 | tf_op jit(solution)/shard_map/ppermute | solution.py:41
  23.8 0.0 collective-permute-done.6.refs_1_
  23.8 0.0 copy-done
  23.8 0.0 copy-done.1
  23.8 0.0 copy-done.2
  23.8 2.5 %scores_first.1 = (f32[16,512]{1,0:T(8,128)S(1)}, bf16[128,512]{1,0:T(8,128)(2,1)S(1)}, f32[16,512]{1,0:T(8,128)S(1)}, bf16[192,8192]{1,0:T(8,128)(2,1)S(1)}) custom-call(s32[1]{0:T(128)} %bitcast._.me_ref, bf16[320,8192]{1,0:T(8,128)(2,1)S(1)} %get-tuple-element.15.low_ref, bf16[512,8192]{1,0:T(8,128)(2,1)} %docs_ref.1, s32[4,16]{1,0:T(4,128)S(1)} %copy-done, ...), custom_call_target="tpu_custom_call" | custom-call | flops 33554432 | bytes 2097152 | tf_op jit(solution)/shard_map/scores_first/pallas_call | solution.py:218
  26.3 0.0 collective-permute-done.9.refs_2_
  26.3 0.9 %collective-permute-done.8.refs_1_ = bf16[2,16,512]{2,1,0:T(8,128)(2,1)S(1)} collective-permute-done((bf16[2,16,512]{2,1,0:T(8,128)(2,1)S(1)}, bf16[2,16,512]{2,1,0:T(8,128)(2,1)S(1)}, u32[]{:S(2)}, u32[]{:S(2)}) %collective-permute-start.8) | collective-permute-done | bytes 32800 | tf_op jit(solution)/shard_map/ppermute | solution.py:41
  27.2 0.0 collective-permute-done.7.refs_0_
  27.2 0.6 %collective-permute-start.10 = (bf16[6,16,512]{2,1,0:T(8,128)(2,1)S(1)}, bf16[6,16,512]{2,1,0:T(8,128)(2,1)S(1)}, u32[]{:S(2)}, u32[]{:S(2)}) collective-permute-start(bf16[6,16,512]{2,1,0:T(8,128)(2,1)S(1)} %stack.13), channel_id=1, source_target_pairs={{0,1},{1,0},{2,3},{3,2},{4,5},{5,4},{6,7},{7,6},{8,9},{9,8},{10,11... | collective-permute-start | bytes 294920 | tf_op jit(solution)/shard_map/ppermute | solution.py:41
  27.8 1.0 %scores_next.1.sum_ref = f32[16,512]{1,0:T(8,128)S(1)} custom-call(s32[1]{0:T(128)} %bitcast._.me_ref, bf16[320,8192]{1,0:T(8,128)(2,1)S(1)} %get-tuple-element.15.low_ref, bf16[192,8192]{1,0:T(8,128)(2,1)S(1)} %get-tuple-element.17.high_ref, f32[16,512]{1,0:T(8,128)S(1)} %get-tuple-element.18.sum_ref.refs_3_, ...), custom_call_target="tpu_custom_call" | custom-call | flops 50331648 | bytes 3145728 | tf_op jit(solution)/shard_map/scores_next/pallas_call | solution.py:218
  28.8 0.0 collective-permute-done.10.refs_0_
  28.8 1.3 %sums.1 = f32[128,16]{1,0:T(8,128)S(1)} custom-call(s32[1]{0:T(128)} %bitcast._.me_ref, bf16[320,8192]{1,0:T(8,128)(2,1)S(1)} %get-tuple-element.15.low_ref, bf16[192,8192]{1,0:T(8,128)(2,1)S(1)} %get-tuple-element.17.high_ref, f32[16,512]{1,0:T(8,128)S(1)} %scores_next.1.sum_ref, bf16[128,512]{1,0:T(8,128)(2,1)S(1)} %get-tuple-element.19.hot_ref, ...), custom_call_target="tpu_custom_call" | custom-call | flops 50331648 | bytes 3145728 | tf_op jit(solution)/shard_map/sums/pallas_call | solution.py:218
  30.1 0.1 all_to_all.7
  30.2 7.9 %all_to_all.11 = f32[16,1,128]{2,1,0:T(1,128)S(1)} all-to-all(f32[16,1,128]{2,1,0:T(1,128)S(1)} %bitcast.11), channel_id=1, replica_groups={{11,10,9,8,7,6,5,4,15,14,13,12,3,2,1,0},{27,26,25,24,23,22,21,20,31,30,..., dimensions={0} | all-to-all | bytes 16384 | tf_op jit(solution)/shard_map/all_to_all | solution.py:315
  38.1 0.7 %total.1 = f32[8,16]{1,0:T(8,128)} custom-call(f32[16,128]{1,0:T(8,128)S(1)} %bitcast.7), custom_call_target="tpu_custom_call" | custom-call | bytes 16384 | tf_op jit(solution)/shard_map/total/pallas_call | solution.py:316
  (2 shorter events, 0.0 us)
Async XLA Ops:
  0.0 4.6 %collective-permute-start = (bf16[1,8192]{1,0:T(2,128)(2,1)}, bf16[1,8192]{1,0:T(2,128)(2,1)S(1)}, u32[]{:S(2)}, u32[]{:S(2)}) collective-permute-start(bf16[1,8192]{1,0:T(2,128)(2,1)} %val_ref.1), channel_id=1, source_target_pairs={{0,3},{1,2},{2,1},{3,0},{4,7},{5,6},{6,5},{7,4},{8,11},{9,10},{10,... | collective-permute-start | bytes 49160 | tf_op jit(solution)/shard_map/ppermute | solution.py:41
  4.7 6.9 %collective-permute-start.3 = (bf16[2,8192]{1,0:T(2,128)(2,1)S(1)}, bf16[2,8192]{1,0:T(2,128)(2,1)S(1)}, u32[]{:S(2)}, u32[]{:S(2)}) collective-permute-start(bf16[2,8192]{1,0:T(2,128)(2,1)S(1)} %pack.2.refs_0_), channel_id=1, source_target_pairs={{0,9},{1,8},{2,11},{3,10},{4,13},{5,12},{6,15},{7,14},{8,1},{9,0},... | collective-permute-start | bytes 98312 | tf_op jit(solution)/shard_map/ppermute | solution.py:41
  7.7 5.3 %collective-permute-start.2 = (bf16[2,8192]{1,0:T(2,128)(2,1)S(1)}, bf16[2,8192]{1,0:T(2,128)(2,1)S(1)}, u32[]{:S(2)}, u32[]{:S(2)}) collective-permute-start(bf16[2,8192]{1,0:T(2,128)(2,1)S(1)} %pack.2.refs_0_), channel_id=1, source_target_pairs={{0,13},{1,12},{2,15},{3,14},{4,9},{5,8},{6,11},{7,10},{8,5},{9,4},... | collective-permute-start | bytes 98312 | tf_op jit(solution)/shard_map/ppermute | solution.py:41
  9.1 3.9 %collective-permute-start.1 = (bf16[2,8192]{1,0:T(2,128)(2,1)S(1)}, bf16[2,8192]{1,0:T(2,128)(2,1)S(1)}, u32[]{:S(2)}, u32[]{:S(2)}) collective-permute-start(bf16[2,8192]{1,0:T(2,128)(2,1)S(1)} %pack.2.refs_0_), channel_id=1, source_target_pairs={{0,5},{1,4},{2,7},{3,6},{4,1},{5,0},{6,3},{7,2},{8,13},{9,12},{10,... | collective-permute-start | bytes 98312 | tf_op jit(solution)/shard_map/ppermute | solution.py:41
  13.1 10.7 %copy-start = (s32[4,16]{1,0:T(4,128)S(1)}, s32[4,16]{1,0:T(4,128)}, u32[]{:S(2)}) copy-start(s32[4,16]{1,0:T(4,128)} %mask_ref.1) | copy-start | bytes 772
  13.1 10.7 %copy-start.1 = (s32[512]{0:T(512)S(1)}, s32[512]{0:T(512)}, u32[]{:S(2)}) copy-start(s32[512]{0:T(512)} %param.10) | copy-start | bytes 6148
  13.1 10.7 %copy-start.2 = (s32[128]{0:T(128)S(1)}, s32[128]{0:T(128)}, u32[]{:S(2)}) copy-start(s32[128]{0:T(128)} %param.11) | copy-start | bytes 1540
  13.1 1.6 %collective-permute-start.4 = (bf16[8,8192]{1,0:T(8,128)(2,1)S(1)}, bf16[8,8192]{1,0:T(8,128)(2,1)S(1)}, u32[]{:S(2)}, u32[]{:S(2)}) collective-permute-start(bf16[8,8192]{1,0:T(8,128)(2,1)S(1)} %pack.3.refs_0_), channel_id=1, source_target_pairs={{0,1},{1,0},{2,3},{3,2},{4,5},{5,4},{6,7},{7,6},{8,9},{9,8},{10,11... | collective-permute-start | bytes 393224 | tf_op jit(solution)/shard_map/ppermute | solution.py:41
  17.2 3.2 %collective-permute-start.5 = (bf16[16,512]{1,0:T(8,128)(2,1)S(1)}, bf16[16,512]{1,0:T(8,128)(2,1)S(1)}, u32[]{:S(2)}, u32[]{:S(2)}) collective-permute-start(bf16[16,512]{1,0:T(8,128)(2,1)S(1)} %get-tuple-element.16), channel_id=1, source_target_pairs={{0,3},{1,2},{2,1},{3,0},{4,7},{5,6},{6,5},{7,4},{8,11},{9,10},{10,... | collective-permute-start | bytes 49160 | tf_op jit(solution)/shard_map/ppermute | solution.py:41
  20.5 3.3 %collective-permute-start.6 = (bf16[2,16,512]{2,1,0:T(8,128)(2,1)S(1)}, bf16[2,16,512]{2,1,0:T(8,128)(2,1)S(1)}, u32[]{:S(2)}, u32[]{:S(2)}) collective-permute-start(bf16[2,16,512]{2,1,0:T(8,128)(2,1)S(1)} %pad_maximum_fusion.refs_0_), channel_id=1, source_target_pairs={{0,1},{1,0},{2,3},{3,2},{4,5},{5,4},{6,7},{7,6},{8,9},{9,8},{10,11... | collective-permute-start | bytes 98312 | tf_op jit(solution)/shard_map/ppermute | solution.py:41
  20.8 5.5 %collective-permute-start.9 = (bf16[2,16,512]{2,1,0:T(8,128)(2,1)S(1)}, bf16[2,16,512]{2,1,0:T(8,128)(2,1)S(1)}, u32[]{:S(2)}, u32[]{:S(2)}) collective-permute-start(bf16[2,16,512]{2,1,0:T(8,128)(2,1)S(1)} %pad_maximum_fusion.refs_0_), channel_id=1, source_target_pairs={{0,9},{1,8},{2,11},{3,10},{4,13},{5,12},{6,15},{7,14},{8,1},{9,0},... | collective-permute-start | bytes 98312 | tf_op jit(solution)/shard_map/ppermute | solution.py:41
  22.1 5.1 %collective-permute-start.8 = (bf16[2,16,512]{2,1,0:T(8,128)(2,1)S(1)}, bf16[2,16,512]{2,1,0:T(8,128)(2,1)S(1)}, u32[]{:S(2)}, u32[]{:S(2)}) collective-permute-start(bf16[2,16,512]{2,1,0:T(8,128)(2,1)S(1)} %pad_maximum_fusion.refs_0_), channel_id=1, source_target_pairs={{0,13},{1,12},{2,15},{3,14},{4,9},{5,8},{6,11},{7,10},{8,5},{9,4},... | collective-permute-start | bytes 98312 | tf_op jit(solution)/shard_map/ppermute | solution.py:41
  22.9 4.3 %collective-permute-start.7 = (bf16[2,16,512]{2,1,0:T(8,128)(2,1)S(1)}, bf16[2,16,512]{2,1,0:T(8,128)(2,1)S(1)}, u32[]{:S(2)}, u32[]{:S(2)}) collective-permute-start(bf16[2,16,512]{2,1,0:T(8,128)(2,1)S(1)} %pad_maximum_fusion.refs_0_), channel_id=1, source_target_pairs={{0,5},{1,4},{2,7},{3,6},{4,1},{5,0},{6,3},{7,2},{8,13},{9,12},{10,... | collective-permute-start | bytes 98312 | tf_op jit(solution)/shard_map/ppermute | solution.py:41
  27.2 1.6 %collective-permute-start.10 = (bf16[6,16,512]{2,1,0:T(8,128)(2,1)S(1)}, bf16[6,16,512]{2,1,0:T(8,128)(2,1)S(1)}, u32[]{:S(2)}, u32[]{:S(2)}) collective-permute-start(bf16[6,16,512]{2,1,0:T(8,128)(2,1)S(1)} %stack.13), channel_id=1, source_target_pairs={{0,1},{1,0},{2,3},{3,2},{4,5},{5,4},{6,7},{7,6},{8,9},{9,8},{10,11... | collective-permute-start | bytes 294920 | tf_op jit(solution)/shard_map/ppermute | solution.py:41

commit v6 on v5

--- a/solution.py
+++ b/solution.py
@@ -151,8 +151,8 @@
     kept = clusters // size
     owner = jnp.zeros_like(row)
     for i, device in enumerate(kept_by(size)):
-        owner = jnp.where(row // kept == i, device, owner)
-    slot = owner * kept + row % kept
+        owner = jnp.where(row % size == i, device, owner)
+    slot = owner * kept + row // size
     by_slot = (slot == slot_ref[...]).astype(jnp.float32).astype(jnp.bfloat16)
     cluster = lax.broadcasted_iota(jnp.int32, (clusters, docs), 0)
     by_doc = (cluster == member_ref[...]).astype(jnp.float32).astype(jnp.bfloat16)
@@ -178,7 +178,10 @@
     masked = 0.125 * (scores * wide_ref[...])
     high = masked.astype(jnp.bfloat16)
     low = (masked - high.astype(jnp.float32)).astype(jnp.bfloat16)
-    out_ref[...] = dot(hot_ref[...], high) + dot(hot_ref[...], low)
+    both = dot(hot_ref[...], jnp.concatenate([high, low], axis=0))
+    both = both[:, : high.shape[0]] + both[:, high.shape[0] :]
+    size = out_ref.shape[0]
+    out_ref[...] = jnp.concatenate([both[r : r + size] for r in range(0, both.shape[0], size)], axis=1)
 
 
 def total_body(parts_ref, out_ref):
@@ -242,7 +245,7 @@
     )(*arrays, sums)
     other = (send(held, size, 1), [mask ^ 1 for mask in sum(masks, [])])
     sums = run(next_body, "scores_next", total, came, (me, *both, sums), [SMEM] + [VMEM] * 3)
-    shape = jax.ShapeDtypeStruct((clusters, count), jnp.float32)
+    shape = jax.ShapeDtypeStruct((size, clusters // size * count), jnp.float32)
     return run(last_body, "sums", shape, [other], (me, *both, sums, hot, wide), [SMEM] + [VMEM] * 5)
 
 
@@ -289,7 +292,7 @@
             )(held, *came, me if near_hess is None else near_hess)
             outgoing = held
     near = [held] + came
-    early = docs * 5 // 8
+    early = docs // 2
     panel, docs_low = call(
         functools.partial(panel_body, order=order),
         "panel",

time: 39 us -> 39 us (level)
  transfers between devices with their start and end apart: 11 -> 11, of which waited for: 4 -> 4; matrix products, arithmetic and copies ran while one was open for 0% -> 0% of each run, Pallas kernels for 20% -> 21%
where the time goes in v6:
time: 39 us; the launch traced here: 38.7 us
  starting transfers between devices  13.1 us (34%)
  Pallas kernels  12.7 us (33%)
  blocking collectives  8.13 us (21%)
  waiting for transfers between devices  4.69 us (12%)
    ppermute x11, starting transfers between devices, send(): return lax.ppermute(x, 'blk', [(i, i ^ mask) for i in range(size)])  13.1 us
    all_to_all x1, blocking collectives, per_device(): lax.all_to_all(sums.reshape(size, kept * count), 'blk', 0, 0, tiled=True,...  8.13 us
    pallas_call x3, Pallas kernels, run(): call(functools.partial(body, masks=masks), name, out_shape, 2 * count * s...  5.01 us
    ppermute x11, waiting for transfers between devices, send(): return lax.ppermute(x, 'blk', [(i, i ^ mask) for i in range(size)])  4.69 us
    pallas_call x1, Pallas kernels, per_device(): call(functools.partial(panel_body, order=order), 'panel', (jax.ShapeDtype...  2.45 us
    pallas_call x1, Pallas kernels, per_device(): call(both_body, 'fetch', shapes, 0, 2 * rows * width, 1)  2.22 us
    pallas_call x1, Pallas kernels, fetch(): run(far_memory(x), after, *([] if into is None else [into]))  2.2 us
  transfers between devices with their start and end apart: 11, of which 4 were waited for; matrix products, arithmetic and copies ran while one was open for 0% of the time, Pallas kernels for 21%

profile of v6, /device:TPU:0, one launch (start us, length us, event | category | flops | bytes accessed | tf_op | source)
XLA Modules:
  0.0 38.7 jit_solution(116640494809353293)
XLA Ops:
  0.0 2.4 %collective-permute-start = (bf16[1,8192]{1,0:T(2,128)(2,1)}, bf16[1,8192]{1,0:T(2,128)(2,1)S(1)}, u32[]{:S(2)}, u32[]{:S(2)}) collective-permute-start(bf16[1,8192]{1,0:T(2,128)(2,1)} %val_ref.1), channel_id=1, source_target_pairs={{0,3},{1,2},{2,1},{3,0},{4,7},{5,6},{6,5},{7,4},{8,11},{9,10},{10,... | collective-permute-start | bytes 49160 | tf_op jit(solution)/shard_map/ppermute | solution.py:41
  2.4 2.2 %fetch.2 = (bf16[1,8192]{1,0:T(2,128)(2,1)S(1)}, bf16[512,8192]{1,0:T(8,128)(2,1)S(1)}) custom-call(bf16[1,8192]{1,0:T(2,128)(2,1)} %val_ref.1, bf16[512,8192]{1,0:T(8,128)(2,1)} %x_ref.1, s32[1]{0:T(128)} %bitcast._.me_ref), custom_call_target="tpu_custom_call" | custom-call | bytes 8388608 | tf_op jit(solution)/shard_map/fetch/pallas_call | solution.py:275
  4.6 0.0 collective-permute-done.refs_1_
  4.6 0.1 pack.2.refs_0_
  4.7 3.1 %collective-permute-start.3 = (bf16[2,8192]{1,0:T(2,128)(2,1)S(1)}, bf16[2,8192]{1,0:T(2,128)(2,1)S(1)}, u32[]{:S(2)}, u32[]{:S(2)}) collective-permute-start(bf16[2,8192]{1,0:T(2,128)(2,1)S(1)} %pack.2.refs_0_), channel_id=1, source_target_pairs={{0,9},{1,8},{2,11},{3,10},{4,13},{5,12},{6,15},{7,14},{8,1},{9,0},... | collective-permute-start | bytes 98312 | tf_op jit(solution)/shard_map/ppermute | solution.py:41
  7.7 1.3 %collective-permute-start.2 = (bf16[2,8192]{1,0:T(2,128)(2,1)S(1)}, bf16[2,8192]{1,0:T(2,128)(2,1)S(1)}, u32[]{:S(2)}, u32[]{:S(2)}) collective-permute-start(bf16[2,8192]{1,0:T(2,128)(2,1)S(1)} %pack.2.refs_0_), channel_id=1, source_target_pairs={{0,13},{1,12},{2,15},{3,14},{4,9},{5,8},{6,11},{7,10},{8,5},{9,4},... | collective-permute-start | bytes 98312 | tf_op jit(solution)/shard_map/ppermute | solution.py:41
  9.1 0.3 collective-permute-start.1
  9.3 2.2 %fetch.3.refs_4_.refs_2_ = bf16[512,8192]{1,0:T(8,128)(2,1)S(1)} custom-call(bf16[512,8192]{1,0:T(8,128)(2,1)} %x_ref.1, bf16[2,8192]{1,0:T(2,128)(2,1)S(1)} %pack.2.refs_0_, bf16[512,8192]{1,0:T(8,128)(2,1)S(1)} %get-tuple-element.14.refs_2_.refs_1_), custom_call_target="tpu_custom_call", output_to_operand_aliasing={{}: (2, {})} | custom-call | bytes 8388608 | tf_op jit(solution)/shard_map/fetch/pallas_call | solution.py:72
  11.5 0.0 collective-permute-done.3.refs_3_
  11.6 1.4 %collective-permute-done.2.refs_2_ = bf16[2,8192]{1,0:T(2,128)(2,1)S(1)} collective-permute-done((bf16[2,8192]{1,0:T(2,128)(2,1)S(1)}, bf16[2,8192]{1,0:T(2,128)(2,1)S(1)}, u32[]{:S(2)}, u32[]{:S(2)}) %collective-permute-start.2) | collective-permute-done | bytes 32800 | tf_op jit(solution)/shard_map/ppermute | solution.py:41
  13.0 0.0 collective-permute-done.1.refs_1_
  13.0 0.1 pack.3.refs_0_
  13.1 0.0 copy-start
  13.1 0.0 copy-start.1
  13.1 0.0 copy-start.2
  13.1 0.6 %collective-permute-start.4 = (bf16[8,8192]{1,0:T(8,128)(2,1)S(1)}, bf16[8,8192]{1,0:T(8,128)(2,1)S(1)}, u32[]{:S(2)}, u32[]{:S(2)}) collective-permute-start(bf16[8,8192]{1,0:T(8,128)(2,1)S(1)} %pack.3.refs_0_), channel_id=1, source_target_pairs={{0,1},{1,0},{2,3},{3,2},{4,5},{5,4},{6,7},{7,6},{8,9},{9,8},{10,11... | collective-permute-start | bytes 393224 | tf_op jit(solution)/shard_map/ppermute | solution.py:41
  13.7 1.0 %collective-permute-done.4.refs_1_ = bf16[8,8192]{1,0:T(8,128)(2,1)S(1)} collective-permute-done((bf16[8,8192]{1,0:T(8,128)(2,1)S(1)}, bf16[8,8192]{1,0:T(8,128)(2,1)S(1)}, u32[]{:S(2)}, u32[]{:S(2)}) %collective-permute-start.4) | collective-permute-done | bytes 131104 | tf_op jit(solution)/shard_map/ppermute | solution.py:41
  14.7 2.5 %panel.1 = (bf16[16,512]{1,0:T(8,128)(2,1)S(1)}, bf16[256,8192]{1,0:T(8,128)(2,1)S(1)}) custom-call(s32[1]{0:T(128)} %bitcast._.me_ref, bf16[8,8192]{1,0:T(8,128)(2,1)S(1)} %pack.3.refs_0_, bf16[8,8192]{1,0:T(8,128)(2,1)S(1)} %collective-permute-done.4.refs_1_, bf16[512,8192]{1,0:T(8,128)(2,1)S(1)} %fetch.3.refs_4_.refs_2_, bf16[512,8192]{1,0:T(8,128)(2,1)} %docs_ref.1), custom_call_target="tpu_custom_call" | custom-call | flops 134217728 | bytes 8388608 | tf_op jit(solution)/shard_map/panel/pallas_call | solution.py:296
  17.2 1.6 %collective-permute-start.5 = (bf16[16,512]{1,0:T(8,128)(2,1)S(1)}, bf16[16,512]{1,0:T(8,128)(2,1)S(1)}, u32[]{:S(2)}, u32[]{:S(2)}) collective-permute-start(bf16[16,512]{1,0:T(8,128)(2,1)S(1)} %get-tuple-element.16), channel_id=1, source_target_pairs={{0,3},{1,2},{2,1},{3,0},{4,7},{5,6},{6,5},{7,4},{8,11},{9,10},{10,... | collective-permute-start | bytes 49160 | tf_op jit(solution)/shard_map/ppermute | solution.py:41
  18.7 1.7 %collective-permute-done.5 = bf16[16,512]{1,0:T(8,128)(2,1)S(1)} collective-permute-done((bf16[16,512]{1,0:T(8,128)(2,1)S(1)}, bf16[16,512]{1,0:T(8,128)(2,1)S(1)}, u32[]{:S(2)}, u32[]{:S(2)}) %collective-permute-start.5) | collective-permute-done | bytes 16416 | tf_op jit(solution)/shard_map/ppermute | solution.py:41
  20.4 0.4 collective-permute-start.6
  20.8 1.2 %collective-permute-start.9 = (bf16[2,16,512]{2,1,0:T(8,128)(2,1)S(1)}, bf16[2,16,512]{2,1,0:T(8,128)(2,1)S(1)}, u32[]{:S(2)}, u32[]{:S(2)}) collective-permute-start(bf16[2,16,512]{2,1,0:T(8,128)(2,1)S(1)} %pad_maximum_fusion.refs_0_), channel_id=1, source_target_pairs={{0,9},{1,8},{2,11},{3,10},{4,13},{5,12},{6,15},{7,14},{8,1},{9,0},... | collective-permute-start | bytes 98312 | tf_op jit(solution)/shard_map/ppermute | solution.py:41
  22.0 0.9 %collective-permute-start.8 = (bf16[2,16,512]{2,1,0:T(8,128)(2,1)S(1)}, bf16[2,16,512]{2,1,0:T(8,128)(2,1)S(1)}, u32[]{:S(2)}, u32[]{:S(2)}) collective-permute-start(bf16[2,16,512]{2,1,0:T(8,128)(2,1)S(1)} %pad_maximum_fusion.refs_0_), channel_id=1, source_target_pairs={{0,13},{1,12},{2,15},{3,14},{4,9},{5,8},{6,11},{7,10},{8,5},{9,4},... | collective-permute-start | bytes 98312 | tf_op jit(solution)/shard_map/ppermute | solution.py:41
  22.9 0.9 %collective-permute-start.7 = (bf16[2,16,512]{2,1,0:T(8,128)(2,1)S(1)}, bf16[2,16,512]{2,1,0:T(8,128)(2,1)S(1)}, u32[]{:S(2)}, u32[]{:S(2)}) collective-permute-start(bf16[2,16,512]{2,1,0:T(8,128)(2,1)S(1)} %pad_maximum_fusion.refs_0_), channel_id=1, source_target_pairs={{0,5},{1,4},{2,7},{3,6},{4,1},{5,0},{6,3},{7,2},{8,13},{9,12},{10,... | collective-permute-start | bytes 98312 | tf_op jit(solution)/shard_map/ppermute | solution.py:41
  23.8 0.0 collective-permute-done.6.refs_1_
  23.8 0.0 copy-done
  23.8 0.0 copy-done.1
  23.8 0.0 copy-done.2
  23.8 2.9 %scores_first.1 = (f32[16,512]{1,0:T(8,128)S(1)}, bf16[128,512]{1,0:T(8,128)(2,1)S(1)}, f32[16,512]{1,0:T(8,128)S(1)}, bf16[256,8192]{1,0:T(8,128)(2,1)S(1)}) custom-call(s32[1]{0:T(128)} %bitcast._.me_ref, bf16[256,8192]{1,0:T(8,128)(2,1)S(1)} %get-tuple-element.15.low_ref, bf16[512,8192]{1,0:T(8,128)(2,1)} %docs_ref.1, s32[4,16]{1,0:T(4,128)S(1)} %copy-done, ...), custom_call_target="tpu_custom_call" | custom-call | flops 33554432 | bytes 2097152 | tf_op jit(solution)/shard_map/scores_first/pallas_call | solution.py:221
  26.7 0.0 collective-permute-done.9.refs_2_
  26.7 0.5 %collective-permute-done.8.refs_1_ = bf16[2,16,512]{2,1,0:T(8,128)(2,1)S(1)} collective-permute-done((bf16[2,16,512]{2,1,0:T(8,128)(2,1)S(1)}, bf16[2,16,512]{2,1,0:T(8,128)(2,1)S(1)}, u32[]{:S(2)}, u32[]{:S(2)}) %collective-permute-start.8) | collective-permute-done | bytes 32800 | tf_op jit(solution)/shard_map/ppermute | solution.py:41
  27.2 0.0 collective-permute-done.7.refs_0_
  27.2 0.6 %collective-permute-start.10 = (bf16[6,16,512]{2,1,0:T(8,128)(2,1)S(1)}, bf16[6,16,512]{2,1,0:T(8,128)(2,1)S(1)}, u32[]{:S(2)}, u32[]{:S(2)}) collective-permute-start(bf16[6,16,512]{2,1,0:T(8,128)(2,1)S(1)} %stack.13), channel_id=1, source_target_pairs={{0,1},{1,0},{2,3},{3,2},{4,5},{5,4},{6,7},{7,6},{8,9},{9,8},{10,11... | collective-permute-start | bytes 294920 | tf_op jit(solution)/shard_map/ppermute | solution.py:41
  27.8 0.9 %scores_next.1.sum_ref = f32[16,512]{1,0:T(8,128)S(1)} custom-call(s32[1]{0:T(128)} %bitcast._.me_ref, bf16[256,8192]{1,0:T(8,128)(2,1)S(1)} %get-tuple-element.15.low_ref, bf16[256,8192]{1,0:T(8,128)(2,1)S(1)} %get-tuple-element.17.high_ref, f32[16,512]{1,0:T(8,128)S(1)} %get-tuple-element.18.sum_ref.refs_3_, ...), custom_call_target="tpu_custom_call" | custom-call | flops 50331648 | bytes 3145728 | tf_op jit(solution)/shard_map/scores_next/pallas_call | solution.py:221
  28.7 0.0 collective-permute-done.10.refs_0_
  28.7 1.2 %sums.1 = f32[16,128]{1,0:T(8,128)S(1)} custom-call(s32[1]{0:T(128)} %bitcast._.me_ref, bf16[256,8192]{1,0:T(8,128)(2,1)S(1)} %get-tuple-element.15.low_ref, bf16[256,8192]{1,0:T(8,128)(2,1)S(1)} %get-tuple-element.17.high_ref, f32[16,512]{1,0:T(8,128)S(1)} %scores_next.1.sum_ref, bf16[128,512]{1,0:T(8,128)(2,1)S(1)} %get-tuple-element.19.hot_ref, ...), custom_call_target="tpu_custom_call" | custom-call | flops 50331648 | bytes 3145728 | tf_op jit(solution)/shard_map/sums/pallas_call | solution.py:221
  29.9 8.1 %all_to_all.11 = f32[16,1,128]{2,1,0:T(1,128)S(1)} all-to-all(f32[16,1,128]{2,1,0:T(1,128)S(1)} %bitcast.9), channel_id=1, replica_groups={{11,10,9,8,7,6,5,4,15,14,13,12,3,2,1,0},{27,26,25,24,23,22,21,20,31,30,..., dimensions={0} | all-to-all | bytes 16384 | tf_op jit(solution)/shard_map/all_to_all | solution.py:318
  38.1 0.7 %total.1 = f32[8,16]{1,0:T(8,128)} custom-call(f32[16,128]{1,0:T(8,128)S(1)} %bitcast.10), custom_call_target="tpu_custom_call" | custom-call | bytes 16384 | tf_op jit(solution)/shard_map/total/pallas_call | solution.py:319
  (2 shorter events, 0.0 us)
Async XLA Ops:
  0.0 4.6 %collective-permute-start = (bf16[1,8192]{1,0:T(2,128)(2,1)}, bf16[1,8192]{1,0:T(2,128)(2,1)S(1)}, u32[]{:S(2)}, u32[]{:S(2)}) collective-permute-start(bf16[1,8192]{1,0:T(2,128)(2,1)} %val_ref.1), channel_id=1, source_target_pairs={{0,3},{1,2},{2,1},{3,0},{4,7},{5,6},{6,5},{7,4},{8,11},{9,10},{10,... | collective-permute-start | bytes 49160 | tf_op jit(solution)/shard_map/ppermute | solution.py:41
  4.7 6.9 %collective-permute-start.3 = (bf16[2,8192]{1,0:T(2,128)(2,1)S(1)}, bf16[2,8192]{1,0:T(2,128)(2,1)S(1)}, u32[]{:S(2)}, u32[]{:S(2)}) collective-permute-start(bf16[2,8192]{1,0:T(2,128)(2,1)S(1)} %pack.2.refs_0_), channel_id=1, source_target_pairs={{0,9},{1,8},{2,11},{3,10},{4,13},{5,12},{6,15},{7,14},{8,1},{9,0},... | collective-permute-start | bytes 98312 | tf_op jit(solution)/shard_map/ppermute | solution.py:41
  7.7 5.3 %collective-permute-start.2 = (bf16[2,8192]{1,0:T(2,128)(2,1)S(1)}, bf16[2,8192]{1,0:T(2,128)(2,1)S(1)}, u32[]{:S(2)}, u32[]{:S(2)}) collective-permute-start(bf16[2,8192]{1,0:T(2,128)(2,1)S(1)} %pack.2.refs_0_), channel_id=1, source_target_pairs={{0,13},{1,12},{2,15},{3,14},{4,9},{5,8},{6,11},{7,10},{8,5},{9,4},... | collective-permute-start | bytes 98312 | tf_op jit(solution)/shard_map/ppermute | solution.py:41
  9.1 3.9 %collective-permute-start.1 = (bf16[2,8192]{1,0:T(2,128)(2,1)S(1)}, bf16[2,8192]{1,0:T(2,128)(2,1)S(1)}, u32[]{:S(2)}, u32[]{:S(2)}) collective-permute-start(bf16[2,8192]{1,0:T(2,128)(2,1)S(1)} %pack.2.refs_0_), channel_id=1, source_target_pairs={{0,5},{1,4},{2,7},{3,6},{4,1},{5,0},{6,3},{7,2},{8,13},{9,12},{10,... | collective-permute-start | bytes 98312 | tf_op jit(solution)/shard_map/ppermute | solution.py:41
  13.1 10.7 %copy-start = (s32[4,16]{1,0:T(4,128)S(1)}, s32[4,16]{1,0:T(4,128)}, u32[]{:S(2)}) copy-start(s32[4,16]{1,0:T(4,128)} %mask_ref.1) | copy-start | bytes 772
  13.1 10.7 %copy-start.1 = (s32[512]{0:T(512)S(1)}, s32[512]{0:T(512)}, u32[]{:S(2)}) copy-start(s32[512]{0:T(512)} %param.10) | copy-start | bytes 6148
  13.1 10.7 %copy-start.2 = (s32[128]{0:T(128)S(1)}, s32[128]{0:T(128)}, u32[]{:S(2)}) copy-start(s32[128]{0:T(128)} %param.11) | copy-start | bytes 1540
  13.1 1.6 %collective-permute-start.4 = (bf16[8,8192]{1,0:T(8,128)(2,1)S(1)}, bf16[8,8192]{1,0:T(8,128)(2,1)S(1)}, u32[]{:S(2)}, u32[]{:S(2)}) collective-permute-start(bf16[8,8192]{1,0:T(8,128)(2,1)S(1)} %pack.3.refs_0_), channel_id=1, source_target_pairs={{0,1},{1,0},{2,3},{3,2},{4,5},{5,4},{6,7},{7,6},{8,9},{9,8},{10,11... | collective-permute-start | bytes 393224 | tf_op jit(solution)/shard_map/ppermute | solution.py:41
  17.2 3.2 %collective-permute-start.5 = (bf16[16,512]{1,0:T(8,128)(2,1)S(1)}, bf16[16,512]{1,0:T(8,128)(2,1)S(1)}, u32[]{:S(2)}, u32[]{:S(2)}) collective-permute-start(bf16[16,512]{1,0:T(8,128)(2,1)S(1)} %get-tuple-element.16), channel_id=1, source_target_pairs={{0,3},{1,2},{2,1},{3,0},{4,7},{5,6},{6,5},{7,4},{8,11},{9,10},{10,... | collective-permute-start | bytes 49160 | tf_op jit(solution)/shard_map/ppermute | solution.py:41
  20.4 3.3 %collective-permute-start.6 = (bf16[2,16,512]{2,1,0:T(8,128)(2,1)S(1)}, bf16[2,16,512]{2,1,0:T(8,128)(2,1)S(1)}, u32[]{:S(2)}, u32[]{:S(2)}) collective-permute-start(bf16[2,16,512]{2,1,0:T(8,128)(2,1)S(1)} %pad_maximum_fusion.refs_0_), channel_id=1, source_target_pairs={{0,1},{1,0},{2,3},{3,2},{4,5},{5,4},{6,7},{7,6},{8,9},{9,8},{10,11... | collective-permute-start | bytes 98312 | tf_op jit(solution)/shard_map/ppermute | solution.py:41
  20.8 5.9 %collective-permute-start.9 = (bf16[2,16,512]{2,1,0:T(8,128)(2,1)S(1)}, bf16[2,16,512]{2,1,0:T(8,128)(2,1)S(1)}, u32[]{:S(2)}, u32[]{:S(2)}) collective-permute-start(bf16[2,16,512]{2,1,0:T(8,128)(2,1)S(1)} %pad_maximum_fusion.refs_0_), channel_id=1, source_target_pairs={{0,9},{1,8},{2,11},{3,10},{4,13},{5,12},{6,15},{7,14},{8,1},{9,0},... | collective-permute-start | bytes 98312 | tf_op jit(solution)/shard_map/ppermute | solution.py:41
  22.0 5.1 %collective-permute-start.8 = (bf16[2,16,512]{2,1,0:T(8,128)(2,1)S(1)}, bf16[2,16,512]{2,1,0:T(8,128)(2,1)S(1)}, u32[]{:S(2)}, u32[]{:S(2)}) collective-permute-start(bf16[2,16,512]{2,1,0:T(8,128)(2,1)S(1)} %pad_maximum_fusion.refs_0_), channel_id=1, source_target_pairs={{0,13},{1,12},{2,15},{3,14},{4,9},{5,8},{6,11},{7,10},{8,5},{9,4},... | collective-permute-start | bytes 98312 | tf_op jit(solution)/shard_map/ppermute | solution.py:41
  22.9 4.3 %collective-permute-start.7 = (bf16[2,16,512]{2,1,0:T(8,128)(2,1)S(1)}, bf16[2,16,512]{2,1,0:T(8,128)(2,1)S(1)}, u32[]{:S(2)}, u32[]{:S(2)}) collective-permute-start(bf16[2,16,512]{2,1,0:T(8,128)(2,1)S(1)} %pad_maximum_fusion.refs_0_), channel_id=1, source_target_pairs={{0,5},{1,4},{2,7},{3,6},{4,1},{5,0},{6,3},{7,2},{8,13},{9,12},{10,... | collective-permute-start | bytes 98312 | tf_op jit(solution)/shard_map/ppermute | solution.py:41
  27.2 1.5 %collective-permute-start.10 = (bf16[6,16,512]{2,1,0:T(8,128)(2,1)S(1)}, bf16[6,16,512]{2,1,0:T(8,128)(2,1)S(1)}, u32[]{:S(2)}, u32[]{:S(2)}) collective-permute-start(bf16[6,16,512]{2,1,0:T(8,128)(2,1)S(1)} %stack.13), channel_id=1, source_target_pairs={{0,1},{1,0},{2,3},{3,2},{4,5},{5,4},{6,7},{7,6},{8,9},{9,8},{10,11... | collective-permute-start | bytes 294920 | tf_op jit(solution)/shard_map/ppermute | solution.py:41

commit v7 on v5

--- a/solution.py
+++ b/solution.py
@@ -255,7 +255,7 @@
     clusters = owner_slot.shape[0]
     kept = clusters // size
     count = size * val_local
-    half = rows // 2
+    half = rows * 3 // 8 // 16 * 16
 
     def both_body(val_ref, hess_ref, _, val_out, hess_out, sems):
         part = pl.ds(0, half)

time: 39 us -> 39 us (level)
  transfers between devices with their start and end apart: 11 -> 11, of which waited for: 4 -> 5; matrix products, arithmetic and copies ran while one was open for 0% -> 0% of each run, Pallas kernels for 20% -> 20%
where the time goes in v7:
time: 39 us; the launch traced here: 38.8 us
  starting transfers between devices  13.3 us (34%)
  Pallas kernels  12.5 us (32%)
  blocking collectives  7.9 us (20%)
  waiting for transfers between devices  4.92 us (13%)
    ppermute x11, starting transfers between devices, send(): return lax.ppermute(x, 'blk', [(i, i ^ mask) for i in range(size)])  13.3 us
    all_to_all x1, blocking collectives, per_device(): lax.all_to_all(sums.reshape(size, kept * count), 'blk', 0, 0, tiled=True,...  7.9 us
    ppermute x11, waiting for transfers between devices, send(): return lax.ppermute(x, 'blk', [(i, i ^ mask) for i in range(size)])  4.92 us
    pallas_call x3, Pallas kernels, run(): call(functools.partial(body, masks=masks), name, out_shape, 2 * count * s...  4.74 us
    pallas_call x1, Pallas kernels, per_device(): call(functools.partial(panel_body, order=order), 'panel', (jax.ShapeDtype...  2.49 us
    pallas_call x1, Pallas kernels, fetch(): run(far_memory(x), after, *([] if into is None else [into]))  2.49 us
    pallas_call x1, Pallas kernels, per_device(): call(both_body, 'fetch', shapes, 0, 2 * rows * width, 1)  1.93 us
  transfers between devices with their start and end apart: 11, of which 5 were waited for; matrix products, arithmetic and copies ran while one was open for 0% of the time, Pallas kernels for 20%

profile of v7, /device:TPU:0, one launch (start us, length us, event | category | flops | bytes accessed | tf_op | source)
XLA Modules:
  0.0 38.8 jit_solution(7745410472029069316)
XLA Ops:
  0.0 2.4 %collective-permute-start = (bf16[1,8192]{1,0:T(2,128)(2,1)}, bf16[1,8192]{1,0:T(2,128)(2,1)S(1)}, u32[]{:S(2)}, u32[]{:S(2)}) collective-permute-start(bf16[1,8192]{1,0:T(2,128)(2,1)} %val_ref.1), channel_id=1, source_target_pairs={{0,3},{1,2},{2,1},{3,0},{4,7},{5,6},{6,5},{7,4},{8,11},{9,10},{10,... | collective-permute-start | bytes 49160 | tf_op jit(solution)/shard_map/ppermute | solution.py:41
  2.4 1.9 %fetch.2 = (bf16[1,8192]{1,0:T(2,128)(2,1)S(1)}, bf16[512,8192]{1,0:T(8,128)(2,1)S(1)}) custom-call(bf16[1,8192]{1,0:T(2,128)(2,1)} %val_ref.1, bf16[512,8192]{1,0:T(8,128)(2,1)} %x_ref.1, s32[1]{0:T(128)} %bitcast._.me_ref), custom_call_target="tpu_custom_call" | custom-call | bytes 8388608 | tf_op jit(solution)/shard_map/fetch/pallas_call | solution.py:272
  4.3 0.2 collective-permute-done.refs_1_
  4.5 3.2 %collective-permute-start.3 = (bf16[2,8192]{1,0:T(2,128)(2,1)S(1)}, bf16[2,8192]{1,0:T(2,128)(2,1)S(1)}, u32[]{:S(2)}, u32[]{:S(2)}) collective-permute-start(bf16[2,8192]{1,0:T(2,128)(2,1)S(1)} %pack.2.refs_0_), channel_id=1, source_target_pairs={{0,9},{1,8},{2,11},{3,10},{4,13},{5,12},{6,15},{7,14},{8,1},{9,0},... | collective-permute-start | bytes 98312 | tf_op jit(solution)/shard_map/ppermute | solution.py:41
  7.7 1.3 %collective-permute-start.2 = (bf16[2,8192]{1,0:T(2,128)(2,1)S(1)}, bf16[2,8192]{1,0:T(2,128)(2,1)S(1)}, u32[]{:S(2)}, u32[]{:S(2)}) collective-permute-start(bf16[2,8192]{1,0:T(2,128)(2,1)S(1)} %pack.2.refs_0_), channel_id=1, source_target_pairs={{0,13},{1,12},{2,15},{3,14},{4,9},{5,8},{6,11},{7,10},{8,5},{9,4},... | collective-permute-start | bytes 98312 | tf_op jit(solution)/shard_map/ppermute | solution.py:41
  9.1 0.3 collective-permute-start.1
  9.3 2.5 %fetch.3.refs_4_.refs_2_ = bf16[512,8192]{1,0:T(8,128)(2,1)S(1)} custom-call(bf16[512,8192]{1,0:T(8,128)(2,1)} %x_ref.1, bf16[2,8192]{1,0:T(2,128)(2,1)S(1)} %pack.2.refs_0_, bf16[512,8192]{1,0:T(8,128)(2,1)S(1)} %get-tuple-element.14.refs_2_.refs_1_), custom_call_target="tpu_custom_call", output_to_operand_aliasing={{}: (2, {})} | custom-call | bytes 10485760 | tf_op jit(solution)/shard_map/fetch/pallas_call | solution.py:72
  11.8 0.0 collective-permute-done.3.refs_3_
  11.9 1.1 %collective-permute-done.2.refs_2_ = bf16[2,8192]{1,0:T(2,128)(2,1)S(1)} collective-permute-done((bf16[2,8192]{1,0:T(2,128)(2,1)S(1)}, bf16[2,8192]{1,0:T(2,128)(2,1)S(1)}, u32[]{:S(2)}, u32[]{:S(2)}) %collective-permute-start.2) | collective-permute-done | bytes 32800 | tf_op jit(solution)/shard_map/ppermute | solution.py:41
  13.0 0.0 collective-permute-done.1.refs_1_
  13.0 0.1 pack.3.refs_0_
  13.1 0.0 copy-start
  13.1 0.0 copy-start.1
  13.1 0.0 copy-start.2
  13.1 0.6 %collective-permute-start.4 = (bf16[8,8192]{1,0:T(8,128)(2,1)S(1)}, bf16[8,8192]{1,0:T(8,128)(2,1)S(1)}, u32[]{:S(2)}, u32[]{:S(2)}) collective-permute-start(bf16[8,8192]{1,0:T(8,128)(2,1)S(1)} %pack.3.refs_0_), channel_id=1, source_target_pairs={{0,1},{1,0},{2,3},{3,2},{4,5},{5,4},{6,7},{7,6},{8,9},{9,8},{10,11... | collective-permute-start | bytes 393224 | tf_op jit(solution)/shard_map/ppermute | solution.py:41
  13.7 1.0 %collective-permute-done.4.refs_1_ = bf16[8,8192]{1,0:T(8,128)(2,1)S(1)} collective-permute-done((bf16[8,8192]{1,0:T(8,128)(2,1)S(1)}, bf16[8,8192]{1,0:T(8,128)(2,1)S(1)}, u32[]{:S(2)}, u32[]{:S(2)}) %collective-permute-start.4) | collective-permute-done | bytes 131104 | tf_op jit(solution)/shard_map/ppermute | solution.py:41
  14.7 2.5 %panel.1 = (bf16[16,512]{1,0:T(8,128)(2,1)S(1)}, bf16[320,8192]{1,0:T(8,128)(2,1)S(1)}) custom-call(s32[1]{0:T(128)} %bitcast._.me_ref, bf16[8,8192]{1,0:T(8,128)(2,1)S(1)} %pack.3.refs_0_, bf16[8,8192]{1,0:T(8,128)(2,1)S(1)} %collective-permute-done.4.refs_1_, bf16[512,8192]{1,0:T(8,128)(2,1)S(1)} %fetch.3.refs_4_.refs_2_, bf16[512,8192]{1,0:T(8,128)(2,1)} %docs_ref.1), custom_call_target="tpu_custom_call" | custom-call | flops 134217728 | bytes 8388608 | tf_op jit(solution)/shard_map/panel/pallas_call | solution.py:293
  17.2 1.6 %collective-permute-start.5 = (bf16[16,512]{1,0:T(8,128)(2,1)S(1)}, bf16[16,512]{1,0:T(8,128)(2,1)S(1)}, u32[]{:S(2)}, u32[]{:S(2)}) collective-permute-start(bf16[16,512]{1,0:T(8,128)(2,1)S(1)} %get-tuple-element.16), channel_id=1, source_target_pairs={{0,3},{1,2},{2,1},{3,0},{4,7},{5,6},{6,5},{7,4},{8,11},{9,10},{10,... | collective-permute-start | bytes 49160 | tf_op jit(solution)/shard_map/ppermute | solution.py:41
  18.8 1.7 %collective-permute-done.5 = bf16[16,512]{1,0:T(8,128)(2,1)S(1)} collective-permute-done((bf16[16,512]{1,0:T(8,128)(2,1)S(1)}, bf16[16,512]{1,0:T(8,128)(2,1)S(1)}, u32[]{:S(2)}, u32[]{:S(2)}) %collective-permute-start.5) | collective-permute-done | bytes 16416 | tf_op jit(solution)/shard_map/ppermute | solution.py:41
  20.5 0.3 collective-permute-start.6
  20.8 1.2 %collective-permute-start.9 = (bf16[2,16,512]{2,1,0:T(8,128)(2,1)S(1)}, bf16[2,16,512]{2,1,0:T(8,128)(2,1)S(1)}, u32[]{:S(2)}, u32[]{:S(2)}) collective-permute-start(bf16[2,16,512]{2,1,0:T(8,128)(2,1)S(1)} %pad_maximum_fusion.refs_0_), channel_id=1, source_target_pairs={{0,9},{1,8},{2,11},{3,10},{4,13},{5,12},{6,15},{7,14},{8,1},{9,0},... | collective-permute-start | bytes 98312 | tf_op jit(solution)/shard_map/ppermute | solution.py:41
  22.1 1.0 %collective-permute-start.8 = (bf16[2,16,512]{2,1,0:T(8,128)(2,1)S(1)}, bf16[2,16,512]{2,1,0:T(8,128)(2,1)S(1)}, u32[]{:S(2)}, u32[]{:S(2)}) collective-permute-start(bf16[2,16,512]{2,1,0:T(8,128)(2,1)S(1)} %pad_maximum_fusion.refs_0_), channel_id=1, source_target_pairs={{0,13},{1,12},{2,15},{3,14},{4,9},{5,8},{6,11},{7,10},{8,5},{9,4},... | collective-permute-start | bytes 98312 | tf_op jit(solution)/shard_map/ppermute | solution.py:41
  23.1 0.7 %collective-permute-start.7 = (bf16[2,16,512]{2,1,0:T(8,128)(2,1)S(1)}, bf16[2,16,512]{2,1,0:T(8,128)(2,1)S(1)}, u32[]{:S(2)}, u32[]{:S(2)}) collective-permute-start(bf16[2,16,512]{2,1,0:T(8,128)(2,1)S(1)} %pad_maximum_fusion.refs_0_), channel_id=1, source_target_pairs={{0,5},{1,4},{2,7},{3,6},{4,1},{5,0},{6,3},{7,2},{8,13},{9,12},{10,... | collective-permute-start | bytes 98312 | tf_op jit(solution)/shard_map/ppermute | solution.py:41
  23.8 0.0 collective-permute-done.6.refs_1_
  23.8 0.0 copy-done
  23.8 0.0 copy-done.1
  23.8 0.0 copy-done.2
  23.8 2.5 %scores_first.1 = (f32[16,512]{1,0:T(8,128)S(1)}, bf16[128,512]{1,0:T(8,128)(2,1)S(1)}, f32[16,512]{1,0:T(8,128)S(1)}, bf16[192,8192]{1,0:T(8,128)(2,1)S(1)}) custom-call(s32[1]{0:T(128)} %bitcast._.me_ref, bf16[320,8192]{1,0:T(8,128)(2,1)S(1)} %get-tuple-element.15.low_ref, bf16[512,8192]{1,0:T(8,128)(2,1)} %docs_ref.1, s32[4,16]{1,0:T(4,128)S(1)} %copy-done, ...), custom_call_target="tpu_custom_call" | custom-call | flops 33554432 | bytes 2097152 | tf_op jit(solution)/shard_map/scores_first/pallas_call | solution.py:218
  26.3 0.0 collective-permute-done.9.refs_2_
  26.3 0.9 %collective-permute-done.8.refs_1_ = bf16[2,16,512]{2,1,0:T(8,128)(2,1)S(1)} collective-permute-done((bf16[2,16,512]{2,1,0:T(8,128)(2,1)S(1)}, bf16[2,16,512]{2,1,0:T(8,128)(2,1)S(1)}, u32[]{:S(2)}, u32[]{:S(2)}) %collective-permute-start.8) | collective-permute-done | bytes 32800 | tf_op jit(solution)/shard_map/ppermute | solution.py:41
  27.2 0.0 collective-permute-done.7.refs_0_
  27.2 0.6 %collective-permute-start.10 = (bf16[6,16,512]{2,1,0:T(8,128)(2,1)S(1)}, bf16[6,16,512]{2,1,0:T(8,128)(2,1)S(1)}, u32[]{:S(2)}, u32[]{:S(2)}) collective-permute-start(bf16[6,16,512]{2,1,0:T(8,128)(2,1)S(1)} %stack.13), channel_id=1, source_target_pairs={{0,1},{1,0},{2,3},{3,2},{4,5},{5,4},{6,7},{7,6},{8,9},{9,8},{10,11... | collective-permute-start | bytes 294920 | tf_op jit(solution)/shard_map/ppermute | solution.py:41
  27.8 1.0 %scores_next.1.sum_ref = f32[16,512]{1,0:T(8,128)S(1)} custom-call(s32[1]{0:T(128)} %bitcast._.me_ref, bf16[320,8192]{1,0:T(8,128)(2,1)S(1)} %get-tuple-element.15.low_ref, bf16[192,8192]{1,0:T(8,128)(2,1)S(1)} %get-tuple-element.17.high_ref, f32[16,512]{1,0:T(8,128)S(1)} %get-tuple-element.18.sum_ref.refs_3_, ...), custom_call_target="tpu_custom_call" | custom-call | flops 50331648 | bytes 3145728 | tf_op jit(solution)/shard_map/scores_next/pallas_call | solution.py:218
  28.8 0.0 collective-permute-done.10.refs_0_
  28.8 1.3 %sums.1 = f32[128,16]{1,0:T(8,128)S(1)} custom-call(s32[1]{0:T(128)} %bitcast._.me_ref, bf16[320,8192]{1,0:T(8,128)(2,1)S(1)} %get-tuple-element.15.low_ref, bf16[192,8192]{1,0:T(8,128)(2,1)S(1)} %get-tuple-element.17.high_ref, f32[16,512]{1,0:T(8,128)S(1)} %scores_next.1.sum_ref, bf16[128,512]{1,0:T(8,128)(2,1)S(1)} %get-tuple-element.19.hot_ref, ...), custom_call_target="tpu_custom_call" | custom-call | flops 50331648 | bytes 3145728 | tf_op jit(solution)/shard_map/sums/pallas_call | solution.py:218
  30.1 0.1 all_to_all.7
  30.2 7.9 %all_to_all.11 = f32[16,1,128]{2,1,0:T(1,128)S(1)} all-to-all(f32[16,1,128]{2,1,0:T(1,128)S(1)} %bitcast.11), channel_id=1, replica_groups={{11,10,9,8,7,6,5,4,15,14,13,12,3,2,1,0},{27,26,25,24,23,22,21,20,31,30,..., dimensions={0} | all-to-all | bytes 16384 | tf_op jit(solution)/shard_map/all_to_all | solution.py:315
  38.1 0.7 %total.1 = f32[8,16]{1,0:T(8,128)} custom-call(f32[16,128]{1,0:T(8,128)S(1)} %bitcast.7), custom_call_target="tpu_custom_call" | custom-call | bytes 16384 | tf_op jit(solution)/shard_map/total/pallas_call | solution.py:316
  (3 shorter events, 0.1 us)
Async XLA Ops:
  0.0 4.5 %collective-permute-start = (bf16[1,8192]{1,0:T(2,128)(2,1)}, bf16[1,8192]{1,0:T(2,128)(2,1)S(1)}, u32[]{:S(2)}, u32[]{:S(2)}) collective-permute-start(bf16[1,8192]{1,0:T(2,128)(2,1)} %val_ref.1), channel_id=1, source_target_pairs={{0,3},{1,2},{2,1},{3,0},{4,7},{5,6},{6,5},{7,4},{8,11},{9,10},{10,... | collective-permute-start | bytes 49160 | tf_op jit(solution)/shard_map/ppermute | solution.py:41
  4.5 7.3 %collective-permute-start.3 = (bf16[2,8192]{1,0:T(2,128)(2,1)S(1)}, bf16[2,8192]{1,0:T(2,128)(2,1)S(1)}, u32[]{:S(2)}, u32[]{:S(2)}) collective-permute-start(bf16[2,8192]{1,0:T(2,128)(2,1)S(1)} %pack.2.refs_0_), channel_id=1, source_target_pairs={{0,9},{1,8},{2,11},{3,10},{4,13},{5,12},{6,15},{7,14},{8,1},{9,0},... | collective-permute-start | bytes 98312 | tf_op jit(solution)/shard_map/ppermute | solution.py:41
  7.7 5.3 %collective-permute-start.2 = (bf16[2,8192]{1,0:T(2,128)(2,1)S(1)}, bf16[2,8192]{1,0:T(2,128)(2,1)S(1)}, u32[]{:S(2)}, u32[]{:S(2)}) collective-permute-start(bf16[2,8192]{1,0:T(2,128)(2,1)S(1)} %pack.2.refs_0_), channel_id=1, source_target_pairs={{0,13},{1,12},{2,15},{3,14},{4,9},{5,8},{6,11},{7,10},{8,5},{9,4},... | collective-permute-start | bytes 98312 | tf_op jit(solution)/shard_map/ppermute | solution.py:41
  9.1 3.9 %collective-permute-start.1 = (bf16[2,8192]{1,0:T(2,128)(2,1)S(1)}, bf16[2,8192]{1,0:T(2,128)(2,1)S(1)}, u32[]{:S(2)}, u32[]{:S(2)}) collective-permute-start(bf16[2,8192]{1,0:T(2,128)(2,1)S(1)} %pack.2.refs_0_), channel_id=1, source_target_pairs={{0,5},{1,4},{2,7},{3,6},{4,1},{5,0},{6,3},{7,2},{8,13},{9,12},{10,... | collective-permute-start | bytes 98312 | tf_op jit(solution)/shard_map/ppermute | solution.py:41
  13.1 10.7 %copy-start = (s32[4,16]{1,0:T(4,128)S(1)}, s32[4,16]{1,0:T(4,128)}, u32[]{:S(2)}) copy-start(s32[4,16]{1,0:T(4,128)} %mask_ref.1) | copy-start | bytes 772
  13.1 10.7 %copy-start.1 = (s32[512]{0:T(512)S(1)}, s32[512]{0:T(512)}, u32[]{:S(2)}) copy-start(s32[512]{0:T(512)} %param.10) | copy-start | bytes 6148
  13.1 10.7 %copy-start.2 = (s32[128]{0:T(128)S(1)}, s32[128]{0:T(128)}, u32[]{:S(2)}) copy-start(s32[128]{0:T(128)} %param.11) | copy-start | bytes 1540
  13.1 1.6 %collective-permute-start.4 = (bf16[8,8192]{1,0:T(8,128)(2,1)S(1)}, bf16[8,8192]{1,0:T(8,128)(2,1)S(1)}, u32[]{:S(2)}, u32[]{:S(2)}) collective-permute-start(bf16[8,8192]{1,0:T(8,128)(2,1)S(1)} %pack.3.refs_0_), channel_id=1, source_target_pairs={{0,1},{1,0},{2,3},{3,2},{4,5},{5,4},{6,7},{7,6},{8,9},{9,8},{10,11... | collective-permute-start | bytes 393224 | tf_op jit(solution)/shard_map/ppermute | solution.py:41
  17.2 3.2 %collective-permute-start.5 = (bf16[16,512]{1,0:T(8,128)(2,1)S(1)}, bf16[16,512]{1,0:T(8,128)(2,1)S(1)}, u32[]{:S(2)}, u32[]{:S(2)}) collective-permute-start(bf16[16,512]{1,0:T(8,128)(2,1)S(1)} %get-tuple-element.16), channel_id=1, source_target_pairs={{0,3},{1,2},{2,1},{3,0},{4,7},{5,6},{6,5},{7,4},{8,11},{9,10},{10,... | collective-permute-start | bytes 49160 | tf_op jit(solution)/shard_map/ppermute | solution.py:41
  20.5 3.3 %collective-permute-start.6 = (bf16[2,16,512]{2,1,0:T(8,128)(2,1)S(1)}, bf16[2,16,512]{2,1,0:T(8,128)(2,1)S(1)}, u32[]{:S(2)}, u32[]{:S(2)}) collective-permute-start(bf16[2,16,512]{2,1,0:T(8,128)(2,1)S(1)} %pad_maximum_fusion.refs_0_), channel_id=1, source_target_pairs={{0,1},{1,0},{2,3},{3,2},{4,5},{5,4},{6,7},{7,6},{8,9},{9,8},{10,11... | collective-permute-start | bytes 98312 | tf_op jit(solution)/shard_map/ppermute | solution.py:41
  20.8 5.5 %collective-permute-start.9 = (bf16[2,16,512]{2,1,0:T(8,128)(2,1)S(1)}, bf16[2,16,512]{2,1,0:T(8,128)(2,1)S(1)}, u32[]{:S(2)}, u32[]{:S(2)}) collective-permute-start(bf16[2,16,512]{2,1,0:T(8,128)(2,1)S(1)} %pad_maximum_fusion.refs_0_), channel_id=1, source_target_pairs={{0,9},{1,8},{2,11},{3,10},{4,13},{5,12},{6,15},{7,14},{8,1},{9,0},... | collective-permute-start | bytes 98312 | tf_op jit(solution)/shard_map/ppermute | solution.py:41
  22.1 5.1 %collective-permute-start.8 = (bf16[2,16,512]{2,1,0:T(8,128)(2,1)S(1)}, bf16[2,16,512]{2,1,0:T(8,128)(2,1)S(1)}, u32[]{:S(2)}, u32[]{:S(2)}) collective-permute-start(bf16[2,16,512]{2,1,0:T(8,128)(2,1)S(1)} %pad_maximum_fusion.refs_0_), channel_id=1, source_target_pairs={{0,13},{1,12},{2,15},{3,14},{4,9},{5,8},{6,11},{7,10},{8,5},{9,4},... | collective-permute-start | bytes 98312 | tf_op jit(solution)/shard_map/ppermute | solution.py:41
  23.1 4.1 %collective-permute-start.7 = (bf16[2,16,512]{2,1,0:T(8,128)(2,1)S(1)}, bf16[2,16,512]{2,1,0:T(8,128)(2,1)S(1)}, u32[]{:S(2)}, u32[]{:S(2)}) collective-permute-start(bf16[2,16,512]{2,1,0:T(8,128)(2,1)S(1)} %pad_maximum_fusion.refs_0_), channel_id=1, source_target_pairs={{0,5},{1,4},{2,7},{3,6},{4,1},{5,0},{6,3},{7,2},{8,13},{9,12},{10,... | collective-permute-start | bytes 98312 | tf_op jit(solution)/shard_map/ppermute | solution.py:41
  27.2 1.6 %collective-permute-start.10 = (bf16[6,16,512]{2,1,0:T(8,128)(2,1)S(1)}, bf16[6,16,512]{2,1,0:T(8,128)(2,1)S(1)}, u32[]{:S(2)}, u32[]{:S(2)}) collective-permute-start(bf16[6,16,512]{2,1,0:T(8,128)(2,1)S(1)} %stack.13), channel_id=1, source_target_pairs={{0,1},{1,0},{2,3},{3,2},{4,5},{5,4},{6,7},{7,6},{8,9},{9,8},{10,11... | collective-permute-start | bytes 294920 | tf_op jit(solution)/shard_map/ppermute | solution.py:41
